TPU v7x, 32 devices: a whole 2x2x4 slice. The times are simulated.
32 devices in a mesh: section: 4 (over y, core), dp: 2 (over x), tensor: 4 (over z).
Axes of the slice: x: 2, y: 2, z: 4, core: 2. Of those that a mesh axis runs over, the one named last changes fastest.
Arguments:
- cache: bfloat16 [4, 256, 5376], P('section'), may hold values from -6 to 6
- token_ids: int32 [128], replicated, may hold values from 0 to 255
- enc_weight: bfloat16 [4, 8192, 5376], P('section', ('dp', 'tensor')), may hold values from -0.078125 to 0.078125
- enc_bias: float32 [4, 8192], P('section', ('dp', 'tensor')), may hold values from -3 to 3
- dec_weight: bfloat16 [4, 4, 2688, 8192], P('section', None, ('dp', 'tensor')), may hold values from -0.09375 to 0.09375
- dec_bias: float32 [4, 2688], P('section', ('dp', 'tensor')), may hold values from -3 to 3
- incoming: float32 [4, 128, 2688], P('section', None, ('dp', 'tensor')), may hold values from -6 to 6
- target: bfloat16 [4, 128, 2688], P('section', None, ('dp', 'tensor')), may hold values from -6 to 6
- returned: bfloat16 [4, 128, 2688], P('section', None, ('dp', 'tensor')), may hold values from -6 to 6
Outputs:
- error: bfloat16 [4, 128, 2688], P('section', None, ('dp', 'tensor'))
- outgoing: float32 [4, 128, 2688], P('section', None, ('dp', 'tensor'))
- lat_grad: float32 [4, 8192, 128], P('section', ('dp', 'tensor'))
All inputs are finite; a program needn't handle non-finite values.
Results may differ from a plain program's by a relative error of at most 0.014.
Values may be sent and summed in bfloat16 or wider, within the bound.
No kernel may reach another device: no remote copies, remote signals or barrier semaphores. Data moves between devices by JAX's collectives and lax.ppermute only.
A program may use at most 128 MiB of HBM per device.

v0:
```python
import jax
import jax.numpy as jnp
from jax import lax
from jax.sharding import PartitionSpec as P


def passed_along(shard, axis, by):
    length = lax.axis_size(axis)
    pairs = [(i, i + by) for i in range(length) if 0 <= i + by < length]
    return lax.ppermute(shard, axis, pairs)


def local(cache, token_ids, enc_weight, enc_bias, dec_weight, dec_bias, incoming, target, returned):
    layers = lax.axis_size("section")
    section = lax.axis_index("section")
    rows = jnp.take(cache[0], token_ids, axis=0)
    pre = lax.dot_general(
        rows, enc_weight[0], (((1,), (1,)), ((), ())), preferred_element_type=jnp.float32
    )
    latents = jnp.maximum(pre + enc_bias[0], 0.0).astype(jnp.bfloat16)
    decoders = dec_weight[0]
    tok_rows = latents.shape[0]
    columns = decoders.shape[1]
    block = decoders
    by_offset = jnp.einsum(
        "tn,kcn->ktc",
        lax.all_gather(latents, ("dp", "tensor"), axis=1, tiled=True),
        block,
        preferred_element_type=jnp.float32,
    )
    slot_ids = jnp.arange(layers)[:, None, None]
    placed = jnp.roll(by_offset, section, axis=0)
    within = jnp.where(slot_ids >= section, placed, 0.0)
    beyond = jnp.where(slot_ids < section, placed, 0.0)
    rising = jnp.zeros_like(within)
    falling = jnp.zeros_like(beyond)
    for step in range(layers - 1):
        rising = passed_along(rising + within, "section", 1)
        falling = passed_along((falling + beyond).astype(jnp.bfloat16), "section", -1).astype(
            jnp.float32
        )
    mine_in = lax.dynamic_index_in_dim(rising + within, section, 0, keepdims=True)
    mine_out = lax.dynamic_index_in_dim(falling + beyond, section, 0, keepdims=True)
    recon = mine_in + incoming + dec_bias[:, None, :]
    error = (recon - target.astype(jnp.float32)).astype(jnp.bfloat16)
    zero_slots = jnp.zeros((layers, tok_rows, columns), jnp.bfloat16)
    own_error = jnp.where(slot_ids == section, error, zero_slots)
    own_return = jnp.where(slot_ids == section, returned, zero_slots)
    lower = zero_slots
    higher = zero_slots
    for step in range(layers - 1):
        lower = passed_along(lower + own_error, "section", -1)
        higher = passed_along(higher + own_return, "section", 1)
    slots = jnp.where(slot_ids >= section, lower + own_error, higher)
    offsets = jnp.roll(slots, -section, axis=0)
    block = decoders
    lat_grad = lax.psum_scatter(
        jnp.einsum("kcn,ktc->nt", block, offsets, preferred_element_type=jnp.float32),
        ("dp", "tensor"),
        scatter_dimension=0,
        tiled=True,
    )
    return (error, mine_out, lat_grad[None])


def solution(mesh):
    placed = (
        P("section", None, None),
        P(),
        P("section", ("dp", "tensor"), None),
        P("section", ("dp", "tensor")),
        P("section", None, ("dp", "tensor"), None),
        P("section", ("dp", "tensor")),
        P("section", None, ("dp", "tensor")),
        P("section", None, ("dp", "tensor")),
        P("section", None, ("dp", "tensor")),
    )
    return jax.shard_map(
        local,
        mesh=mesh,
        in_specs=placed,
        out_specs=(
            P("section", None, ("dp", "tensor")),
            P("section", None, ("dp", "tensor")),
            P("section", ("dp", "tensor"), None),
        ),
        check_vma=False,
    )
```

profile of v0, /device:TPU:0, one launch (start us, length us, event | category | flops | bytes accessed | tf_op | source)
XLA Modules:
  0.0 275.4 jit_solution(5897628812235745976)
XLA Ops:
  9.0 2.5 gather_fusion
  11.5 9.0 %fusion.27 = bf16[128,1024]{1,0:T(8,128)(2,1)} fusion(bf16[1,1024,5376]{2,1,0:T(8,128)(2,1)} %param.11, bf16[128,5376]{1,0:T(8,128)(2,1)} %gather_fusion, pred[128]{0:T(512)(128)(4,1)S(1)} %compare_and_fusion, f32[1024]{0:T(1024)S(1)} %bitcast.43), kind=kOutput, calls=%fused_computation.16 | convolution fusion | flops 1410367488 | bytes 12652672 | tf_op jit(solution)/shard_map/dot_general | solution.py:17
  20.5 52.2 %all-gather.2.cloned.1.call-done = bf16[128,8192]{1,0:T(8,128)(2,1)} async-done(((bf16[128,1024]{1,0:T(8,128)(2,1)}), bf16[128,8192]{1,0:T(8,128)(2,1)}) %all-gather.2.cloned.1.call-update) | async-done | bytes 2097168 | tf_op jit(solution)/shard_map/all_gather | solution.py:27
  72.8 11.0 %fusion.12 = f32[4,128,336]{1,2,0:T(8,128)S(1)} fusion(bf16[1,4,336,8192]{3,2,1,0:T(8,128)(2,1)} %param.13, bf16[128,8192]{1,0:T(8,128)(2,1)} %all-gather.2.cloned.1.call-done), kind=kOutput, calls=%fused_computation.13 | convolution fusion | flops 2818572288 | bytes 24805376 | tf_op jit(solution)/shard_map/tn,kcn->ktc/dot_general | solution.py:25
  84.7 1.5 collective-permute-start
  86.2 1.7 collective-permute-done
  88.0 10.3 %collective-permute-start.1 = (f32[4,128,336]{1,2,0:T(8,128)S(1)}, f32[4,128,336]{1,2,0:T(8,128)S(1)}, u32[]{:S(2)}, u32[]{:S(2)}) collective-permute-start(f32[4,128,336]{1,2,0:T(8,128)S(1)} %add.97), channel_id=1, source_target_pairs={{0,8},{8,16},{16,24},{1,9},{9,17},{17,25},{2,10},{10,18},{18,26},{... | collective-permute-start | bytes 2064392 | tf_op jit(solution)/shard_map/ppermute | solution.py:10
  98.2 1.7 collective-permute-done.1
  100.9 11.4 %collective-permute-start.2 = (f32[4,128,336]{1,2,0:T(8,128)}, f32[4,128,336]{1,2,0:T(8,128)}, u32[]{:S(2)}, u32[]{:S(2)}) collective-permute-start(f32[4,128,336]{1,2,0:T(8,128)} %add.98), channel_id=1, source_target_pairs={{0,8},{8,16},{16,24},{1,9},{9,17},{17,25},{2,10},{10,18},{18,26},{... | collective-permute-start | bytes 2064392 | tf_op jit(solution)/shard_map/ppermute | solution.py:10
  114.9 1.3 collective-permute-start.6
  116.2 10.3 %collective-permute-done.6 = bf16[4,128,336]{1,2,0:T(8,128)(2,1)S(1)} collective-permute-done((bf16[4,128,336]{1,2,0:T(8,128)(2,1)S(1)}, bf16[4,128,336]{1,2,0:T(8,128)(2,1)S(1)}, u32[]{:S(2)}, u32[]{:S(2)}) %collective-permute-start.6) | collective-permute-done | bytes 344096 | tf_op jit(solution)/shard_map/ppermute | solution.py:10
  128.8 8.8 %collective-permute-start.9 = (bf16[4,128,336]{1,2,0:T(8,128)(2,1)S(1)}, bf16[4,128,336]{1,2,0:T(8,128)(2,1)S(1)}, u32[]{:S(2)}, u32[]{:S(2)}) collective-permute-start(bf16[4,128,336]{1,2,0:T(8,128)(2,1)S(1)} %get-tuple-element.12), channel_id=1, source_target_pairs={{0,8},{8,16},{16,24},{1,9},{9,17},{17,25},{2,10},{10,18},{18,26},{... | collective-permute-start | bytes 1032200 | tf_op jit(solution)/shard_map/ppermute | solution.py:10
  138.9 1.8 select_add_fusion.1
  140.6 6.6 %collective-permute-start.10 = (bf16[4,128,336]{1,2,0:T(8,128)(2,1)S(1)}, bf16[4,128,336]{1,2,0:T(8,128)(2,1)S(1)}, u32[]{:S(2)}, u32[]{:S(2)}) collective-permute-start(bf16[4,128,336]{1,2,0:T(8,128)(2,1)S(1)} %get-tuple-element.10), channel_id=1, source_target_pairs={{0,8},{8,16},{16,24},{1,9},{9,17},{17,25},{2,10},{10,18},{18,26},{... | collective-permute-start | bytes 1032200 | tf_op jit(solution)/shard_map/ppermute | solution.py:10
  147.2 1.3 collective-permute-start.8
  148.5 1.7 fusion.41
  150.2 8.0 %collective-permute-start.11 = (bf16[4,128,336]{1,2,0:T(8,128)(2,1)}, bf16[4,128,336]{1,2,0:T(8,128)(2,1)}, u32[]{:S(2)}, u32[]{:S(2)}) collective-permute-start(bf16[4,128,336]{1,2,0:T(8,128)(2,1)} %fusion.41), channel_id=1, source_target_pairs={{0,8},{8,16},{16,24},{1,9},{9,17},{17,25},{2,10},{10,18},{18,26},{... | collective-permute-start | bytes 1032200 | tf_op jit(solution)/shard_map/ppermute | solution.py:10
  160.3 12.9 %fusion.6 = f32[8192,128]{0,1:T(8,128)} fusion(bf16[1,4,336,8192]{3,2,1,0:T(8,128)(2,1)} %param.13, s32[]{:T(128)S(6)} %select_n.66, bf16[4,128,336]{1,2,0:T(8,128)(2,1)S(1)} %fusion.34), kind=kOutput, calls=%fused_computation.7 | convolution fusion | flops 2818744320 | bytes 26558468 | tf_op jit(solution)/shard_map/kcn,ktc->nt/dot_general | solution.py:58
  174.5 7.3 %collective-permute-done.3 = bf16[4,128,336]{1,2,0:T(8,128)(2,1)S(1)} collective-permute-done((bf16[4,128,336]{1,2,0:T(8,128)(2,1)}, bf16[4,128,336]{1,2,0:T(8,128)(2,1)S(1)}, u32[]{:S(2)}, u32[]{:S(2)}) %collective-permute-start.3) | collective-permute-done | bytes 344096 | tf_op jit(solution)/shard_map/ppermute | solution.py:10
  183.2 8.4 %collective-permute-done.4 = bf16[4,128,336]{1,2,0:T(8,128)(2,1)S(1)} collective-permute-done((bf16[4,128,336]{1,2,0:T(8,128)(2,1)S(1)}, bf16[4,128,336]{1,2,0:T(8,128)(2,1)S(1)}, u32[]{:S(2)}, u32[]{:S(2)}) %collective-permute-start.4) | collective-permute-done | bytes 344096 | tf_op jit(solution)/shard_map/ppermute | solution.py:10
  191.7 1.3 collective-permute-start.5
  193.0 7.7 %collective-permute-done.5 = bf16[4,128,336]{1,2,0:T(8,128)(2,1)S(1)} collective-permute-done((bf16[4,128,336]{1,2,0:T(8,128)(2,1)S(1)}, bf16[4,128,336]{1,2,0:T(8,128)(2,1)S(1)}, u32[]{:S(2)}, u32[]{:S(2)}) %collective-permute-start.5) | collective-permute-done | bytes 344096 | tf_op jit(solution)/shard_map/ppermute | solution.py:10
  201.3 65.2 %reduce-scatter.2.cloned.1.call-done = f32[1024,128]{0,1:T(8,128)} async-done(((f32[8192,128]{0,1:T(8,128)}), f32[1024,128]{0,1:T(8,128)}) %reduce-scatter.2.cloned.1.call-update) | async-done | bytes 524304 | tf_op jit(solution)/shard_map/reduce_scatter | solution.py:57
  266.6 2.0 copy.12
  (39 shorter events, 15.5 us)
Async XLA Ops:
  7.2 1.8 copy-start
  7.2 65.6 %all-gather.2.cloned.1.call-start = ((), (), s32[]{:S(2)}) async-start(), calls=%async_computation.1 | async-start | bytes 2359296 | tf_op jit(solution)/shard_map/all_gather | solution.py:27
  9.0 2.5 copy-start.4
  20.5 246.1 %reduce-scatter.2.cloned.1.call-start = ((), (), s32[]{:S(2)}) async-start(), calls=%async_computation.2 | async-start | bytes 4718592 | tf_op jit(solution)/shard_map/reduce_scatter | solution.py:57
  84.7 15.2 %copy-start.1 = (f32[4,128,336]{1,2,0:T(8,128)}, f32[4,128,336]{1,2,0:T(8,128)S(1)}, u32[]{:S(2)}) copy-start(f32[4,128,336]{1,2,0:T(8,128)S(1)} %get-tuple-element.8) | copy-start | bytes 2064388
  84.7 27.6 %copy-start.3 = (f32[1,336]{1,0:T(1,128)S(1)}, f32[1,336]{1,0:T(1,128)}, u32[]{:S(2)}) copy-start(f32[1,336]{1,0:T(1,128)} %param.14) | copy-start | bytes 4036
  84.7 3.2 %collective-permute-start = (f32[4,128,336]{1,2,0:T(8,128)S(1)}, f32[4,128,336]{1,2,0:T(8,128)S(1)}, u32[]{:S(2)}, u32[]{:S(2)}) collective-permute-start(f32[4,128,336]{1,2,0:T(8,128)S(1)} %get-tuple-element.8), channel_id=1, source_target_pairs={{0,8},{8,16},{16,24},{1,9},{9,17},{17,25},{2,10},{10,18},{18,26},{... | collective-permute-start | bytes 2064392 | tf_op jit(solution)/shard_map/ppermute | solution.py:10
  88.0 12.0 %collective-permute-start.1 = (f32[4,128,336]{1,2,0:T(8,128)S(1)}, f32[4,128,336]{1,2,0:T(8,128)S(1)}, u32[]{:S(2)}, u32[]{:S(2)}) collective-permute-start(f32[4,128,336]{1,2,0:T(8,128)S(1)} %add.97), channel_id=1, source_target_pairs={{0,8},{8,16},{16,24},{1,9},{9,17},{17,25},{2,10},{10,18},{18,26},{... | collective-permute-start | bytes 2064392 | tf_op jit(solution)/shard_map/ppermute | solution.py:10
  100.9 12.6 %collective-permute-start.2 = (f32[4,128,336]{1,2,0:T(8,128)}, f32[4,128,336]{1,2,0:T(8,128)}, u32[]{:S(2)}, u32[]{:S(2)}) collective-permute-start(f32[4,128,336]{1,2,0:T(8,128)} %add.98), channel_id=1, source_target_pairs={{0,8},{8,16},{16,24},{1,9},{9,17},{17,25},{2,10},{10,18},{18,26},{... | collective-permute-start | bytes 2064392 | tf_op jit(solution)/shard_map/ppermute | solution.py:10
  114.8 45.5 %copy-start.2 = (bf16[1,128,336]{1,2,0:T(8,128)(2,1)}, bf16[1,128,336]{1,2,0:T(8,128)(2,1)S(1)}, u32[]{:S(2)}) copy-start(bf16[1,128,336]{1,2,0:T(8,128)(2,1)S(1)} %fusion.40) | copy-start | bytes 258052
  114.9 11.6 %collective-permute-start.6 = (bf16[4,128,336]{1,2,0:T(8,128)(2,1)S(1)}, bf16[4,128,336]{1,2,0:T(8,128)(2,1)S(1)}, u32[]{:S(2)}, u32[]{:S(2)}) collective-permute-start(bf16[4,128,336]{1,2,0:T(8,128)(2,1)S(1)} %broadcast_select_fusion.3), channel_id=1, source_target_pairs={{8,0},{16,8},{24,16},{9,1},{17,9},{25,17},{10,2},{18,10},{26,18},{... | collective-permute-start | bytes 1032200 | tf_op jit(solution)/shard_map/ppermute | solution.py:10
  127.5 10.1 %collective-permute-start.7 = (bf16[4,128,336]{1,2,0:T(8,128)(2,1)S(1)}, bf16[4,128,336]{1,2,0:T(8,128)(2,1)S(1)}, u32[]{:S(2)}, u32[]{:S(2)}) collective-permute-start(bf16[4,128,336]{1,2,0:T(8,128)(2,1)S(1)} %get-tuple-element.11), channel_id=1, source_target_pairs={{8,0},{16,8},{24,16},{9,1},{17,9},{25,17},{10,2},{18,10},{26,18},{... | collective-permute-start | bytes 1032200 | tf_op jit(solution)/shard_map/ppermute | solution.py:10
  128.8 10.1 %collective-permute-start.9 = (bf16[4,128,336]{1,2,0:T(8,128)(2,1)S(1)}, bf16[4,128,336]{1,2,0:T(8,128)(2,1)S(1)}, u32[]{:S(2)}, u32[]{:S(2)}) collective-permute-start(bf16[4,128,336]{1,2,0:T(8,128)(2,1)S(1)} %get-tuple-element.12), channel_id=1, source_target_pairs={{0,8},{8,16},{16,24},{1,9},{9,17},{17,25},{2,10},{10,18},{18,26},{... | collective-permute-start | bytes 1032200 | tf_op jit(solution)/shard_map/ppermute | solution.py:10
  140.6 7.9 %collective-permute-start.10 = (bf16[4,128,336]{1,2,0:T(8,128)(2,1)S(1)}, bf16[4,128,336]{1,2,0:T(8,128)(2,1)S(1)}, u32[]{:S(2)}, u32[]{:S(2)}) collective-permute-start(bf16[4,128,336]{1,2,0:T(8,128)(2,1)S(1)} %get-tuple-element.10), channel_id=1, source_target_pairs={{0,8},{8,16},{16,24},{1,9},{9,17},{17,25},{2,10},{10,18},{18,26},{... | collective-permute-start | bytes 1032200 | tf_op jit(solution)/shard_map/ppermute | solution.py:10
  147.2 11.0 %collective-permute-start.8 = (bf16[4,128,336]{1,2,0:T(8,128)(2,1)}, bf16[4,128,336]{1,2,0:T(8,128)(2,1)}, u32[]{:S(2)}, u32[]{:S(2)}) collective-permute-start(bf16[4,128,336]{1,2,0:T(8,128)(2,1)} %get-tuple-element.9), channel_id=1, source_target_pairs={{8,0},{16,8},{24,16},{9,1},{17,9},{25,17},{10,2},{18,10},{26,18},{... | collective-permute-start | bytes 1032200 | tf_op jit(solution)/shard_map/ppermute | solution.py:10
  150.2 8.8 %collective-permute-start.11 = (bf16[4,128,336]{1,2,0:T(8,128)(2,1)}, bf16[4,128,336]{1,2,0:T(8,128)(2,1)}, u32[]{:S(2)}, u32[]{:S(2)}) collective-permute-start(bf16[4,128,336]{1,2,0:T(8,128)(2,1)} %fusion.41), channel_id=1, source_target_pairs={{0,8},{8,16},{16,24},{1,9},{9,17},{17,25},{2,10},{10,18},{18,26},{... | collective-permute-start | bytes 1032200 | tf_op jit(solution)/shard_map/ppermute | solution.py:10
  173.2 8.6 %collective-permute-start.3 = (bf16[4,128,336]{1,2,0:T(8,128)(2,1)}, bf16[4,128,336]{1,2,0:T(8,128)(2,1)S(1)}, u32[]{:S(2)}, u32[]{:S(2)}) collective-permute-start(bf16[4,128,336]{1,2,0:T(8,128)(2,1)} %get-tuple-element.6), channel_id=1, source_target_pairs={{8,0},{16,8},{24,16},{9,1},{17,9},{25,17},{10,2},{18,10},{26,18},{... | collective-permute-start | bytes 1032200 | tf_op jit(solution)/shard_map/ppermute | solution.py:10
  181.9 9.7 %collective-permute-start.4 = (bf16[4,128,336]{1,2,0:T(8,128)(2,1)S(1)}, bf16[4,128,336]{1,2,0:T(8,128)(2,1)S(1)}, u32[]{:S(2)}, u32[]{:S(2)}) collective-permute-start(bf16[4,128,336]{1,2,0:T(8,128)(2,1)S(1)} %add_convert_fusion.1), channel_id=1, source_target_pairs={{8,0},{16,8},{24,16},{9,1},{17,9},{25,17},{10,2},{18,10},{26,18},{... | collective-permute-start | bytes 1032200 | tf_op jit(solution)/shard_map/ppermute | solution.py:10
  191.7 9.0 %collective-permute-start.5 = (bf16[4,128,336]{1,2,0:T(8,128)(2,1)S(1)}, bf16[4,128,336]{1,2,0:T(8,128)(2,1)S(1)}, u32[]{:S(2)}, u32[]{:S(2)}) collective-permute-start(bf16[4,128,336]{1,2,0:T(8,128)(2,1)S(1)} %add_convert_fusion), channel_id=1, source_target_pairs={{8,0},{16,8},{24,16},{9,1},{17,9},{25,17},{10,2},{18,10},{26,18},{... | collective-permute-start | bytes 1032200 | tf_op jit(solution)/shard_map/ppermute | solution.py:10
Sparse Core Ops, SparseCore 0:
  20.6 52.1 all-gather.1
  173.3 93.1 reduce-scatter.1
where the time goes:
time: 276 us; the launch traced here: 275 us
  waiting for transfers between devices  158 us (57%)
  starting transfers between devices  54.3 us (20%)
  matrix products  32.8 us (12%)
  between operations  14.2 us (5%)
  other arithmetic  11.4 us (4%)
  local copies, waits for them, and re-layouts  4.82 us (2%)
    reduce_scatter x1, waiting for transfers between devices, local(): lax.psum_scatter(jnp.einsum('kcn,ktc->nt', block, offsets, preferred_elem...  65.2 us
    ppermute x12, starting transfers between devices, passed_along(): return lax.ppermute(shard, axis, pairs)  54.2 us
    all_gather x1, waiting for transfers between devices, local(): lax.all_gather(latents, ('dp', 'tensor'), axis=1, tiled=True)  52.2 us
    ppermute x12, waiting for transfers between devices, passed_along(): return lax.ppermute(shard, axis, pairs)  40.4 us
    dot_general x1, matrix products, local(): jnp.einsum('kcn,ktc->nt', block, offsets, preferred_element_type=jnp.floa...  12.9 us
    dot_general x1, matrix products, local(): jnp.einsum('tn,kcn->ktc', lax.all_gather(latents, ('dp', 'tensor'), axis=...  11 us
    dot_general x1, matrix products, local(): lax.dot_general(rows, enc_weight[0], (((1,), (1,)), ((), ())), preferred_...  8.96 us
  transfers between devices with their start and end apart: 14, of which 11 were waited for; matrix products, arithmetic and copies ran while one was open for 1% of the time, Pallas kernels for 0%

commit v1 on v0

v1 whole, which is shorter than its diff:
```python
import jax
import jax.numpy as jnp
from jax import lax
from jax.sharding import PartitionSpec as P

GROUP = ("dp", "tensor")
BF16 = jnp.bfloat16
F32 = jnp.float32


def cycle_order(rows, columns):
    order = []
    for row in range(rows):
        line = [row * columns + column for column in range(columns)]
        order += line if row % 2 == 0 else line[::-1]
    return order


def local(cache, token_ids, enc_weight, enc_bias, dec_weight, dec_bias, incoming, target, returned):
    layers = lax.axis_size("section")
    section = lax.axis_index("section")
    order = cycle_order(lax.axis_size("dp"), lax.axis_size("tensor"))
    size = len(order)
    place_of = [order.index(i) for i in range(size)]
    me = lax.axis_index(GROUP)
    place = jnp.asarray(place_of, jnp.int32)[me]

    def along(value, by):
        pairs = [(order[i], order[(i + by) % size]) for i in range(size)]
        return lax.ppermute(value, GROUP, pairs)

    def member(distance):
        return jnp.asarray(order, jnp.int32)[(place + distance) % size]

    def shifted(value, by):
        return lax.ppermute(value, "section", [(i, (i + by) % layers) for i in range(layers)])

    mine = enc_weight.shape[1]
    half = mine // 2
    columns = dec_weight.shape[2]
    tokens = token_ids.shape[0]
    decoders = dec_weight[0].reshape(layers * columns, dec_weight.shape[3])

    def part(owner, which):
        return lax.dynamic_slice_in_dim(decoders, owner * mine + which * half, half, 1)

    rows = cache[0].at[token_ids].get(mode="promise_in_bounds")

    def encode(which):
        pre = lax.dot_general(
            rows,
            enc_weight[0, which * half : (which + 1) * half],
            (((1,), (1,)), ((), ())),
            preferred_element_type=F32,
        )
        bias = enc_bias[0, which * half : (which + 1) * half]
        return jnp.maximum(pre + bias, 0.0).astype(BF16)

    def decode(latents, owner, which):
        return lax.dot_general(
            part(owner, which), latents, (((1,), (1,)), ((), ())), preferred_element_type=F32
        )

    own = [encode(0), encode(1)]
    total = decode(own[0], me, 0) + decode(own[1], me, 1)
    up, down = list(own), list(own)
    for step in range(1, (size - 1) // 2 + 1):
        for which in (0, 1):
            up[which] = along(up[which], 1)
            down[which] = along(down[which], -1)
            total = total + decode(up[which], member(-step), which)
            total = total + decode(down[which], member(step), which)
    if size % 2 == 0:
        total = total + decode(along(up[0], 1), member(size // 2), 0)
        total = total + decode(along(down[1], -1), member(size // 2), 1)

    by_offset = total.reshape(layers, columns, tokens)
    within = by_offset[0]
    beyond = jnp.zeros_like(within)
    for offset in range(1, layers):
        came = shifted(by_offset[offset].astype(BF16), offset).astype(F32)
        within = within + jnp.where(section >= offset, came, 0.0)
        beyond = beyond + jnp.where(section < offset, came, 0.0)
    recon = within + incoming[0].T + dec_bias[0][:, None]
    error = (recon - target[0].T.astype(F32)).astype(BF16)
    passed = returned[0].T
    upstream = [error]
    for offset in range(1, layers):
        upstream.append(shifted(jnp.where(section >= offset, error, passed), -offset))
    back = jnp.concatenate(upstream, 0)

    def gradient(owner, which):
        return lax.dot_general(
            part(owner, which), back, (((0,), (0,)), ((), ())), preferred_element_type=F32
        )

    up, down = [None, None], [None, None]
    if size % 2 == 0:
        up[0] = along(gradient(member(size // 2), 0).astype(BF16), 1)
        down[1] = along(gradient(member(size // 2), 1).astype(BF16), -1)
    for step in range((size - 1) // 2, 0, -1):
        for which in (0, 1):
            rise = gradient(member(step), which)
            fall = gradient(member(-step), which)
            if up[which] is not None:
                rise = rise + up[which].astype(F32)
            if down[which] is not None:
                fall = fall + down[which].astype(F32)
            up[which] = along(rise.astype(BF16), 1)
            down[which] = along(fall.astype(BF16), -1)
    parts = []
    for which in (0, 1):
        own_part = gradient(me, which)
        for came in (up[which], down[which]):
            if came is not None:
                own_part = own_part + came.astype(F32)
        parts.append(own_part)
    lat_grad = jnp.concatenate(parts, 0)
    return (error.T[None], beyond.T[None], lat_grad[None])


def solution(mesh):
    placed = (
        P("section", None, None),
        P(),
        P("section", GROUP, None),
        P("section", GROUP),
        P("section", None, GROUP, None),
        P("section", GROUP),
        P("section", None, GROUP),
        P("section", None, GROUP),
        P("section", None, GROUP),
    )
    return jax.shard_map(
        local,
        mesh=mesh,
        in_specs=placed,
        out_specs=(
            P("section", None, GROUP),
            P("section", None, GROUP),
            P("section", GROUP, None),
        ),
        check_vma=False,
    )
```

time: 276 us -> 142 us (0.51)
  waiting for transfers between devices: 158 us -> 11.6 us
  matrix products: 32.8 us -> 73.5 us
  starting transfers between devices: 54.3 us -> 36.8 us
  other arithmetic: 11.4 us -> 3.57 us
  between operations: 14.2 us -> 10.1 us
    reduce_scatter x1 -> x0, waiting for transfers between devices: 65.2 us -> none  [local(): lax.psum_scatter(jnp.einsum('kcn,ktc->nt', block, offsets, preferred_elem...]
    all_gather x1 -> x0, waiting for transfers between devices: 52.2 us -> none  [local(): lax.all_gather(latents, ('dp', 'tensor'), axis=1, tiled=True)]
    dot_general x3 -> x34, matrix products: 32.8 us -> 73.5 us  [the longest x16 31.9 us: decode(): lax.dot_general(part(owner, which), latents, (((1,), (1,)), ((), ())), pr...]
    ppermute x12 -> x34, waiting for transfers between devices: 40.4 us -> 11.6 us  [the longest x28 5.98 us: along(): return lax.ppermute(value, GROUP, pairs)]
    ppermute x12 -> x34, starting transfers between devices: 54.2 us -> 36.8 us  [the longest x28 30.6 us: along(): return lax.ppermute(value, GROUP, pairs)]
    add x6 -> x0, other arithmetic: 6.23 us -> none  [the longest x2 2.76 us: local(): lower = passed_along(lower + own_error, 'section', -1)]
  transfers between devices with their start and end apart: 14 -> 34, of which waited for: 11 -> 8; matrix products, arithmetic and copies ran while one was open for 1% -> 45% of each run, Pallas kernels for 0% -> 0%
where the time goes in v1:
time: 142 us; the launch traced here: 141 us
  matrix products  73.5 us (52%)
  starting transfers between devices  36.8 us (26%)
  waiting for transfers between devices  11.6 us (8%)
  between operations  10.1 us (7%)
  local copies, waits for them, and re-layouts  4.85 us (3%)
  other arithmetic  3.57 us (3%)
    dot_general x16, matrix products, decode(): lax.dot_general(part(owner, which), latents, (((1,), (1,)), ((), ())), pr...  31.9 us
    dot_general x16, matrix products, gradient(): lax.dot_general(part(owner, which), back, (((0,), (0,)), ((), ())), prefe...  30.9 us
    ppermute x28, starting transfers between devices, along(): return lax.ppermute(value, GROUP, pairs)  30.6 us
    dot_general x2, matrix products, encode(): lax.dot_general(rows, enc_weight[0, which * half:(which + 1) * half], (((...  10.7 us
    ppermute x6, starting transfers between devices, shifted(): lax.ppermute(value, 'section', [(i, (i + by) % layers) for i in range(lay...  6.19 us
    ppermute x28, waiting for transfers between devices, along(): return lax.ppermute(value, GROUP, pairs)  5.98 us
    ppermute x6, waiting for transfers between devices, shifted(): lax.ppermute(value, 'section', [(i, (i + by) % layers) for i in range(lay...  5.67 us
  transfers between devices with their start and end apart: 34, of which 8 were waited for; matrix products, arithmetic and copies ran while one was open for 45% of the time, Pallas kernels for 0%

profile of v1, /device:TPU:0, one launch (start us, length us, event | category | flops | bytes accessed | tf_op | source)
XLA Modules:
  0.0 140.5 jit_solution(15839765190192759729)
XLA Ops:
  2.4 2.5 %gather_fusion = bf16[128,5376]{1,0:T(8,128)(2,1)} fusion(bf16[256,5376]{1,0:T(8,128)(2,1)S(1)} %bitcast.97, s32[1024]{0:T(1024)S(1)} %pad_clamp_fusion), kind=kCustom, calls=%fused_computation | custom fusion | bytes 2753024 | tf_op jit(solution)/shard_map/gather | solution.py:47
  5.0 5.6 %fusion.174 = bf16[128,512]{1,0:T(8,128)(2,1)} fusion(bf16[128,5376]{1,0:T(8,128)(2,1)} %gather_fusion, bf16[1,1024,5376]{2,1,0:T(8,128)(2,1)} %param.40, f32[512]{0:T(512)S(1)} %bitcast.132), kind=kOutput, calls=%fused_computation.114 | convolution fusion | flops 704839680 | bytes 7014400 | tf_op jit(solution)/shard_map/dot_general | solution.py:50
  10.6 3.0 %collective-permute-start.2 = (bf16[128,512]{1,0:T(8,128)(2,1)}, bf16[128,512]{1,0:T(8,128)(2,1)}, u32[]{:S(2)}, u32[]{:S(2)}) collective-permute-start(bf16[128,512]{1,0:T(8,128)(2,1)} %fusion.174), channel_id=1, source_target_pairs={{0,1},{1,2},{2,3},{3,7},{7,6},{6,5},{5,4},{4,0},{8,9},{9,10},{10,1... | collective-permute-start | bytes 393224 | tf_op jit(solution)/shard_map/ppermute | solution.py:30
  13.6 5.1 %fusion.171 = bf16[128,512]{1,0:T(8,128)(2,1)} fusion(bf16[128,5376]{1,0:T(8,128)(2,1)S(1)} %copy-done.1, bf16[1,1024,5376]{2,1,0:T(8,128)(2,1)} %param.40, f32[512]{0:T(512)S(1)} %bitcast.131), kind=kOutput, calls=%fused_computation.113 | convolution fusion | flops 704839680 | bytes 7014400 | tf_op jit(solution)/shard_map/dot_general | solution.py:50
  18.7 1.9 %collective-permute-start.1 = (bf16[128,512]{1,0:T(8,128)(2,1)}, bf16[128,512]{1,0:T(8,128)(2,1)}, u32[]{:S(2)}, u32[]{:S(2)}) collective-permute-start(bf16[128,512]{1,0:T(8,128)(2,1)} %fusion.171), channel_id=1, source_target_pairs={{0,4},{1,0},{2,1},{3,2},{7,3},{6,7},{5,6},{4,5},{8,12},{9,8},{10,9... | collective-permute-start | bytes 393224 | tf_op jit(solution)/shard_map/ppermute | solution.py:30
  20.7 2.7 %fusion.73 = f32[1344,128]{1,0:T(8,128)} fusion(bf16[128,512]{1,0:T(8,128)(2,1)} %fusion.171, bf16[1344,8192]{1,0:T(8,128)(2,1)} %bitcast.98, s32[]{:T(128)S(6)} %select_n.265), kind=kOutput, calls=%fused_computation.79 | convolution fusion | flops 176160768 | bytes 2195460 | tf_op jit(solution)/shard_map/dot_general | solution.py:60
  23.5 2.1 %convolution_add_fusion.4 = f32[1344,128]{1,0:T(8,128)S(1)} fusion(f32[1344,128]{1,0:T(8,128)} %fusion.73, bf16[128,512]{1,0:T(8,128)(2,1)} %fusion.174, bf16[1344,8192]{1,0:T(8,128)(2,1)} %bitcast.99, s32[]{:T(128)S(6)} %select_n.267), kind=kOutput, calls=%fused_computation.21 | convolution fusion | flops 176332800 | bytes 2883588 | tf_op jit(solution)/shard_map/dot_general | solution.py:60
  35.9 2.1 %collective-permute-start.6 = (bf16[128,512]{1,0:T(8,128)(2,1)}, bf16[128,512]{1,0:T(8,128)(2,1)S(1)}, u32[]{:S(2)}, u32[]{:S(2)}) collective-permute-start(bf16[128,512]{1,0:T(8,128)(2,1)} %collective-permute-done.2), channel_id=1, source_target_pairs={{0,1},{1,2},{2,3},{3,7},{7,6},{6,5},{5,4},{4,0},{8,9},{9,10},{10,1... | collective-permute-start | bytes 393224 | tf_op jit(solution)/shard_map/ppermute | solution.py:30
  41.8 2.0 %collective-permute-start.7 = (bf16[128,512]{1,0:T(8,128)(2,1)}, bf16[128,512]{1,0:T(8,128)(2,1)S(1)}, u32[]{:S(2)}, u32[]{:S(2)}) collective-permute-start(bf16[128,512]{1,0:T(8,128)(2,1)} %collective-permute-done.3), channel_id=1, source_target_pairs={{0,4},{1,0},{2,1},{3,2},{7,3},{6,7},{5,6},{4,5},{8,12},{9,8},{10,9... | collective-permute-start | bytes 393224 | tf_op jit(solution)/shard_map/ppermute | solution.py:30
  47.8 2.0 %collective-permute-start.9 = (bf16[128,512]{1,0:T(8,128)(2,1)S(1)}, bf16[128,512]{1,0:T(8,128)(2,1)S(1)}, u32[]{:S(2)}, u32[]{:S(2)}) collective-permute-start(bf16[128,512]{1,0:T(8,128)(2,1)S(1)} %collective-permute-done.5), channel_id=1, source_target_pairs={{0,4},{1,0},{2,1},{3,2},{7,3},{6,7},{5,6},{4,5},{8,12},{9,8},{10,9... | collective-permute-start | bytes 393224 | tf_op jit(solution)/shard_map/ppermute | solution.py:30
  53.6 2.0 %collective-permute-start.11 = (bf16[128,512]{1,0:T(8,128)(2,1)S(1)}, bf16[128,512]{1,0:T(8,128)(2,1)S(1)}, u32[]{:S(2)}, u32[]{:S(2)}) collective-permute-start(bf16[128,512]{1,0:T(8,128)(2,1)S(1)} %collective-permute-done.7), channel_id=1, source_target_pairs={{0,4},{1,0},{2,1},{3,2},{7,3},{6,7},{5,6},{4,5},{8,12},{9,8},{10,9... | collective-permute-start | bytes 393224 | tf_op jit(solution)/shard_map/ppermute | solution.py:30
  59.6 2.0 %collective-permute-start.13 = (bf16[128,512]{1,0:T(8,128)(2,1)S(1)}, bf16[128,512]{1,0:T(8,128)(2,1)S(1)}, u32[]{:S(2)}, u32[]{:S(2)}) collective-permute-start(bf16[128,512]{1,0:T(8,128)(2,1)S(1)} %collective-permute-done.11), channel_id=1, source_target_pairs={{0,4},{1,0},{2,1},{3,2},{7,3},{6,7},{5,6},{4,5},{8,12},{9,8},{10,9... | collective-permute-start | bytes 393224 | tf_op jit(solution)/shard_map/ppermute | solution.py:30
  61.5 2.2 %collective-permute-done.8 = bf16[128,512]{1,0:T(8,128)(2,1)S(1)} collective-permute-done((bf16[128,512]{1,0:T(8,128)(2,1)S(1)}, bf16[128,512]{1,0:T(8,128)(2,1)S(1)}, u32[]{:S(2)}, u32[]{:S(2)}) %collective-permute-start.8) | collective-permute-done | bytes 131104 | tf_op jit(solution)/shard_map/ppermute | solution.py:30
  69.5 1.9 %fusion.9 = f32[1344,128]{1,0:T(8,128)S(1)} fusion(f32[1344,128]{1,0:T(8,128)S(1)} %fusion.25, f32[1344,128]{1,0:T(8,128)S(1)} %fusion.29, f32[1344,128]{1,0:T(8,128)S(1)} %fusion.33, f32[1344,128]{1,0:T(8,128)S(1)} %fusion.12, bf16[128,512]{1,0:T(8,128)(2,1)S(1)} %collective-permute-done.8, bf16[1344,8192]{1,0:T(8,128)(2,1)} %bitcast.111, s32[]{:T(128)S(6)} %select_n.287), kind=kOutput, calls=%fused_computation.12 | convolution fusion | flops 176848896 | bytes 4947972 | tf_op jit(solution)/shard_map/dot_general | solution.py:60
  73.4 2.7 %fusion.223 = (bf16[1344,128]{1,0:T(8,128)(2,1)S(1)}, f32[1344,128]{1,0:T(8,128)}) fusion(f32[1344,128]{1,0:T(8,128)S(1)} %fusion.18, f32[1344,128]{1,0:T(8,128)S(1)} %fusion.9, bf16[128,512]{1,0:T(8,128)(2,1)S(1)} %collective-permute-done.12, bf16[1344,8192]{1,0:T(8,128)(2,1)} %bitcast.113, s32[]{:T(128)S(6)} %select_n.295), kind=kOutput, calls=%fused_computation.174 | convolution fusion | flops 176676864 | bytes 3915780 | tf_op jit(solution)/shard_map/dot_general | solution.py:60
  90.0 1.9 %fusion.165 = bf16[512,128]{1,0:T(8,128)(2,1)S(1)} fusion(bf16[1344,8192]{1,0:T(8,128)(2,1)} %bitcast.114, s32[]{:T(128)S(6)} %select_n.295, bf16[336,128]{1,0:T(8,128)(2,1)S(1)} %collective-permute-done.19, bf16[336,128]{1,0:T(8,128)(2,1)S(1)} %collective-permute-done.18, bf16[336,128]{1,0:T(8,128)(2,1)S(1)} %collective-permute-done.17, ...), kind=kOutput, calls=%fused_computation.111 | convolution fusion | flops 177602560 | bytes 1851396 | tf_op jit(solution)/shard_map/dot_general | solution.py:93
  102.0 1.9 %fusion.132 = bf16[512,128]{1,0:T(8,128)(2,1)S(1)} fusion(bf16[1344,8192]{1,0:T(8,128)(2,1)} %bitcast.118, s32[]{:T(128)S(6)} %select_n.290, bf16[512,128]{1,0:T(8,128)(2,1)S(1)} %collective-permute-done.20, bf16[336,128]{1,0:T(8,128)(2,1)S(1)} %collective-permute-done.19, bf16[336,128]{1,0:T(8,128)(2,1)S(1)} %collective-permute-done.18, ...), kind=kOutput, calls=%fused_computation.100 | convolution fusion | flops 177733632 | bytes 1982468 | tf_op jit(solution)/shard_map/dot_general | solution.py:93
  105.7 1.9 %fusion.144 = bf16[512,128]{1,0:T(8,128)(2,1)S(1)} fusion(bf16[1344,8192]{1,0:T(8,128)(2,1)} %bitcast.119, s32[]{:T(128)S(6)} %select_n.279, bf16[512,128]{1,0:T(8,128)(2,1)S(1)} %collective-permute-done.24, bf16[336,128]{1,0:T(8,128)(2,1)S(1)} %collective-permute-done.19, bf16[336,128]{1,0:T(8,128)(2,1)S(1)} %collective-permute-done.18, ...), kind=kOutput, calls=%fused_computation.104 | convolution fusion | flops 177733632 | bytes 1982468 | tf_op jit(solution)/shard_map/dot_general | solution.py:93
  108.0 1.9 %fusion.135 = bf16[512,128]{1,0:T(8,128)(2,1)S(1)} fusion(bf16[1344,8192]{1,0:T(8,128)(2,1)} %bitcast.120, s32[]{:T(128)S(6)} %select_n.284, bf16[512,128]{1,0:T(8,128)(2,1)S(1)} %collective-permute-done.27, bf16[336,128]{1,0:T(8,128)(2,1)S(1)} %collective-permute-done.19, bf16[336,128]{1,0:T(8,128)(2,1)S(1)} %collective-permute-done.18, ...), kind=kOutput, calls=%fused_computation.101 | convolution fusion | flops 177733632 | bytes 1982468 | tf_op jit(solution)/shard_map/dot_general | solution.py:93
  111.8 1.9 %fusion.129 = bf16[512,128]{1,0:T(8,128)(2,1)S(1)} fusion(bf16[1344,8192]{1,0:T(8,128)(2,1)} %bitcast.121, s32[]{:T(128)S(6)} %select_n.291, bf16[512,128]{1,0:T(8,128)(2,1)S(1)} %collective-permute-done.30, bf16[336,128]{1,0:T(8,128)(2,1)S(1)} %collective-permute-done.19, bf16[336,128]{1,0:T(8,128)(2,1)S(1)} %collective-permute-done.18, ...), kind=kOutput, calls=%fused_computation.99 | convolution fusion | flops 177733632 | bytes 1982468 | tf_op jit(solution)/shard_map/dot_general | solution.py:93
  114.1 1.9 %fusion.141 = bf16[512,128]{1,0:T(8,128)(2,1)S(1)} fusion(bf16[1344,8192]{1,0:T(8,128)(2,1)} %bitcast.122, s32[]{:T(128)S(6)} %select_n.282, bf16[512,128]{1,0:T(8,128)(2,1)S(1)} %collective-permute-done.21, bf16[336,128]{1,0:T(8,128)(2,1)S(1)} %collective-permute-done.19, bf16[336,128]{1,0:T(8,128)(2,1)S(1)} %collective-permute-done.18, ...), kind=kOutput, calls=%fused_computation.103 | convolution fusion | flops 177733632 | bytes 1982468 | tf_op jit(solution)/shard_map/dot_general | solution.py:93
  117.8 1.9 %fusion.156 = bf16[512,128]{1,0:T(8,128)(2,1)S(1)} fusion(bf16[1344,8192]{1,0:T(8,128)(2,1)} %bitcast.123, s32[]{:T(128)S(6)} %select_n.271, bf16[512,128]{1,0:T(8,128)(2,1)S(1)} %collective-permute-done.25, bf16[336,128]{1,0:T(8,128)(2,1)S(1)} %collective-permute-done.19, bf16[336,128]{1,0:T(8,128)(2,1)S(1)} %collective-permute-done.18, ...), kind=kOutput, calls=%fused_computation.108 | convolution fusion | flops 177733632 | bytes 1982468 | tf_op jit(solution)/shard_map/dot_general | solution.py:93
  130.8 1.9 %fusion.150 = bf16[512,128]{1,0:T(8,128)(2,1)S(1)} fusion(bf16[1344,8192]{1,0:T(8,128)(2,1)} %bitcast.127, s32[]{:T(128)S(6)} %select_n.275, bf16[512,128]{1,0:T(8,128)(2,1)S(1)} %collective-permute-done.32, bf16[336,128]{1,0:T(8,128)(2,1)S(1)} %collective-permute-done.19, bf16[336,128]{1,0:T(8,128)(2,1)S(1)} %collective-permute-done.18, ...), kind=kOutput, calls=%fused_computation.106 | convolution fusion | flops 177733632 | bytes 1982468 | tf_op jit(solution)/shard_map/dot_general | solution.py:93
  135.0 2.7 %collective-permute-done.33 = bf16[512,128]{1,0:T(8,128)(2,1)S(1)} collective-permute-done((bf16[512,128]{1,0:T(8,128)(2,1)S(1)}, bf16[512,128]{1,0:T(8,128)(2,1)S(1)}, u32[]{:S(2)}, u32[]{:S(2)}) %collective-permute-start.33) | collective-permute-done | bytes 131104 | tf_op jit(solution)/shard_map/ppermute | solution.py:30
  (102 shorter events, 72.3 us)
Async XLA Ops:
  10.6 25.3 %collective-permute-start.2 = (bf16[128,512]{1,0:T(8,128)(2,1)}, bf16[128,512]{1,0:T(8,128)(2,1)}, u32[]{:S(2)}, u32[]{:S(2)}) collective-permute-start(bf16[128,512]{1,0:T(8,128)(2,1)} %fusion.174), channel_id=1, source_target_pairs={{0,1},{1,2},{2,3},{3,7},{7,6},{6,5},{5,4},{4,0},{8,9},{9,10},{10,1... | collective-permute-start | bytes 393224 | tf_op jit(solution)/shard_map/ppermute | solution.py:30
  13.6 28.2 %collective-permute-start.3 = (bf16[128,512]{1,0:T(8,128)(2,1)}, bf16[128,512]{1,0:T(8,128)(2,1)}, u32[]{:S(2)}, u32[]{:S(2)}) collective-permute-start(bf16[128,512]{1,0:T(8,128)(2,1)} %fusion.174), channel_id=1, source_target_pairs={{0,4},{1,0},{2,1},{3,2},{7,3},{6,7},{5,6},{4,5},{8,12},{9,8},{10,9... | collective-permute-start | bytes 393224 | tf_op jit(solution)/shard_map/ppermute | solution.py:30
  18.7 21.1 %collective-permute-start.1 = (bf16[128,512]{1,0:T(8,128)(2,1)}, bf16[128,512]{1,0:T(8,128)(2,1)}, u32[]{:S(2)}, u32[]{:S(2)}) collective-permute-start(bf16[128,512]{1,0:T(8,128)(2,1)} %fusion.171), channel_id=1, source_target_pairs={{0,4},{1,0},{2,1},{3,2},{7,3},{6,7},{5,6},{4,5},{8,12},{9,8},{10,9... | collective-permute-start | bytes 393224 | tf_op jit(solution)/shard_map/ppermute | solution.py:30
  20.7 25.0 %collective-permute-start = (bf16[128,512]{1,0:T(8,128)(2,1)}, bf16[128,512]{1,0:T(8,128)(2,1)}, u32[]{:S(2)}, u32[]{:S(2)}) collective-permute-start(bf16[128,512]{1,0:T(8,128)(2,1)} %fusion.171), channel_id=1, source_target_pairs={{0,1},{1,2},{2,3},{3,7},{7,6},{6,5},{5,4},{4,0},{8,9},{9,10},{10,1... | collective-permute-start | bytes 393224 | tf_op jit(solution)/shard_map/ppermute | solution.py:30
  35.9 15.7 %collective-permute-start.6 = (bf16[128,512]{1,0:T(8,128)(2,1)}, bf16[128,512]{1,0:T(8,128)(2,1)S(1)}, u32[]{:S(2)}, u32[]{:S(2)}) collective-permute-start(bf16[128,512]{1,0:T(8,128)(2,1)} %collective-permute-done.2), channel_id=1, source_target_pairs={{0,1},{1,2},{2,3},{3,7},{7,6},{6,5},{5,4},{4,0},{8,9},{9,10},{10,1... | collective-permute-start | bytes 393224 | tf_op jit(solution)/shard_map/ppermute | solution.py:30
  39.9 7.9 %collective-permute-start.5 = (bf16[128,512]{1,0:T(8,128)(2,1)}, bf16[128,512]{1,0:T(8,128)(2,1)S(1)}, u32[]{:S(2)}, u32[]{:S(2)}) collective-permute-start(bf16[128,512]{1,0:T(8,128)(2,1)} %collective-permute-done.1), channel_id=1, source_target_pairs={{0,4},{1,0},{2,1},{3,2},{7,3},{6,7},{5,6},{4,5},{8,12},{9,8},{10,9... | collective-permute-start | bytes 393224 | tf_op jit(solution)/shard_map/ppermute | solution.py:30
  41.8 11.8 %collective-permute-start.7 = (bf16[128,512]{1,0:T(8,128)(2,1)}, bf16[128,512]{1,0:T(8,128)(2,1)S(1)}, u32[]{:S(2)}, u32[]{:S(2)}) collective-permute-start(bf16[128,512]{1,0:T(8,128)(2,1)} %collective-permute-done.3), channel_id=1, source_target_pairs={{0,4},{1,0},{2,1},{3,2},{7,3},{6,7},{5,6},{4,5},{8,12},{9,8},{10,9... | collective-permute-start | bytes 393224 | tf_op jit(solution)/shard_map/ppermute | solution.py:30
  45.6 11.8 %collective-permute-start.4 = (bf16[128,512]{1,0:T(8,128)(2,1)}, bf16[128,512]{1,0:T(8,128)(2,1)S(1)}, u32[]{:S(2)}, u32[]{:S(2)}) collective-permute-start(bf16[128,512]{1,0:T(8,128)(2,1)} %collective-permute-done), channel_id=1, source_target_pairs={{0,1},{1,2},{2,3},{3,7},{7,6},{6,5},{5,4},{4,0},{8,9},{9,10},{10,1... | collective-permute-start | bytes 393224 | tf_op jit(solution)/shard_map/ppermute | solution.py:30
  47.8 18.0 %collective-permute-start.9 = (bf16[128,512]{1,0:T(8,128)(2,1)S(1)}, bf16[128,512]{1,0:T(8,128)(2,1)S(1)}, u32[]{:S(2)}, u32[]{:S(2)}) collective-permute-start(bf16[128,512]{1,0:T(8,128)(2,1)S(1)} %collective-permute-done.5), channel_id=1, source_target_pairs={{0,4},{1,0},{2,1},{3,2},{7,3},{6,7},{5,6},{4,5},{8,12},{9,8},{10,9... | collective-permute-start | bytes 393224 | tf_op jit(solution)/shard_map/ppermute | solution.py:30
  51.6 16.1 %collective-permute-start.10 = (bf16[128,512]{1,0:T(8,128)(2,1)S(1)}, bf16[128,512]{1,0:T(8,128)(2,1)S(1)}, u32[]{:S(2)}, u32[]{:S(2)}) collective-permute-start(bf16[128,512]{1,0:T(8,128)(2,1)S(1)} %collective-permute-done.6), channel_id=1, source_target_pairs={{0,1},{1,2},{2,3},{3,7},{7,6},{6,5},{5,4},{4,0},{8,9},{9,10},{10,1... | collective-permute-start | bytes 393224 | tf_op jit(solution)/shard_map/ppermute | solution.py:30
  57.4 6.3 %collective-permute-start.8 = (bf16[128,512]{1,0:T(8,128)(2,1)S(1)}, bf16[128,512]{1,0:T(8,128)(2,1)S(1)}, u32[]{:S(2)}, u32[]{:S(2)}) collective-permute-start(bf16[128,512]{1,0:T(8,128)(2,1)S(1)} %collective-permute-done.4), channel_id=1, source_target_pairs={{0,1},{1,2},{2,3},{3,7},{7,6},{6,5},{5,4},{4,0},{8,9},{9,10},{10,1... | collective-permute-start | bytes 393224 | tf_op jit(solution)/shard_map/ppermute | solution.py:30
  59.6 11.9 %collective-permute-start.13 = (bf16[128,512]{1,0:T(8,128)(2,1)S(1)}, bf16[128,512]{1,0:T(8,128)(2,1)S(1)}, u32[]{:S(2)}, u32[]{:S(2)}) collective-permute-start(bf16[128,512]{1,0:T(8,128)(2,1)S(1)} %collective-permute-done.11), channel_id=1, source_target_pairs={{0,4},{1,0},{2,1},{3,2},{7,3},{6,7},{5,6},{4,5},{8,12},{9,8},{10,9... | collective-permute-start | bytes 393224 | tf_op jit(solution)/shard_map/ppermute | solution.py:30
  63.8 9.6 %collective-permute-start.12 = (bf16[128,512]{1,0:T(8,128)(2,1)S(1)}, bf16[128,512]{1,0:T(8,128)(2,1)S(1)}, u32[]{:S(2)}, u32[]{:S(2)}) collective-permute-start(bf16[128,512]{1,0:T(8,128)(2,1)S(1)} %collective-permute-done.8), channel_id=1, source_target_pairs={{0,1},{1,2},{2,3},{3,7},{7,6},{6,5},{5,4},{4,0},{8,9},{9,10},{10,1... | collective-permute-start | bytes 393224 | tf_op jit(solution)/shard_map/ppermute | solution.py:30
  91.9 10.1 %collective-permute-start.20 = (bf16[512,128]{1,0:T(8,128)(2,1)S(1)}, bf16[512,128]{1,0:T(8,128)(2,1)S(1)}, u32[]{:S(2)}, u32[]{:S(2)}) collective-permute-start(bf16[512,128]{1,0:T(8,128)(2,1)S(1)} %fusion.165), channel_id=1, source_target_pairs={{0,1},{1,2},{2,3},{3,7},{7,6},{6,5},{5,4},{4,0},{8,9},{9,10},{10,1... | collective-permute-start | bytes 393224 | tf_op jit(solution)/shard_map/ppermute | solution.py:30
  95.7 10.1 %collective-permute-start.24 = (bf16[512,128]{1,0:T(8,128)(2,1)S(1)}, bf16[512,128]{1,0:T(8,128)(2,1)S(1)}, u32[]{:S(2)}, u32[]{:S(2)}) collective-permute-start(bf16[512,128]{1,0:T(8,128)(2,1)S(1)} %fusion.159), channel_id=1, source_target_pairs={{0,4},{1,0},{2,1},{3,2},{7,3},{6,7},{5,6},{4,5},{8,12},{9,8},{10,9... | collective-permute-start | bytes 393224 | tf_op jit(solution)/shard_map/ppermute | solution.py:30
  97.9 10.1 %collective-permute-start.27 = (bf16[512,128]{1,0:T(8,128)(2,1)S(1)}, bf16[512,128]{1,0:T(8,128)(2,1)S(1)}, u32[]{:S(2)}, u32[]{:S(2)}) collective-permute-start(bf16[512,128]{1,0:T(8,128)(2,1)S(1)} %fusion.162), channel_id=1, source_target_pairs={{0,1},{1,2},{2,3},{3,7},{7,6},{6,5},{5,4},{4,0},{8,9},{9,10},{10,1... | collective-permute-start | bytes 393224 | tf_op jit(solution)/shard_map/ppermute | solution.py:30
  101.7 10.1 %collective-permute-start.30 = (bf16[512,128]{1,0:T(8,128)(2,1)S(1)}, bf16[512,128]{1,0:T(8,128)(2,1)S(1)}, u32[]{:S(2)}, u32[]{:S(2)}) collective-permute-start(bf16[512,128]{1,0:T(8,128)(2,1)S(1)} %fusion.168), channel_id=1, source_target_pairs={{0,4},{1,0},{2,1},{3,2},{7,3},{6,7},{5,6},{4,5},{8,12},{9,8},{10,9... | collective-permute-start | bytes 393224 | tf_op jit(solution)/shard_map/ppermute | solution.py:30
  104.0 10.1 %collective-permute-start.21 = (bf16[512,128]{1,0:T(8,128)(2,1)S(1)}, bf16[512,128]{1,0:T(8,128)(2,1)S(1)}, u32[]{:S(2)}, u32[]{:S(2)}) collective-permute-start(bf16[512,128]{1,0:T(8,128)(2,1)S(1)} %fusion.132), channel_id=1, source_target_pairs={{0,1},{1,2},{2,3},{3,7},{7,6},{6,5},{5,4},{4,0},{8,9},{9,10},{10,1... | collective-permute-start | bytes 393224 | tf_op jit(solution)/shard_map/ppermute | solution.py:30
  107.7 10.1 %collective-permute-start.25 = (bf16[512,128]{1,0:T(8,128)(2,1)S(1)}, bf16[512,128]{1,0:T(8,128)(2,1)S(1)}, u32[]{:S(2)}, u32[]{:S(2)}) collective-permute-start(bf16[512,128]{1,0:T(8,128)(2,1)S(1)} %fusion.144), channel_id=1, source_target_pairs={{0,4},{1,0},{2,1},{3,2},{7,3},{6,7},{5,6},{4,5},{8,12},{9,8},{10,9... | collective-permute-start | bytes 393224 | tf_op jit(solution)/shard_map/ppermute | solution.py:30
  110.0 10.1 %collective-permute-start.28 = (bf16[512,128]{1,0:T(8,128)(2,1)S(1)}, bf16[512,128]{1,0:T(8,128)(2,1)S(1)}, u32[]{:S(2)}, u32[]{:S(2)}) collective-permute-start(bf16[512,128]{1,0:T(8,128)(2,1)S(1)} %fusion.135), channel_id=1, source_target_pairs={{0,1},{1,2},{2,3},{3,7},{7,6},{6,5},{5,4},{4,0},{8,9},{9,10},{10,1... | collective-permute-start | bytes 393224 | tf_op jit(solution)/shard_map/ppermute | solution.py:30
  113.7 10.1 %collective-permute-start.31 = (bf16[512,128]{1,0:T(8,128)(2,1)S(1)}, bf16[512,128]{1,0:T(8,128)(2,1)S(1)}, u32[]{:S(2)}, u32[]{:S(2)}) collective-permute-start(bf16[512,128]{1,0:T(8,128)(2,1)S(1)} %fusion.129), channel_id=1, source_target_pairs={{0,4},{1,0},{2,1},{3,2},{7,3},{6,7},{5,6},{4,5},{8,12},{9,8},{10,9... | collective-permute-start | bytes 393224 | tf_op jit(solution)/shard_map/ppermute | solution.py:30
  116.0 10.1 %collective-permute-start.22 = (bf16[512,128]{1,0:T(8,128)(2,1)S(1)}, bf16[512,128]{1,0:T(8,128)(2,1)S(1)}, u32[]{:S(2)}, u32[]{:S(2)}) collective-permute-start(bf16[512,128]{1,0:T(8,128)(2,1)S(1)} %fusion.141), channel_id=1, source_target_pairs={{0,1},{1,2},{2,3},{3,7},{7,6},{6,5},{5,4},{4,0},{8,9},{9,10},{10,1... | collective-permute-start | bytes 393224 | tf_op jit(solution)/shard_map/ppermute | solution.py:30
  119.7 13.3 %collective-permute-start.26 = (bf16[512,128]{1,0:T(8,128)(2,1)S(1)}, bf16[512,128]{1,0:T(8,128)(2,1)S(1)}, u32[]{:S(2)}, u32[]{:S(2)}) collective-permute-start(bf16[512,128]{1,0:T(8,128)(2,1)S(1)} %fusion.156), channel_id=1, source_target_pairs={{0,4},{1,0},{2,1},{3,2},{7,3},{6,7},{5,6},{4,5},{8,12},{9,8},{10,9... | collective-permute-start | bytes 393224 | tf_op jit(solution)/shard_map/ppermute | solution.py:30
  122.0 13.0 %collective-permute-start.29 = (bf16[512,128]{1,0:T(8,128)(2,1)S(1)}, bf16[512,128]{1,0:T(8,128)(2,1)S(1)}, u32[]{:S(2)}, u32[]{:S(2)}) collective-permute-start(bf16[512,128]{1,0:T(8,128)(2,1)S(1)} %fusion.147), channel_id=1, source_target_pairs={{0,1},{1,2},{2,3},{3,7},{7,6},{6,5},{5,4},{4,0},{8,9},{9,10},{10,1... | collective-permute-start | bytes 393224 | tf_op jit(solution)/shard_map/ppermute | solution.py:30
  (16 other events, 136.7 us)

commit v2 on v1

v2 whole, which is shorter than its diff:
```python
import functools

import jax
import jax.numpy as jnp
from jax import lax
from jax.experimental import pallas as pl
from jax.experimental.pallas import tpu as pltpu
from jax.sharding import PartitionSpec as P

GROUP = ("dp", "tensor")
BF16 = jnp.bfloat16
F32 = jnp.float32
VMEM = pl.BlockSpec(memory_space=pltpu.VMEM)
SMEM = pl.BlockSpec(memory_space=pltpu.SMEM)
HBM = pl.BlockSpec(memory_space=pltpu.HBM)
NT = (((1,), (1,)), ((), ()))
TN = (((0,), (0,)), ((), ()))


def cycle_order(rows, columns):
    order = []
    for row in range(rows):
        line = [row * columns + column for column in range(columns)]
        order += line if row % 2 == 0 else line[::-1]
    return order


def ring_tools():
    order = cycle_order(lax.axis_size("dp"), lax.axis_size("tensor"))
    size = len(order)
    layers = lax.axis_size("section")

    def along(value, by):
        pairs = [(order[i], order[(i + by) % size]) for i in range(size)]
        return lax.ppermute(value, GROUP, pairs)

    def shifted(value, by):
        return lax.ppermute(value, "section", [(i, (i + by) % layers) for i in range(layers)])

    return order, along, shifted


def call(kernel, name, outs, operands, specs, scratch=(), limit=4, flops=0, bytes_accessed=0):
    return pl.pallas_call(
        kernel,
        out_shape=[pltpu.VMEM(shape, dtype) for shape, dtype in outs],
        in_specs=specs,
        out_specs=[VMEM] * len(outs),
        scratch_shapes=list(scratch),
        compiler_params=pltpu.CompilerParams(vmem_limit_bytes=limit * 2**20),
        cost_estimate=pl.CostEstimate(
            flops=flops, bytes_accessed=bytes_accessed, transcendentals=0
        ),
        name=name,
    )(*operands)


def gather_encode_kernel(ids, cache, weight, bias, rows, latents, held, blocks, sems, *, first, block):
    count = latents.shape[1] // block
    copies = [pltpu.make_async_copy(cache.at[0], held, sems.at[0])]
    for i in range(count):
        source = weight.at[0, pl.ds(first + i * block, block)]
        copies.append(pltpu.make_async_copy(source, blocks.at[i], sems.at[i + 1]))
    for copy in copies:
        copy.start()
    slots = lax.broadcasted_iota(jnp.int32, (held.shape[0], ids.shape[1]), 0)
    picked = (slots == ids[...]).astype(F32).astype(BF16)
    copies[0].wait()
    rows[...] = lax.dot_general(picked, held[...], TN, preferred_element_type=F32).astype(BF16)
    for i in range(count):
        copies[i + 1].wait()
        pre = lax.dot_general(rows[...], blocks[i], NT, preferred_element_type=F32)
        pre = pre + bias[:, first + i * block : first + (i + 1) * block]
        latents[:, i * block : (i + 1) * block] = jnp.maximum(pre, 0.0).astype(BF16)


def encode_kernel(rows, weight, bias, latents, blocks, sems, *, first, block):
    count = latents.shape[1] // block
    copies = []
    for i in range(count):
        source = weight.at[0, pl.ds(first + i * block, block)]
        copies.append(pltpu.make_async_copy(source, blocks.at[i], sems.at[i]))
    for copy in copies:
        copy.start()
    for i in range(count):
        copies[i].wait()
        pre = lax.dot_general(rows[...], blocks[i], NT, preferred_element_type=F32)
        pre = pre + bias[:, first + i * block : first + (i + 1) * block]
        latents[:, i * block : (i + 1) * block] = jnp.maximum(pre, 0.0).astype(BF16)


def columns_of(decoders, owner, which, half):
    start = pl.multiple_of(owner * (2 * half) + which * half, half)
    return decoders[:, pl.ds(start, half)]


def decoded(meta, decoders, pieces, half):
    total = None
    for distance, which, piece in pieces:
        columns = columns_of(decoders, meta[distance], which, half)
        part = lax.dot_general(columns, piece[...], NT, preferred_element_type=F32)
        total = part if total is None else total + part
    return total


def decode_first_kernel(meta, decoders, low, high, incoming, bias, target, total, base):
    half = low.shape[1]
    total[...] = decoded(meta, decoders, [(0, 0, low), (0, 1, high)], half)
    base[...] = incoming[...] + bias[...] - target[...].astype(F32)


def decode_kernel(meta, decoders, before, one, other, total, *, pieces):
    half = one.shape[1]
    (d0, w0), (d1, w1) = pieces
    total[...] = before[...] + decoded(meta, decoders, [(d0, w0, one), (d1, w1, other)], half)


def decode_last_kernel(meta, decoders, before, one, other, own, *sent, pieces):
    half = one.shape[1]
    (d0, w0), (d1, w1) = pieces
    total = before[...] + decoded(meta, decoders, [(d0, w0, one), (d1, w1, other)], half)
    rows = own.shape[0]
    own[...] = total[:rows]
    for offset, out in enumerate(sent, 1):
        out[...] = total[offset * rows : (offset + 1) * rows].astype(BF16)


def error_kernel(meta, own, base, returned, *refs, layers, slot):
    came, (error, beyond, *sent) = refs[: layers - 1], refs[layers - 1 :]
    section = meta[slot]
    within = own[...] + base[...]
    after = jnp.zeros_like(within)
    for offset in range(1, layers):
        part = came[offset - 1][...].astype(F32)
        inside = section >= offset
        within = within + jnp.where(inside, part, 0.0)
        after = after + jnp.where(inside, 0.0, part)
    mine = within.astype(BF16)
    error[...] = mine
    beyond[...] = after
    passed = returned[...]
    for offset in range(1, layers):
        sent[offset - 1][...] = jnp.where(section >= offset, mine, passed)


def gradient(meta, decoders, back, distance, which, half):
    columns = columns_of(decoders, meta[distance], which, half)
    return lax.dot_general(back[...], columns, TN, preferred_element_type=F32)


def gradient_first_kernel(meta, decoders, *refs, layers, pieces, half):
    parts, (back, *outs) = refs[:layers], refs[layers:]
    rows = parts[0].shape[0]
    for offset in range(layers):
        back[offset * rows : (offset + 1) * rows] = parts[offset][...]
    for (distance, which), out in zip(pieces, outs):
        out[...] = gradient(meta, decoders, back, distance, which, half).astype(BF16)


def gradient_kernel(meta, decoders, back, *refs, pieces, half):
    count = len(pieces)
    came, outs = refs[:-count], refs[-count:]
    for i, (distance, which) in enumerate(pieces):
        total = gradient(meta, decoders, back, distance, which, half)
        if came:
            total = total + came[i][...].astype(F32)
        outs[i][...] = total.astype(BF16)


def gradient_own_kernel(meta, decoders, back, low, high, total, *, half):
    for which, came in ((0, low), (1, high)):
        part = gradient(meta, decoders, back, 0, which, half) + came[...].astype(F32)
        total[:, which * half : (which + 1) * half] = part


def gradient_last_kernel(before, low, high, out):
    half = low.shape[1]
    for which, came in ((0, low), (1, high)):
        part = before[:, which * half : (which + 1) * half] + came[...].astype(F32)
        out[which * half : (which + 1) * half, :] = part.T


def tiled_local(cache, token_ids, enc_weight, enc_bias, dec_weight, dec_bias, incoming, target, returned):
    order, along, shifted = ring_tools()
    size = len(order)
    far = size // 2
    layers = lax.axis_size("section")
    rows_, line = lax.axis_size("dp"), lax.axis_size("tensor")
    tokens = token_ids.shape[0]
    slots, width = cache.shape[1:]
    mine = enc_weight.shape[1]
    half = mine // 2
    columns = dec_weight.shape[2]
    outs_all = layers * columns

    def snake(index):
        row, column = index // line, index % line
        return row * line + jnp.where(row % 2 == 0, column, line - 1 - column)

    place = snake(lax.axis_index(GROUP))
    members = snake((place + jnp.arange(size, dtype=jnp.int32)) % size)
    meta = jnp.concatenate([members, lax.axis_index("section").reshape(1)]).astype(jnp.int32)

    weight = pltpu.with_memory_space_constraint(enc_weight, pltpu.HBM)
    kept = pltpu.with_memory_space_constraint(cache, pltpu.HBM)
    decoders = dec_weight.reshape(outs_all, dec_weight.shape[3])

    block = min(256, half)
    count = half // block
    rows, low = call(
        functools.partial(gather_encode_kernel, first=0, block=block),
        "encode_low",
        [((tokens, width), BF16), ((tokens, half), BF16)],
        (token_ids.reshape(1, tokens), kept, weight, enc_bias),
        [VMEM, HBM, HBM, VMEM],
        [
            pltpu.VMEM((slots, width), BF16),
            pltpu.VMEM((count, block, width), BF16),
            pltpu.SemaphoreType.DMA((count + 1,)),
        ],
        limit=16,
        flops=2 * tokens * width * (half + slots),
        bytes_accessed=2 * width * (half + slots),
    )
    (high,) = call(
        functools.partial(encode_kernel, first=half, block=block),
        "encode_high",
        [((tokens, half), BF16)],
        (rows, weight, enc_bias),
        [VMEM, HBM, VMEM],
        [pltpu.VMEM((count, block, width), BF16), pltpu.SemaphoreType.DMA((count,))],
        limit=16,
        flops=2 * tokens * width * half,
        bytes_accessed=2 * width * half,
    )
    piece_flops = 2 * tokens * half * outs_all
    own_low, own_high = low, high
    total, base = call(
        decode_first_kernel,
        "decode_own",
        [((outs_all, tokens), F32), ((columns, tokens), F32)],
        (
            meta,
            decoders,
            own_low,
            own_high,
            incoming[0].T,
            dec_bias.reshape(columns, 1),
            target[0].T,
        ),
        [SMEM] + [VMEM] * 6,
        flops=2 * piece_flops,
    )
    up, down = [low, high], [low, high]
    for step in range(1, far):
        for which in (0, 1):
            up[which] = along(up[which], 1)
            down[which] = along(down[which], -1)
            (total,) = call(
                functools.partial(
                    decode_kernel, pieces=((size - step, which), (step, which))
                ),
                f"decode_{step}_{which}",
                [((outs_all, tokens), F32)],
                (meta, decoders, total, up[which], down[which]),
                [SMEM] + [VMEM] * 4,
                flops=2 * piece_flops,
            )
    own, *sent = call(
        functools.partial(decode_last_kernel, pieces=((far, 0), (far, 1))),
        "decode_last",
        [((columns, tokens), F32)] + [((columns, tokens), BF16)] * (layers - 1),
        (meta, decoders, total, along(up[0], 1), along(down[1], -1)),
        [SMEM] + [VMEM] * 4,
        flops=2 * piece_flops,
    )
    came = [shifted(value, offset) for offset, value in enumerate(sent, 1)]
    error, beyond, *sent = call(
        functools.partial(error_kernel, layers=layers, slot=size),
        "error",
        [((columns, tokens), BF16), ((columns, tokens), F32)]
        + [((columns, tokens), BF16)] * (layers - 1),
        (meta, own, base, returned[0].T, *came),
        [SMEM] + [VMEM] * (layers + 2),
    )
    came = [shifted(value, -offset) for offset, value in enumerate(sent, 1)]
    piece = ((tokens, half), BF16)
    back, *first = call(
        functools.partial(
            gradient_first_kernel, layers=layers, pieces=((far, 0), (far, 1)), half=half
        ),
        "gradient_far",
        [((outs_all, tokens), BF16), piece, piece],
        (meta, decoders, error, *came),
        [SMEM] + [VMEM] * (layers + 1),
        flops=2 * piece_flops,
    )
    outer, inner = first, []
    for step in range(far - 1, -1, -1):
        if outer:
            outer = [along(outer[0], 1), along(outer[1], -1)]
        if step == 0:
            break
        inner = call(
            functools.partial(
                gradient_kernel, pieces=((size - step, 0), (step, 1)), half=half
            ),
            f"gradient_inner_{step}",
            [piece, piece],
            (meta, decoders, back, *inner),
            [SMEM] + [VMEM] * (2 + len(inner)),
            flops=2 * piece_flops,
        )
        inner = [along(inner[0], -1), along(inner[1], 1)]
        outer = call(
            functools.partial(
                gradient_kernel, pieces=((step, 0), (size - step, 1)), half=half
            ),
            f"gradient_outer_{step}",
            [piece, piece],
            (meta, decoders, back, *outer),
            [SMEM] + [VMEM] * (2 + len(outer)),
            flops=2 * piece_flops,
        )
    (part,) = call(
        functools.partial(gradient_own_kernel, half=half),
        "gradient_own",
        [((tokens, mine), F32)],
        (meta, decoders, back, *inner),
        [SMEM] + [VMEM] * 4,
        flops=2 * piece_flops,
    )
    lat_grad = pl.pallas_call(
        gradient_last_kernel,
        out_shape=jax.ShapeDtypeStruct((mine, tokens), F32),
        in_specs=[VMEM] * 3,
        out_specs=VMEM,
        compiler_params=pltpu.CompilerParams(vmem_limit_bytes=4 * 2**20),
        name="gradient_last",
    )(part, *outer)
    return (error.T[None], beyond.T[None], lat_grad[None])


def plain_local(cache, token_ids, enc_weight, enc_bias, dec_weight, dec_bias, incoming, target, returned):
    order, along, shifted = ring_tools()
    size = len(order)
    layers = lax.axis_size("section")
    section = lax.axis_index("section")
    place = jnp.asarray([order.index(i) for i in range(size)], jnp.int32)[lax.axis_index(GROUP)]
    mine = enc_weight.shape[1]
    columns = dec_weight.shape[2]
    tokens = token_ids.shape[0]
    halves = [slice(0, mine // 2), slice(mine // 2, mine)]
    decoders = dec_weight[0].reshape(layers * columns, dec_weight.shape[3])

    def member(distance):
        return jnp.asarray(order, jnp.int32)[(place + distance) % size]

    def part(owner, which):
        start, length = halves[which].start, halves[which].stop - halves[which].start
        return lax.dynamic_slice_in_dim(decoders, owner * mine + start, length, 1)

    def decode(latents, owner, which):
        return lax.dot_general(part(owner, which), latents, NT, preferred_element_type=F32)

    rows = cache[0].at[token_ids].get(mode="promise_in_bounds")
    pre = lax.dot_general(rows, enc_weight[0], NT, preferred_element_type=F32)
    latents = jnp.maximum(pre + enc_bias[0], 0.0).astype(BF16)
    up = [latents[:, cut] for cut in halves]
    down = list(up)
    total = decode(up[0], member(0), 0) + decode(up[1], member(0), 1)
    for step in range(1, (size - 1) // 2 + 1):
        for which in (0, 1):
            up[which] = along(up[which], 1)
            down[which] = along(down[which], -1)
            total = total + decode(up[which], member(-step), which)
            total = total + decode(down[which], member(step), which)
    if size % 2 == 0:
        total = total + decode(along(up[0], 1), member(size // 2), 0)
        total = total + decode(along(down[1], -1), member(size // 2), 1)

    by_offset = total.reshape(layers, columns, tokens)
    within = by_offset[0]
    beyond = jnp.zeros_like(within)
    for offset in range(1, layers):
        came = shifted(by_offset[offset].astype(BF16), offset).astype(F32)
        within = within + jnp.where(section >= offset, came, 0.0)
        beyond = beyond + jnp.where(section < offset, came, 0.0)
    recon = within + incoming[0].T + dec_bias[0][:, None]
    error = (recon - target[0].T.astype(F32)).astype(BF16)
    passed = returned[0].T
    upstream = [error]
    for offset in range(1, layers):
        upstream.append(shifted(jnp.where(section >= offset, error, passed), -offset))
    back = jnp.concatenate(upstream, 0)

    def gradient_of(owner, which):
        return lax.dot_general(part(owner, which), back, TN, preferred_element_type=F32)

    up, down = [None, None], [None, None]
    if size % 2 == 0:
        up[0] = along(gradient_of(member(size // 2), 0).astype(BF16), 1)
        down[1] = along(gradient_of(member(size // 2), 1).astype(BF16), -1)
    for step in range((size - 1) // 2, 0, -1):
        for which in (0, 1):
            rise = gradient_of(member(step), which)
            fall = gradient_of(member(-step), which)
            if up[which] is not None:
                rise = rise + up[which].astype(F32)
            if down[which] is not None:
                fall = fall + down[which].astype(F32)
            up[which] = along(rise.astype(BF16), 1)
            down[which] = along(fall.astype(BF16), -1)
    parts = []
    for which in (0, 1):
        own_part = gradient_of(member(0), which)
        for came in (up[which], down[which]):
            if came is not None:
                own_part = own_part + came.astype(F32)
        parts.append(own_part)
    lat_grad = jnp.concatenate(parts, 0)
    return (error.T[None], beyond.T[None], lat_grad[None])


def local(cache, token_ids, enc_weight, enc_bias, dec_weight, *rest):
    size = lax.axis_size("dp") * lax.axis_size("tensor")
    mine, width = enc_weight.shape[1:]
    whole_tiles = (
        size % 2 == 0
        and size >= 4
        and mine % 256 == 0
        and width % 128 == 0
        and dec_weight.shape[2] % 16 == 0
        and token_ids.shape[0] % 128 == 0
        and cache.shape[1] % 16 == 0
    )
    form = tiled_local if whole_tiles else plain_local
    return form(cache, token_ids, enc_weight, enc_bias, dec_weight, *rest)


def solution(mesh):
    placed = (
        P("section", None, None),
        P(),
        P("section", GROUP, None),
        P("section", GROUP),
        P("section", None, GROUP, None),
        P("section", GROUP),
        P("section", None, GROUP),
        P("section", None, GROUP),
        P("section", None, GROUP),
    )
    return jax.shard_map(
        local,
        mesh=mesh,
        in_specs=placed,
        out_specs=(
            P("section", None, GROUP),
            P("section", None, GROUP),
            P("section", GROUP, None),
        ),
        check_vma=False,
    )
```

time: 142 us -> 103 us (0.73); the launches traced: 141 us -> 103 us
  matrix products: 73.5 us -> 0 us
  Pallas kernels: 0 us -> 33.3 us
  local copies, waits for them, and re-layouts: 4.85 us -> 15.1 us
  between operations: 10.1 us -> 0.9 us
  waiting for transfers between devices: 11.6 us -> 18.1 us
  other arithmetic: 3.57 us -> 0.1 us
    dot_general x34 -> x0, matrix products: 73.5 us -> none  [the longest x16 31.9 us: decode(): lax.dot_general(part(owner, which), latents, (((1,), (1,)), ((), ())), pr...]
    pallas_call x0 -> x20, Pallas kernels: none -> 33.3 us  [the longest x19 32.3 us: call(): pl.pallas_call(kernel, out_shape=[pltpu.VMEM(shape, dtype) for shape, dty...]
    unnamed x12 -> x18, local copies, waits for them, and re-layouts: 0.28 us -> 15 us
    ppermute x28, waiting for transfers between devices: 5.98 us -> 10.6 us  [along(): return lax.ppermute(value, GROUP, pairs)]
    gather x1 -> x0, local copies, waits for them, and re-layouts: 2.55 us -> none  [local(): rows = cache[0].at[token_ids].get(mode='promise_in_bounds')]
    select_n x3 -> x0, other arithmetic: 1.99 us -> none  [the longest x2 1.19 us: local(): jnp.where(section >= offset, error, passed)]
    ppermute x6, waiting for transfers between devices: 5.67 us -> 7.56 us  [shifted(): lax.ppermute(value, 'section', [(i, (i + by) % layers) for i in range(lay...]
    broadcast_in_dim x2 -> x0, other arithmetic: 1.55 us -> none  [local(): return (error.T[None], beyond.T[None], lat_grad[None])]
  transfers between devices with their start and end apart: 34 -> 34, of which waited for: 8 -> 14; matrix products, arithmetic and copies ran while one was open for 45% -> 1% of each run, Pallas kernels for 0% -> 22%
where the time goes in v2:
time: 103 us
  starting transfers between devices  35.8 us (35%)
  Pallas kernels  33.3 us (32%)
  waiting for transfers between devices  18.1 us (18%)
  local copies, waits for them, and re-layouts  15.1 us (15%)
    pallas_call x19, Pallas kernels, call(): pl.pallas_call(kernel, out_shape=[pltpu.VMEM(shape, dtype) for shape, dty...  32.3 us
    ppermute x28, starting transfers between devices, along(): return lax.ppermute(value, GROUP, pairs)  30.3 us
    unnamed x18, local copies, waits for them, and re-layouts  15 us
    ppermute x28, waiting for transfers between devices, along(): return lax.ppermute(value, GROUP, pairs)  10.6 us
    ppermute x6, waiting for transfers between devices, shifted(): lax.ppermute(value, 'section', [(i, (i + by) % layers) for i in range(lay...  7.56 us
    ppermute x6, starting transfers between devices, shifted(): lax.ppermute(value, 'section', [(i, (i + by) % layers) for i in range(lay...  5.5 us
  transfers between devices with their start and end apart: 34, of which 14 were waited for; matrix products, arithmetic and copies ran while one was open for 1% of the time, Pallas kernels for 22%

profile of v2, /device:TPU:0, one launch (start us, length us, event | category | flops | bytes accessed | tf_op | source)
XLA Modules:
  0.0 103.2 jit_solution(5825884535471937750)
XLA Ops:
  2.0 5.9 %encode_low.1 = (bf16[128,5376]{1,0:T(8,128)(2,1)S(1)}, bf16[128,512]{1,0:T(8,128)(2,1)S(1)}) custom-call(s32[1,128]{1,0:T(1,128)S(1)} %bitcast.41, bf16[1,256,5376]{2,1,0:T(8,128)(2,1)} %cache.1, bf16[1,1024,5376]{2,1,0:T(8,128)(2,1)} %weight.3, f32[1,1024]{1,0:T(1,128)S(1)} %copy-done.5), custom_call_target="tpu_custom_call" | custom-call | flops 1056964608 | bytes 8257536 | tf_op jit(solution)/shard_map/encode_low/pallas_call | solution.py:44
  7.9 3.1 %collective-permute-start = (bf16[128,512]{1,0:T(8,128)(2,1)S(1)}, bf16[128,512]{1,0:T(8,128)(2,1)S(1)}, u32[]{:S(2)}, u32[]{:S(2)}) collective-permute-start(bf16[128,512]{1,0:T(8,128)(2,1)S(1)} %get-tuple-element.31.low), channel_id=1, source_target_pairs={{0,1},{1,2},{2,3},{3,7},{7,6},{6,5},{5,4},{4,0},{8,9},{9,10},{10,1... | collective-permute-start | bytes 393224 | tf_op jit(solution)/shard_map/ppermute | solution.py:35
  11.0 5.0 %encode_high.1.high = bf16[128,512]{1,0:T(8,128)(2,1)S(1)} custom-call(bf16[128,5376]{1,0:T(8,128)(2,1)S(1)} %get-tuple-element.32.rows, bf16[1,1024,5376]{2,1,0:T(8,128)(2,1)} %weight.3, f32[1,1024]{1,0:T(1,128)S(1)} %copy-done.5), custom_call_target="tpu_custom_call" | custom-call | flops 704643072 | bytes 5505024 | tf_op jit(solution)/shard_map/encode_high/pallas_call | solution.py:44
  16.1 1.9 %collective-permute-start.1 = (bf16[128,512]{1,0:T(8,128)(2,1)S(1)}, bf16[128,512]{1,0:T(8,128)(2,1)S(1)}, u32[]{:S(2)}, u32[]{:S(2)}) collective-permute-start(bf16[128,512]{1,0:T(8,128)(2,1)S(1)} %get-tuple-element.31.low), channel_id=1, source_target_pairs={{0,4},{1,0},{2,1},{3,2},{7,3},{6,7},{5,6},{4,5},{8,12},{9,8},{10,9... | collective-permute-start | bytes 393224 | tf_op jit(solution)/shard_map/ppermute | solution.py:35
  18.2 2.0 %collective-permute-start.4 = (bf16[128,512]{1,0:T(8,128)(2,1)S(1)}, bf16[128,512]{1,0:T(8,128)(2,1)S(1)}, u32[]{:S(2)}, u32[]{:S(2)}) collective-permute-start(bf16[128,512]{1,0:T(8,128)(2,1)S(1)} %collective-permute-done.one), channel_id=1, source_target_pairs={{0,1},{1,2},{2,3},{3,7},{7,6},{6,5},{5,4},{4,0},{8,9},{9,10},{10,1... | collective-permute-start | bytes 393224 | tf_op jit(solution)/shard_map/ppermute | solution.py:35
  20.1 2.4 %collective-permute-done.3.other = bf16[128,512]{1,0:T(8,128)(2,1)S(1)} collective-permute-done((bf16[128,512]{1,0:T(8,128)(2,1)S(1)}, bf16[128,512]{1,0:T(8,128)(2,1)S(1)}, u32[]{:S(2)}, u32[]{:S(2)}) %collective-permute-start.3) | collective-permute-done | bytes 131104 | tf_op jit(solution)/shard_map/ppermute | solution.py:35
  22.5 2.8 %collective-permute-done.1.other = bf16[128,512]{1,0:T(8,128)(2,1)S(1)} collective-permute-done((bf16[128,512]{1,0:T(8,128)(2,1)S(1)}, bf16[128,512]{1,0:T(8,128)(2,1)S(1)}, u32[]{:S(2)}, u32[]{:S(2)}) %collective-permute-start.1) | collective-permute-done | bytes 131104 | tf_op jit(solution)/shard_map/ppermute | solution.py:35
  25.3 2.0 %collective-permute-start.6 = (bf16[128,512]{1,0:T(8,128)(2,1)S(1)}, bf16[128,512]{1,0:T(8,128)(2,1)S(1)}, u32[]{:S(2)}, u32[]{:S(2)}) collective-permute-start(bf16[128,512]{1,0:T(8,128)(2,1)S(1)} %collective-permute-done.2.one), channel_id=1, source_target_pairs={{0,1},{1,2},{2,3},{3,7},{7,6},{6,5},{5,4},{4,0},{8,9},{9,10},{10,1... | collective-permute-start | bytes 393224 | tf_op jit(solution)/shard_map/ppermute | solution.py:35
  27.3 1.6 %collective-permute-start.8 = (bf16[128,512]{1,0:T(8,128)(2,1)S(1)}, bf16[128,512]{1,0:T(8,128)(2,1)S(1)}, u32[]{:S(2)}, u32[]{:S(2)}) collective-permute-start(bf16[128,512]{1,0:T(8,128)(2,1)S(1)} %collective-permute-done.4.one), channel_id=1, source_target_pairs={{0,1},{1,2},{2,3},{3,7},{7,6},{6,5},{5,4},{4,0},{8,9},{9,10},{10,1... | collective-permute-start | bytes 393224 | tf_op jit(solution)/shard_map/ppermute | solution.py:35
  29.6 7.3 %copy-done = bf16[1,4,336,8192]{3,2,1,0:T(8,128)(2,1)S(1)} copy-done((bf16[1,4,336,8192]{3,2,1,0:T(8,128)(2,1)S(1)}, bf16[1,4,336,8192]{3,2,1,0:T(8,128)(2,1)}, u32[]{:S(2)}) %copy-start) | copy-done | bytes 22020120
  39.1 5.0 %copy-done.1 = bf16[1,4,336,8192]{3,2,1,0:T(8,128)(2,1)S(1)} copy-done((bf16[1,4,336,8192]{3,2,1,0:T(8,128)(2,1)S(1)}, bf16[1,4,336,8192]{3,2,1,0:T(8,128)(2,1)}, u32[]{:S(2)}) %copy-start.1) | copy-done | bytes 22020120
  45.6 1.6 %collective-permute-start.10 = (bf16[128,512]{1,0:T(8,128)(2,1)S(1)}, bf16[128,512]{1,0:T(8,128)(2,1)S(1)}, u32[]{:S(2)}, u32[]{:S(2)}) collective-permute-start(bf16[128,512]{1,0:T(8,128)(2,1)S(1)} %collective-permute-done.6.one), channel_id=1, source_target_pairs={{0,1},{1,2},{2,3},{3,7},{7,6},{6,5},{5,4},{4,0},{8,9},{9,10},{10,1... | collective-permute-start | bytes 393224 | tf_op jit(solution)/shard_map/ppermute | solution.py:35
  49.1 1.6 %collective-permute-start.12 = (bf16[128,512]{1,0:T(8,128)(2,1)S(1)}, bf16[128,512]{1,0:T(8,128)(2,1)S(1)}, u32[]{:S(2)}, u32[]{:S(2)}) collective-permute-start(bf16[128,512]{1,0:T(8,128)(2,1)S(1)} %collective-permute-done.8.one), channel_id=1, source_target_pairs={{0,1},{1,2},{2,3},{3,7},{7,6},{6,5},{5,4},{4,0},{8,9},{9,10},{10,1... | collective-permute-start | bytes 393224 | tf_op jit(solution)/shard_map/ppermute | solution.py:35
  58.0 1.5 %collective-permute-start.15 = (bf16[336,128]{1,0:T(8,128)(2,1)S(1)}, bf16[336,128]{1,0:T(8,128)(2,1)S(1)}, u32[]{:S(2)}, u32[]{:S(2)}) collective-permute-start(bf16[336,128]{1,0:T(8,128)(2,1)S(1)} %get-tuple-element.37), channel_id=1, source_target_pairs={{0,16},{8,24},{16,0},{24,8},{1,17},{9,25},{17,1},{25,9},{2,18},{10... | collective-permute-start | bytes 258056 | tf_op jit(solution)/shard_map/ppermute | solution.py:38
  64.4 2.0 %collective-permute-start.17 = (bf16[336,128]{1,0:T(8,128)(2,1)S(1)}, bf16[336,128]{1,0:T(8,128)(2,1)S(1)}, u32[]{:S(2)}, u32[]{:S(2)}) collective-permute-start(bf16[336,128]{1,0:T(8,128)(2,1)S(1)} %get-tuple-element.41), channel_id=1, source_target_pairs={{0,24},{8,0},{16,8},{24,16},{1,25},{9,1},{17,9},{25,17},{2,26},{10... | collective-permute-start | bytes 258056 | tf_op jit(solution)/shard_map/ppermute | solution.py:38
  66.9 1.9 %collective-permute-done.17.refs_1_ = bf16[336,128]{1,0:T(8,128)(2,1)S(1)} collective-permute-done((bf16[336,128]{1,0:T(8,128)(2,1)S(1)}, bf16[336,128]{1,0:T(8,128)(2,1)S(1)}, u32[]{:S(2)}, u32[]{:S(2)}) %collective-permute-start.17) | collective-permute-done | bytes 86048 | tf_op jit(solution)/shard_map/ppermute | solution.py:38
  68.8 2.9 %collective-permute-done.18.refs_2_ = bf16[336,128]{1,0:T(8,128)(2,1)S(1)} collective-permute-done((bf16[336,128]{1,0:T(8,128)(2,1)S(1)}, bf16[336,128]{1,0:T(8,128)(2,1)S(1)}, u32[]{:S(2)}, u32[]{:S(2)}) %collective-permute-start.18) | collective-permute-done | bytes 86048 | tf_op jit(solution)/shard_map/ppermute | solution.py:38
  72.9 1.6 %collective-permute-start.26 = (bf16[128,512]{1,0:T(8,128)(2,1)S(1)}, bf16[128,512]{1,0:T(8,128)(2,1)S(1)}, u32[]{:S(2)}, u32[]{:S(2)}) collective-permute-start(bf16[128,512]{1,0:T(8,128)(2,1)S(1)} %get-tuple-element.51), channel_id=1, source_target_pairs={{0,1},{1,2},{2,3},{3,7},{7,6},{6,5},{5,4},{4,0},{8,9},{9,10},{10,1... | collective-permute-start | bytes 393224 | tf_op jit(solution)/shard_map/ppermute | solution.py:35
  76.6 1.6 %collective-permute-start.21 = (bf16[128,512]{1,0:T(8,128)(2,1)S(1)}, bf16[128,512]{1,0:T(8,128)(2,1)S(1)}, u32[]{:S(2)}, u32[]{:S(2)}) collective-permute-start(bf16[128,512]{1,0:T(8,128)(2,1)S(1)} %get-tuple-element.46), channel_id=1, source_target_pairs={{0,1},{1,2},{2,3},{3,7},{7,6},{6,5},{5,4},{4,0},{8,9},{9,10},{10,1... | collective-permute-start | bytes 393224 | tf_op jit(solution)/shard_map/ppermute | solution.py:35
  78.5 1.5 %collective-permute-done.27.refs_1_ = bf16[128,512]{1,0:T(8,128)(2,1)S(1)} collective-permute-done((bf16[128,512]{1,0:T(8,128)(2,1)S(1)}, bf16[128,512]{1,0:T(8,128)(2,1)S(1)}, u32[]{:S(2)}, u32[]{:S(2)}) %collective-permute-start.27) | collective-permute-done | bytes 131104 | tf_op jit(solution)/shard_map/ppermute | solution.py:35
  81.2 1.6 %collective-permute-start.28 = (bf16[128,512]{1,0:T(8,128)(2,1)S(1)}, bf16[128,512]{1,0:T(8,128)(2,1)S(1)}, u32[]{:S(2)}, u32[]{:S(2)}) collective-permute-start(bf16[128,512]{1,0:T(8,128)(2,1)S(1)} %get-tuple-element.53), channel_id=1, source_target_pairs={{0,1},{1,2},{2,3},{3,7},{7,6},{6,5},{5,4},{4,0},{8,9},{9,10},{10,1... | collective-permute-start | bytes 393224 | tf_op jit(solution)/shard_map/ppermute | solution.py:35
  84.9 1.6 %collective-permute-start.23 = (bf16[128,512]{1,0:T(8,128)(2,1)S(1)}, bf16[128,512]{1,0:T(8,128)(2,1)S(1)}, u32[]{:S(2)}, u32[]{:S(2)}) collective-permute-start(bf16[128,512]{1,0:T(8,128)(2,1)S(1)} %get-tuple-element.48), channel_id=1, source_target_pairs={{0,1},{1,2},{2,3},{3,7},{7,6},{6,5},{5,4},{4,0},{8,9},{9,10},{10,1... | collective-permute-start | bytes 393224 | tf_op jit(solution)/shard_map/ppermute | solution.py:35
  88.9 1.6 %collective-permute-start.30 = (bf16[128,512]{1,0:T(8,128)(2,1)S(1)}, bf16[128,512]{1,0:T(8,128)(2,1)S(1)}, u32[]{:S(2)}, u32[]{:S(2)}) collective-permute-start(bf16[128,512]{1,0:T(8,128)(2,1)S(1)} %get-tuple-element.55), channel_id=1, source_target_pairs={{0,1},{1,2},{2,3},{3,7},{7,6},{6,5},{5,4},{4,0},{8,9},{9,10},{10,1... | collective-permute-start | bytes 393224 | tf_op jit(solution)/shard_map/ppermute | solution.py:35
  92.7 1.5 %collective-permute-start.25 = (bf16[128,512]{1,0:T(8,128)(2,1)S(1)}, bf16[128,512]{1,0:T(8,128)(2,1)S(1)}, u32[]{:S(2)}, u32[]{:S(2)}) collective-permute-start(bf16[128,512]{1,0:T(8,128)(2,1)S(1)} %get-tuple-element.50), channel_id=1, source_target_pairs={{0,1},{1,2},{2,3},{3,7},{7,6},{6,5},{5,4},{4,0},{8,9},{9,10},{10,1... | collective-permute-start | bytes 393224 | tf_op jit(solution)/shard_map/ppermute | solution.py:35
  (85 shorter events, 40.8 us)
Async XLA Ops:
  7.9 10.3 %collective-permute-start = (bf16[128,512]{1,0:T(8,128)(2,1)S(1)}, bf16[128,512]{1,0:T(8,128)(2,1)S(1)}, u32[]{:S(2)}, u32[]{:S(2)}) collective-permute-start(bf16[128,512]{1,0:T(8,128)(2,1)S(1)} %get-tuple-element.31.low), channel_id=1, source_target_pairs={{0,1},{1,2},{2,3},{3,7},{7,6},{6,5},{5,4},{4,0},{8,9},{9,10},{10,1... | collective-permute-start | bytes 393224 | tf_op jit(solution)/shard_map/ppermute | solution.py:35
  16.0 6.5 %collective-permute-start.3 = (bf16[128,512]{1,0:T(8,128)(2,1)S(1)}, bf16[128,512]{1,0:T(8,128)(2,1)S(1)}, u32[]{:S(2)}, u32[]{:S(2)}) collective-permute-start(bf16[128,512]{1,0:T(8,128)(2,1)S(1)} %encode_high.1.high), channel_id=1, source_target_pairs={{0,4},{1,0},{2,1},{3,2},{7,3},{6,7},{5,6},{4,5},{8,12},{9,8},{10,9... | collective-permute-start | bytes 393224 | tf_op jit(solution)/shard_map/ppermute | solution.py:35
  16.1 9.2 %collective-permute-start.1 = (bf16[128,512]{1,0:T(8,128)(2,1)S(1)}, bf16[128,512]{1,0:T(8,128)(2,1)S(1)}, u32[]{:S(2)}, u32[]{:S(2)}) collective-permute-start(bf16[128,512]{1,0:T(8,128)(2,1)S(1)} %get-tuple-element.31.low), channel_id=1, source_target_pairs={{0,4},{1,0},{2,1},{3,2},{7,3},{6,7},{5,6},{4,5},{8,12},{9,8},{10,9... | collective-permute-start | bytes 393224 | tf_op jit(solution)/shard_map/ppermute | solution.py:35
  18.0 7.3 %collective-permute-start.2 = (bf16[128,512]{1,0:T(8,128)(2,1)S(1)}, bf16[128,512]{1,0:T(8,128)(2,1)S(1)}, u32[]{:S(2)}, u32[]{:S(2)}) collective-permute-start(bf16[128,512]{1,0:T(8,128)(2,1)S(1)} %encode_high.1.high), channel_id=1, source_target_pairs={{0,1},{1,2},{2,3},{3,7},{7,6},{6,5},{5,4},{4,0},{8,9},{9,10},{10,1... | collective-permute-start | bytes 393224 | tf_op jit(solution)/shard_map/ppermute | solution.py:35
  18.2 9.2 %collective-permute-start.4 = (bf16[128,512]{1,0:T(8,128)(2,1)S(1)}, bf16[128,512]{1,0:T(8,128)(2,1)S(1)}, u32[]{:S(2)}, u32[]{:S(2)}) collective-permute-start(bf16[128,512]{1,0:T(8,128)(2,1)S(1)} %collective-permute-done.one), channel_id=1, source_target_pairs={{0,1},{1,2},{2,3},{3,7},{7,6},{6,5},{5,4},{4,0},{8,9},{9,10},{10,1... | collective-permute-start | bytes 393224 | tf_op jit(solution)/shard_map/ppermute | solution.py:35
  22.5 6.4 %collective-permute-start.7 = (bf16[128,512]{1,0:T(8,128)(2,1)S(1)}, bf16[128,512]{1,0:T(8,128)(2,1)S(1)}, u32[]{:S(2)}, u32[]{:S(2)}) collective-permute-start(bf16[128,512]{1,0:T(8,128)(2,1)S(1)} %collective-permute-done.3.other), channel_id=1, source_target_pairs={{0,4},{1,0},{2,1},{3,2},{7,3},{6,7},{5,6},{4,5},{8,12},{9,8},{10,9... | collective-permute-start | bytes 393224 | tf_op jit(solution)/shard_map/ppermute | solution.py:35
  25.3 13.0 %collective-permute-start.5 = (bf16[128,512]{1,0:T(8,128)(2,1)S(1)}, bf16[128,512]{1,0:T(8,128)(2,1)S(1)}, u32[]{:S(2)}, u32[]{:S(2)}) collective-permute-start(bf16[128,512]{1,0:T(8,128)(2,1)S(1)} %collective-permute-done.1.other), channel_id=1, source_target_pairs={{0,4},{1,0},{2,1},{3,2},{7,3},{6,7},{5,6},{4,5},{8,12},{9,8},{10,9... | collective-permute-start | bytes 393224 | tf_op jit(solution)/shard_map/ppermute | solution.py:35
  25.3 20.3 %collective-permute-start.6 = (bf16[128,512]{1,0:T(8,128)(2,1)S(1)}, bf16[128,512]{1,0:T(8,128)(2,1)S(1)}, u32[]{:S(2)}, u32[]{:S(2)}) collective-permute-start(bf16[128,512]{1,0:T(8,128)(2,1)S(1)} %collective-permute-done.2.one), channel_id=1, source_target_pairs={{0,1},{1,2},{2,3},{3,7},{7,6},{6,5},{5,4},{4,0},{8,9},{9,10},{10,1... | collective-permute-start | bytes 393224 | tf_op jit(solution)/shard_map/ppermute | solution.py:35
  27.3 21.8 %collective-permute-start.8 = (bf16[128,512]{1,0:T(8,128)(2,1)S(1)}, bf16[128,512]{1,0:T(8,128)(2,1)S(1)}, u32[]{:S(2)}, u32[]{:S(2)}) collective-permute-start(bf16[128,512]{1,0:T(8,128)(2,1)S(1)} %collective-permute-done.4.one), channel_id=1, source_target_pairs={{0,1},{1,2},{2,3},{3,7},{7,6},{6,5},{5,4},{4,0},{8,9},{9,10},{10,1... | collective-permute-start | bytes 393224 | tf_op jit(solution)/shard_map/ppermute | solution.py:35
  28.9 19.7 %collective-permute-start.11 = (bf16[128,512]{1,0:T(8,128)(2,1)S(1)}, bf16[128,512]{1,0:T(8,128)(2,1)S(1)}, u32[]{:S(2)}, u32[]{:S(2)}) collective-permute-start(bf16[128,512]{1,0:T(8,128)(2,1)S(1)} %collective-permute-done.7.other), channel_id=1, source_target_pairs={{0,4},{1,0},{2,1},{3,2},{7,3},{6,7},{5,6},{4,5},{8,12},{9,8},{10,9... | collective-permute-start | bytes 393224 | tf_op jit(solution)/shard_map/ppermute | solution.py:35
  38.3 15.3 %collective-permute-start.9 = (bf16[128,512]{1,0:T(8,128)(2,1)S(1)}, bf16[128,512]{1,0:T(8,128)(2,1)S(1)}, u32[]{:S(2)}, u32[]{:S(2)}) collective-permute-start(bf16[128,512]{1,0:T(8,128)(2,1)S(1)} %collective-permute-done.5.other), channel_id=1, source_target_pairs={{0,4},{1,0},{2,1},{3,2},{7,3},{6,7},{5,6},{4,5},{8,12},{9,8},{10,9... | collective-permute-start | bytes 393224 | tf_op jit(solution)/shard_map/ppermute | solution.py:35
  45.6 9.5 %collective-permute-start.10 = (bf16[128,512]{1,0:T(8,128)(2,1)S(1)}, bf16[128,512]{1,0:T(8,128)(2,1)S(1)}, u32[]{:S(2)}, u32[]{:S(2)}) collective-permute-start(bf16[128,512]{1,0:T(8,128)(2,1)S(1)} %collective-permute-done.6.one), channel_id=1, source_target_pairs={{0,1},{1,2},{2,3},{3,7},{7,6},{6,5},{5,4},{4,0},{8,9},{9,10},{10,1... | collective-permute-start | bytes 393224 | tf_op jit(solution)/shard_map/ppermute | solution.py:35
  48.6 7.9 %collective-permute-start.13 = (bf16[128,512]{1,0:T(8,128)(2,1)S(1)}, bf16[128,512]{1,0:T(8,128)(2,1)S(1)}, u32[]{:S(2)}, u32[]{:S(2)}) collective-permute-start(bf16[128,512]{1,0:T(8,128)(2,1)S(1)} %collective-permute-done.11.other), channel_id=1, source_target_pairs={{0,4},{1,0},{2,1},{3,2},{7,3},{6,7},{5,6},{4,5},{8,12},{9,8},{10,9... | collective-permute-start | bytes 393224 | tf_op jit(solution)/shard_map/ppermute | solution.py:35
  49.1 7.4 %collective-permute-start.12 = (bf16[128,512]{1,0:T(8,128)(2,1)S(1)}, bf16[128,512]{1,0:T(8,128)(2,1)S(1)}, u32[]{:S(2)}, u32[]{:S(2)}) collective-permute-start(bf16[128,512]{1,0:T(8,128)(2,1)S(1)} %collective-permute-done.8.one), channel_id=1, source_target_pairs={{0,1},{1,2},{2,3},{3,7},{7,6},{6,5},{5,4},{4,0},{8,9},{9,10},{10,1... | collective-permute-start | bytes 393224 | tf_op jit(solution)/shard_map/ppermute | solution.py:35
  58.0 5.4 %collective-permute-start.15 = (bf16[336,128]{1,0:T(8,128)(2,1)S(1)}, bf16[336,128]{1,0:T(8,128)(2,1)S(1)}, u32[]{:S(2)}, u32[]{:S(2)}) collective-permute-start(bf16[336,128]{1,0:T(8,128)(2,1)S(1)} %get-tuple-element.37), channel_id=1, source_target_pairs={{0,16},{8,24},{16,0},{24,8},{1,17},{9,25},{17,1},{25,9},{2,18},{10... | collective-permute-start | bytes 258056 | tf_op jit(solution)/shard_map/ppermute | solution.py:38
  72.9 5.6 %collective-permute-start.26 = (bf16[128,512]{1,0:T(8,128)(2,1)S(1)}, bf16[128,512]{1,0:T(8,128)(2,1)S(1)}, u32[]{:S(2)}, u32[]{:S(2)}) collective-permute-start(bf16[128,512]{1,0:T(8,128)(2,1)S(1)} %get-tuple-element.51), channel_id=1, source_target_pairs={{0,1},{1,2},{2,3},{3,7},{7,6},{6,5},{5,4},{4,0},{8,9},{9,10},{10,1... | collective-permute-start | bytes 393224 | tf_op jit(solution)/shard_map/ppermute | solution.py:35
  74.5 5.5 %collective-permute-start.27 = (bf16[128,512]{1,0:T(8,128)(2,1)S(1)}, bf16[128,512]{1,0:T(8,128)(2,1)S(1)}, u32[]{:S(2)}, u32[]{:S(2)}) collective-permute-start(bf16[128,512]{1,0:T(8,128)(2,1)S(1)} %get-tuple-element.52), channel_id=1, source_target_pairs={{0,4},{1,0},{2,1},{3,2},{7,3},{6,7},{5,6},{4,5},{8,12},{9,8},{10,9... | collective-permute-start | bytes 393224 | tf_op jit(solution)/shard_map/ppermute | solution.py:35
  76.1 7.2 %collective-permute-start.20 = (bf16[128,512]{1,0:T(8,128)(2,1)S(1)}, bf16[128,512]{1,0:T(8,128)(2,1)S(1)}, u32[]{:S(2)}, u32[]{:S(2)}) collective-permute-start(bf16[128,512]{1,0:T(8,128)(2,1)S(1)} %get-tuple-element.45), channel_id=1, source_target_pairs={{0,4},{1,0},{2,1},{3,2},{7,3},{6,7},{5,6},{4,5},{8,12},{9,8},{10,9... | collective-permute-start | bytes 393224 | tf_op jit(solution)/shard_map/ppermute | solution.py:35
  76.6 6.7 %collective-permute-start.21 = (bf16[128,512]{1,0:T(8,128)(2,1)S(1)}, bf16[128,512]{1,0:T(8,128)(2,1)S(1)}, u32[]{:S(2)}, u32[]{:S(2)}) collective-permute-start(bf16[128,512]{1,0:T(8,128)(2,1)S(1)} %get-tuple-element.46), channel_id=1, source_target_pairs={{0,1},{1,2},{2,3},{3,7},{7,6},{6,5},{5,4},{4,0},{8,9},{9,10},{10,1... | collective-permute-start | bytes 393224 | tf_op jit(solution)/shard_map/ppermute | solution.py:35
  81.2 5.6 %collective-permute-start.28 = (bf16[128,512]{1,0:T(8,128)(2,1)S(1)}, bf16[128,512]{1,0:T(8,128)(2,1)S(1)}, u32[]{:S(2)}, u32[]{:S(2)}) collective-permute-start(bf16[128,512]{1,0:T(8,128)(2,1)S(1)} %get-tuple-element.53), channel_id=1, source_target_pairs={{0,1},{1,2},{2,3},{3,7},{7,6},{6,5},{5,4},{4,0},{8,9},{9,10},{10,1... | collective-permute-start | bytes 393224 | tf_op jit(solution)/shard_map/ppermute | solution.py:35
  84.4 6.6 %collective-permute-start.22 = (bf16[128,512]{1,0:T(8,128)(2,1)S(1)}, bf16[128,512]{1,0:T(8,128)(2,1)S(1)}, u32[]{:S(2)}, u32[]{:S(2)}) collective-permute-start(bf16[128,512]{1,0:T(8,128)(2,1)S(1)} %get-tuple-element.47), channel_id=1, source_target_pairs={{0,4},{1,0},{2,1},{3,2},{7,3},{6,7},{5,6},{4,5},{8,12},{9,8},{10,9... | collective-permute-start | bytes 393224 | tf_op jit(solution)/shard_map/ppermute | solution.py:35
  84.9 6.1 %collective-permute-start.23 = (bf16[128,512]{1,0:T(8,128)(2,1)S(1)}, bf16[128,512]{1,0:T(8,128)(2,1)S(1)}, u32[]{:S(2)}, u32[]{:S(2)}) collective-permute-start(bf16[128,512]{1,0:T(8,128)(2,1)S(1)} %get-tuple-element.48), channel_id=1, source_target_pairs={{0,1},{1,2},{2,3},{3,7},{7,6},{6,5},{5,4},{4,0},{8,9},{9,10},{10,1... | collective-permute-start | bytes 393224 | tf_op jit(solution)/shard_map/ppermute | solution.py:35
  92.2 7.8 %collective-permute-start.24 = (bf16[128,512]{1,0:T(8,128)(2,1)S(1)}, bf16[128,512]{1,0:T(8,128)(2,1)S(1)}, u32[]{:S(2)}, u32[]{:S(2)}) collective-permute-start(bf16[128,512]{1,0:T(8,128)(2,1)S(1)} %get-tuple-element.49), channel_id=1, source_target_pairs={{0,4},{1,0},{2,1},{3,2},{7,3},{6,7},{5,6},{4,5},{8,12},{9,8},{10,9... | collective-permute-start | bytes 393224 | tf_op jit(solution)/shard_map/ppermute | solution.py:35
  92.7 7.3 %collective-permute-start.25 = (bf16[128,512]{1,0:T(8,128)(2,1)S(1)}, bf16[128,512]{1,0:T(8,128)(2,1)S(1)}, u32[]{:S(2)}, u32[]{:S(2)}) collective-permute-start(bf16[128,512]{1,0:T(8,128)(2,1)S(1)} %get-tuple-element.50), channel_id=1, source_target_pairs={{0,1},{1,2},{2,3},{3,7},{7,6},{6,5},{5,4},{4,0},{8,9},{9,10},{10,1... | collective-permute-start | bytes 393224 | tf_op jit(solution)/shard_map/ppermute | solution.py:35
  (18 other events, 154.0 us)

commit v3 on v2

v3 whole, which is shorter than its diff:
```python
import functools

import jax
import jax.numpy as jnp
from jax import lax
from jax.experimental import pallas as pl
from jax.experimental.pallas import tpu as pltpu
from jax.sharding import PartitionSpec as P

GROUP = ("dp", "tensor")
BF16 = jnp.bfloat16
F32 = jnp.float32
VMEM = pl.BlockSpec(memory_space=pltpu.VMEM)
HBM = pl.BlockSpec(memory_space=pltpu.HBM)
NT = (((1,), (1,)), ((), ()))
TN = (((0,), (0,)), ((), ()))


def cycle_order(rows, columns):
    order = []
    for row in range(rows):
        line = [row * columns + column for column in range(columns)]
        order += line if row % 2 == 0 else line[::-1]
    return order


def ring_tools():
    order = cycle_order(lax.axis_size("dp"), lax.axis_size("tensor"))
    size = len(order)
    layers = lax.axis_size("section")

    def along(value, by):
        pairs = [(order[i], order[(i + by) % size]) for i in range(size)]
        return lax.ppermute(value, GROUP, pairs)

    def shifted(value, by):
        return lax.ppermute(value, "section", [(i, (i + by) % layers) for i in range(layers)])

    return order, along, shifted


def call(kernel, name, outs, operands, specs, scratch=(), limit=4, flops=0, bytes_accessed=0):
    return pl.pallas_call(
        kernel,
        out_shape=[pltpu.VMEM(shape, dtype) for shape, dtype in outs],
        in_specs=specs,
        out_specs=[VMEM] * len(outs),
        scratch_shapes=list(scratch),
        compiler_params=pltpu.CompilerParams(vmem_limit_bytes=limit * 2**20),
        cost_estimate=pl.CostEstimate(
            flops=flops, bytes_accessed=bytes_accessed, transcendentals=0
        ),
        name=name,
    )(*operands)


def owner_at(distance):
    rows, line = lax.axis_size("dp"), lax.axis_size("tensor")

    def snake(index):
        row, column = index // line, index % line
        return row * line + jnp.where(row % 2 == 0, column, line - 1 - column)

    place = snake(lax.axis_index("dp") * line + lax.axis_index("tensor"))
    return snake((place + distance) % (rows * line))


def columns_of(decoders, distance, which, half):
    start = owner_at(distance) * (2 * half) + which * half
    return decoders[:, pl.ds(pl.multiple_of(start, half), half)]


def upright(row, lanes):
    return jnp.broadcast_to(row, (lanes, row.shape[1])).T


def encode_kernel(ids, cache, weight, bias, low, high, ids_, held, blocks, bias_, across, sems):
    count, block = blocks.shape[:2]
    tokens, half = across.shape[1], low.shape[0]
    copies = [
        pltpu.make_async_copy(ids, ids_.at[0], sems.at[count]),
        pltpu.make_async_copy(cache.at[0], held, sems.at[count + 1]),
        pltpu.make_async_copy(bias, bias_, sems.at[count + 2]),
    ]
    for copy in copies:
        copy.start()
    streams = []
    for i in range(count):
        source = weight.at[0, pl.ds(i * block, block)]
        streams.append(pltpu.make_async_copy(source, blocks.at[i], sems.at[i]))
        streams[i].start()
    copies[0].wait()
    slots = lax.broadcasted_iota(jnp.int32, (held.shape[0], tokens), 0)
    picked = (slots == ids_[...]).astype(F32).astype(BF16)
    copies[1].wait()
    rows = lax.dot_general(picked, held[...], TN, preferred_element_type=F32)
    across[...] = rows.astype(BF16).T
    copies[2].wait()
    for i in range(count):
        streams[i].wait()
        pre = jnp.dot(blocks[i], across[...], preferred_element_type=F32)
        pre = pre + upright(bias_[:, i * block : (i + 1) * block], tokens)
        out = low if (i + 1) * block <= half else high
        start = i * block % half
        out[start : start + block] = jnp.maximum(pre, 0.0).astype(BF16)


def decoded(decoders, pieces):
    total = None
    for distance, which, piece in pieces:
        columns = columns_of(decoders, distance, which, piece.shape[0])
        part = jnp.dot(columns, piece[...], preferred_element_type=F32)
        total = part if total is None else total + part
    return total


def load_decode_kernel(source, low, high, decoders, total, sems):
    layers = sems.shape[0]
    rows = source.shape[0] // layers
    copies = []
    for i in range(layers):
        part = pl.ds(i * rows, rows)
        copies.append(pltpu.make_async_copy(source.at[part], decoders.at[part], sems.at[i]))
        copies[i].start()
    for i in range(layers):
        part = pl.ds(i * rows, rows)
        copies[i].wait()
        total[part] = decoded(decoders.at[part], [(0, 0, low), (0, 1, high)])


def decode_kernel(decoders, before, one, other, total, *, pieces):
    (d0, w0), (d1, w1) = pieces
    total[...] = before[...] + decoded(decoders, [(d0, w0, one), (d1, w1, other)])


def decode_last_kernel(decoders, before, one, other, own, *sent, pieces):
    (d0, w0), (d1, w1) = pieces
    total = before[...] + decoded(decoders, [(d0, w0, one), (d1, w1, other)])
    rows = own.shape[0]
    own[...] = total[:rows]
    for offset, out in enumerate(sent, 1):
        out[...] = total[offset * rows : (offset + 1) * rows].astype(BF16)


def error_kernel(own, incoming, bias, target, returned, *refs, layers):
    came, (error, beyond, *sent) = refs[: layers - 1], refs[layers - 1 :]
    section = lax.axis_index("section")
    shift = upright(bias[...], incoming.shape[1])
    within = own[...] + (incoming[...] + shift) - target[...].astype(F32)
    after = jnp.zeros_like(within)
    for offset in range(1, layers):
        part = came[offset - 1][...].astype(F32)
        inside = section >= offset
        within = within + jnp.where(inside, part, 0.0)
        after = after + jnp.where(inside, 0.0, part)
    mine = within.astype(BF16)
    error[...] = mine
    beyond[...] = after
    passed = returned[...]
    for offset in range(1, layers):
        sent[offset - 1][...] = jnp.where(section >= offset, mine, passed)


def gradient(decoders, back, distance, which, half):
    columns = columns_of(decoders, distance, which, half)
    return jnp.dot(back[...], columns, preferred_element_type=F32)


def gradient_first_kernel(decoders, *refs, layers, pieces):
    parts, (back, *outs) = refs[:layers], refs[layers:]
    back[...] = jnp.concatenate([part[...] for part in parts], 0).T
    for (distance, which), out in zip(pieces, outs):
        out[...] = gradient(decoders, back, distance, which, out.shape[1]).astype(BF16)


def gradient_kernel(decoders, back, *refs, pieces):
    count = len(pieces)
    came, outs = refs[:-count], refs[-count:]
    for i, (distance, which) in enumerate(pieces):
        total = gradient(decoders, back, distance, which, outs[i].shape[1])
        if came:
            total = total + came[i][...].astype(F32)
        outs[i][...] = total.astype(BF16)


def gradient_own_kernel(decoders, back, low, high, total):
    half = low.shape[1]
    for which, came in ((0, low), (1, high)):
        part = gradient(decoders, back, 0, which, half) + came[...].astype(F32)
        total[:, which * half : (which + 1) * half] = part


def gradient_last_kernel(before, low, high, out):
    half = low.shape[1]
    for which, came in ((0, low), (1, high)):
        part = before[:, which * half : (which + 1) * half] + came[...].astype(F32)
        out[which * half : (which + 1) * half, :] = part.T


def tiled_local(cache, token_ids, enc_weight, enc_bias, dec_weight, dec_bias, incoming, target, returned):
    order, along, shifted = ring_tools()
    size = len(order)
    far = size // 2
    layers = lax.axis_size("section")
    tokens = token_ids.shape[0]
    slots, width = cache.shape[1:]
    mine = enc_weight.shape[1]
    half = mine // 2
    columns = dec_weight.shape[2]
    outs_all = layers * columns
    in_hbm = functools.partial(pltpu.with_memory_space_constraint, memory_space=pltpu.HBM)
    decoders = dec_weight.reshape(outs_all, dec_weight.shape[3])

    block = min(256, half)
    count = mine // block
    low, high = call(
        encode_kernel,
        "encode",
        [((half, tokens), BF16)] * 2,
        [in_hbm(value) for value in (token_ids, cache, enc_weight, enc_bias)],
        [HBM] * 4,
        [
            pltpu.VMEM((1, tokens), jnp.int32),
            pltpu.VMEM((slots, width), BF16),
            pltpu.VMEM((count, block, width), BF16),
            pltpu.VMEM((1, mine), F32),
            pltpu.VMEM((width, tokens), BF16),
            pltpu.SemaphoreType.DMA((count + 3,)),
        ],
        limit=20,
        flops=2 * tokens * width * (mine + slots),
        bytes_accessed=2 * width * (mine + slots),
    )
    piece_flops = 2 * tokens * half * outs_all
    outer = [along(low, 1), along(high, -1)]
    inner = [along(high, 1), along(low, -1)]
    decoders, total = call(
        load_decode_kernel,
        "load_decode",
        [(decoders.shape, BF16), ((outs_all, tokens), F32)],
        (in_hbm(decoders), low, high),
        [HBM] + [VMEM] * 2,
        [pltpu.SemaphoreType.DMA((layers,))],
        flops=2 * piece_flops,
        bytes_accessed=4 * decoders.size,
    )
    for step in range(1, far):
        rise, fall, total = lax.optimization_barrier((*outer, total))
        near = rise, fall
        outer = [along(rise, 1), along(fall, -1)]
        rise, fall, *near = lax.optimization_barrier((*inner, *near))
        if step < far - 1:
            inner = [along(rise, 1), along(fall, -1)]
        for (one, other), which in ((near, 0), ((rise, fall), 1)):
            (total,) = call(
                functools.partial(
                    decode_kernel, pieces=((size - step, which), (step, 1 - which))
                ),
                f"decode_{step}_{which}",
                [((outs_all, tokens), F32)],
                (decoders, total, one, other),
                [VMEM] * 4,
                flops=2 * piece_flops,
            )
    own, *sent = call(
        functools.partial(decode_last_kernel, pieces=((far, 0), (far, 1))),
        "decode_last",
        [((columns, tokens), F32)] + [((columns, tokens), BF16)] * (layers - 1),
        (decoders, total, *outer),
        [VMEM] * 4,
        flops=2 * piece_flops,
    )
    came = [shifted(value, offset) for offset, value in enumerate(sent, 1)]
    error, beyond, *sent = call(
        functools.partial(error_kernel, layers=layers),
        "error",
        [((columns, tokens), BF16), ((columns, tokens), F32)]
        + [((columns, tokens), BF16)] * (layers - 1),
        (own, incoming[0].T, dec_bias, target[0].T, returned[0].T, *came),
        [VMEM] * (layers + 4),
    )
    came = [shifted(value, -offset) for offset, value in enumerate(sent, 1)]
    piece = ((tokens, half), BF16)
    back, *outer = call(
        functools.partial(gradient_first_kernel, layers=layers, pieces=((far, 0), (far, 1))),
        "gradient_far",
        [((tokens, outs_all), BF16), piece, piece],
        (decoders, error, *came),
        [VMEM] * (layers + 1),
        flops=2 * piece_flops,
    )
    inner = []
    for step in range(far - 1, -1, -1):
        outer = [along(outer[0], 1), along(outer[1], -1)]
        if step == 0:
            break
        inner = call(
            functools.partial(gradient_kernel, pieces=((size - step, 0), (step, 1))),
            f"gradient_inner_{step}",
            [piece, piece],
            (decoders, back, *inner),
            [VMEM] * (2 + len(inner)),
            flops=2 * piece_flops,
        )
        inner = [along(inner[0], -1), along(inner[1], 1)]
        outer = call(
            functools.partial(gradient_kernel, pieces=((step, 0), (size - step, 1))),
            f"gradient_outer_{step}",
            [piece, piece],
            (decoders, back, *outer),
            [VMEM] * (2 + len(outer)),
            flops=2 * piece_flops,
        )
    (part,) = call(
        gradient_own_kernel,
        "gradient_own",
        [((tokens, mine), F32)],
        (decoders, back, *inner),
        [VMEM] * 4,
        flops=2 * piece_flops,
    )
    lat_grad = pl.pallas_call(
        gradient_last_kernel,
        out_shape=jax.ShapeDtypeStruct((mine, tokens), F32),
        in_specs=[VMEM] * 3,
        out_specs=VMEM,
        compiler_params=pltpu.CompilerParams(vmem_limit_bytes=4 * 2**20),
        name="gradient_last",
    )(part, *outer)
    return (error.T[None], beyond.T[None], lat_grad[None])


def plain_local(cache, token_ids, enc_weight, enc_bias, dec_weight, dec_bias, incoming, target, returned):
    order, along, shifted = ring_tools()
    size = len(order)
    layers = lax.axis_size("section")
    section = lax.axis_index("section")
    place = jnp.asarray([order.index(i) for i in range(size)], jnp.int32)[lax.axis_index(GROUP)]
    mine = enc_weight.shape[1]
    columns = dec_weight.shape[2]
    tokens = token_ids.shape[0]
    halves = [slice(0, mine // 2), slice(mine // 2, mine)]
    decoders = dec_weight[0].reshape(layers * columns, dec_weight.shape[3])

    def member(distance):
        return jnp.asarray(order, jnp.int32)[(place + distance) % size]

    def part(owner, which):
        start, length = halves[which].start, halves[which].stop - halves[which].start
        return lax.dynamic_slice_in_dim(decoders, owner * mine + start, length, 1)

    def decode(latents, owner, which):
        return lax.dot_general(part(owner, which), latents, NT, preferred_element_type=F32)

    rows = cache[0].at[token_ids].get(mode="promise_in_bounds")
    pre = lax.dot_general(rows, enc_weight[0], NT, preferred_element_type=F32)
    latents = jnp.maximum(pre + enc_bias[0], 0.0).astype(BF16)
    up = [latents[:, cut] for cut in halves]
    down = list(up)
    total = decode(up[0], member(0), 0) + decode(up[1], member(0), 1)
    for step in range(1, (size - 1) // 2 + 1):
        for which in (0, 1):
            up[which] = along(up[which], 1)
            down[which] = along(down[which], -1)
            total = total + decode(up[which], member(-step), which)
            total = total + decode(down[which], member(step), which)
    if size % 2 == 0:
        total = total + decode(along(up[0], 1), member(size // 2), 0)
        total = total + decode(along(down[1], -1), member(size // 2), 1)

    by_offset = total.reshape(layers, columns, tokens)
    within = by_offset[0]
    beyond = jnp.zeros_like(within)
    for offset in range(1, layers):
        came = shifted(by_offset[offset].astype(BF16), offset).astype(F32)
        within = within + jnp.where(section >= offset, came, 0.0)
        beyond = beyond + jnp.where(section < offset, came, 0.0)
    recon = within + incoming[0].T + dec_bias[0][:, None]
    error = (recon - target[0].T.astype(F32)).astype(BF16)
    passed = returned[0].T
    upstream = [error]
    for offset in range(1, layers):
        upstream.append(shifted(jnp.where(section >= offset, error, passed), -offset))
    back = jnp.concatenate(upstream, 0)

    def gradient_of(owner, which):
        return lax.dot_general(part(owner, which), back, TN, preferred_element_type=F32)

    up, down = [None, None], [None, None]
    if size % 2 == 0:
        up[0] = along(gradient_of(member(size // 2), 0).astype(BF16), 1)
        down[1] = along(gradient_of(member(size // 2), 1).astype(BF16), -1)
    for step in range((size - 1) // 2, 0, -1):
        for which in (0, 1):
            rise = gradient_of(member(step), which)
            fall = gradient_of(member(-step), which)
            if up[which] is not None:
                rise = rise + up[which].astype(F32)
            if down[which] is not None:
                fall = fall + down[which].astype(F32)
            up[which] = along(rise.astype(BF16), 1)
            down[which] = along(fall.astype(BF16), -1)
    parts = []
    for which in (0, 1):
        own_part = gradient_of(member(0), which)
        for came in (up[which], down[which]):
            if came is not None:
                own_part = own_part + came.astype(F32)
        parts.append(own_part)
    lat_grad = jnp.concatenate(parts, 0)
    return (error.T[None], beyond.T[None], lat_grad[None])


def local(cache, token_ids, enc_weight, enc_bias, dec_weight, *rest):
    size = lax.axis_size("dp") * lax.axis_size("tensor")
    mine, width = enc_weight.shape[1:]
    whole_tiles = (
        size % 2 == 0
        and size >= 4
        and mine % 256 == 0
        and width % 128 == 0
        and dec_weight.shape[2] % 16 == 0
        and token_ids.shape[0] % 128 == 0
        and cache.shape[1] % 16 == 0
    )
    form = tiled_local if whole_tiles else plain_local
    return form(cache, token_ids, enc_weight, enc_bias, dec_weight, *rest)


def solution(mesh):
    placed = (
        P("section", None, None),
        P(),
        P("section", GROUP, None),
        P("section", GROUP),
        P("section", None, GROUP, None),
        P("section", GROUP),
        P("section", None, GROUP),
        P("section", None, GROUP),
        P("section", None, GROUP),
    )
    return jax.shard_map(
        local,
        mesh=mesh,
        in_specs=placed,
        out_specs=(
            P("section", None, GROUP),
            P("section", None, GROUP),
            P("section", GROUP, None),
        ),
        check_vma=False,
    )
```

time: 103 us -> 83.9 us (0.81)
  local copies, waits for them, and re-layouts: 15.1 us -> 1.33 us
  Pallas kernels: 33.3 us -> 26.5 us
  waiting for transfers between devices: 18.1 us -> 19.7 us
    unnamed x18 -> x10, local copies, waits for them, and re-layouts: 15 us -> 1.33 us
    pallas_call x19 -> x18, Pallas kernels: 32.3 us -> 25.5 us  [call(): pl.pallas_call(kernel, out_shape=[pltpu.VMEM(shape, dtype) for shape, dty...]
    ppermute x28, waiting for transfers between devices: 10.6 us -> 12.1 us  [along(): return lax.ppermute(value, GROUP, pairs)]
  transfers between devices with their start and end apart: 34 -> 34, of which waited for: 14 -> 19; matrix products, arithmetic and copies ran while one was open for 1% -> 2% of each run, Pallas kernels for 22% -> 21%
where the time goes in v3:
time: 83.9 us; the launch traced here: 83.7 us
  starting transfers between devices  35.4 us (42%)
  Pallas kernels  26.5 us (32%)
  waiting for transfers between devices  19.7 us (23%)
  local copies, waits for them, and re-layouts  1.33 us (2%)
  between operations  0.84 us (1%)
    ppermute x28, starting transfers between devices, along(): return lax.ppermute(value, GROUP, pairs)  29.9 us
    pallas_call x18, Pallas kernels, call(): pl.pallas_call(kernel, out_shape=[pltpu.VMEM(shape, dtype) for shape, dty...  25.5 us
    ppermute x28, waiting for transfers between devices, along(): return lax.ppermute(value, GROUP, pairs)  12.1 us
    ppermute x6, waiting for transfers between devices, shifted(): lax.ppermute(value, 'section', [(i, (i + by) % layers) for i in range(lay...  7.56 us
    ppermute x6, starting transfers between devices, shifted(): lax.ppermute(value, 'section', [(i, (i + by) % layers) for i in range(lay...  5.5 us
  transfers between devices with their start and end apart: 34, of which 19 were waited for; matrix products, arithmetic and copies ran while one was open for 2% of the time, Pallas kernels for 21%

profile of v3, /device:TPU:0, one launch (start us, length us, event | category | flops | bytes accessed | tf_op | source)
XLA Modules:
  0.0 83.7 jit_solution(5177189595510395110)
XLA Ops:
  0.6 6.3 %encode.1 = (bf16[512,128]{1,0:T(8,128)(2,1)S(1)}, bf16[512,128]{1,0:T(8,128)(2,1)S(1)}) custom-call(s32[128]{0:T(128)} %ids.1, bf16[1,256,5376]{2,1,0:T(8,128)(2,1)} %cache.1, bf16[1,1024,5376]{2,1,0:T(8,128)(2,1)} %weight.1, f32[1,1024]{1,0:T(1,128)} %bias.2), custom_call_target="tpu_custom_call" | custom-call | flops 1761607680 | bytes 13762560 | tf_op jit(solution)/shard_map/encode/pallas_call | solution.py:43
  7.0 3.1 %collective-permute-start = (bf16[512,128]{1,0:T(8,128)(2,1)S(1)}, bf16[512,128]{1,0:T(8,128)(2,1)S(1)}, u32[]{:S(2)}, u32[]{:S(2)}) collective-permute-start(bf16[512,128]{1,0:T(8,128)(2,1)S(1)} %get-tuple-element.52.low), channel_id=1, source_target_pairs={{0,1},{1,2},{2,3},{3,7},{7,6},{6,5},{5,4},{4,0},{8,9},{9,10},{10,1... | collective-permute-start | bytes 393224 | tf_op jit(solution)/shard_map/ppermute | solution.py:34
  10.0 1.9 %collective-permute-start.5 = (bf16[512,128]{1,0:T(8,128)(2,1)S(1)}, bf16[512,128]{1,0:T(8,128)(2,1)S(1)}, u32[]{:S(2)}, u32[]{:S(2)}) collective-permute-start(bf16[512,128]{1,0:T(8,128)(2,1)S(1)} %get-tuple-element.52.low), channel_id=1, source_target_pairs={{0,4},{1,0},{2,1},{3,2},{7,3},{6,7},{5,6},{4,5},{8,12},{9,8},{10,9... | collective-permute-start | bytes 393224 | tf_op jit(solution)/shard_map/ppermute | solution.py:34
  12.1 7.9 %load_decode.1 = (bf16[1344,8192]{1,0:T(8,128)(2,1)S(1)}, f32[1344,128]{1,0:T(8,128)S(1)}) custom-call(bf16[1344,8192]{1,0:T(8,128)(2,1)} %bitcast.22, bf16[512,128]{1,0:T(8,128)(2,1)S(1)} %get-tuple-element.52.low, bf16[512,128]{1,0:T(8,128)(2,1)S(1)} %get-tuple-element.53.high), custom_call_target="tpu_custom_call" | custom-call | flops 352321536 | bytes 44040192 | tf_op jit(solution)/shard_map/load_decode/pallas_call | solution.py:43
  20.0 2.0 %collective-permute-start.2 = (bf16[512,128]{1,0:T(8,128)(2,1)S(1)}, bf16[512,128]{1,0:T(8,128)(2,1)S(1)}, u32[]{:S(2)}, u32[]{:S(2)}) collective-permute-start(bf16[512,128]{1,0:T(8,128)(2,1)S(1)} %collective-permute-done.one), channel_id=1, source_target_pairs={{0,1},{1,2},{2,3},{3,7},{7,6},{6,5},{5,4},{4,0},{8,9},{9,10},{10,1... | collective-permute-start | bytes 393224 | tf_op jit(solution)/shard_map/ppermute | solution.py:34
  22.1 2.0 %collective-permute-start.8 = (bf16[512,128]{1,0:T(8,128)(2,1)S(1)}, bf16[512,128]{1,0:T(8,128)(2,1)S(1)}, u32[]{:S(2)}, u32[]{:S(2)}) collective-permute-start(bf16[512,128]{1,0:T(8,128)(2,1)S(1)} %collective-permute-done.4.one), channel_id=1, source_target_pairs={{0,1},{1,2},{2,3},{3,7},{7,6},{6,5},{5,4},{4,0},{8,9},{9,10},{10,1... | collective-permute-start | bytes 393224 | tf_op jit(solution)/shard_map/ppermute | solution.py:34
  25.9 1.4 %collective-permute-done.3.other = bf16[512,128]{1,0:T(8,128)(2,1)S(1)} collective-permute-done((bf16[512,128]{1,0:T(8,128)(2,1)S(1)}, bf16[512,128]{1,0:T(8,128)(2,1)S(1)}, u32[]{:S(2)}, u32[]{:S(2)}) %collective-permute-start.3) | collective-permute-done | bytes 131104 | tf_op jit(solution)/shard_map/ppermute | solution.py:34
  27.3 1.6 %collective-permute-start.6 = (bf16[512,128]{1,0:T(8,128)(2,1)S(1)}, bf16[512,128]{1,0:T(8,128)(2,1)S(1)}, u32[]{:S(2)}, u32[]{:S(2)}) collective-permute-start(bf16[512,128]{1,0:T(8,128)(2,1)S(1)} %collective-permute-done.2.one), channel_id=1, source_target_pairs={{0,1},{1,2},{2,3},{3,7},{7,6},{6,5},{5,4},{4,0},{8,9},{9,10},{10,1... | collective-permute-start | bytes 393224 | tf_op jit(solution)/shard_map/ppermute | solution.py:34
  29.6 1.6 %collective-permute-start.10 = (bf16[512,128]{1,0:T(8,128)(2,1)S(1)}, bf16[512,128]{1,0:T(8,128)(2,1)S(1)}, u32[]{:S(2)}, u32[]{:S(2)}) collective-permute-start(bf16[512,128]{1,0:T(8,128)(2,1)S(1)} %collective-permute-done.8.one), channel_id=1, source_target_pairs={{0,1},{1,2},{2,3},{3,7},{7,6},{6,5},{5,4},{4,0},{8,9},{9,10},{10,1... | collective-permute-start | bytes 393224 | tf_op jit(solution)/shard_map/ppermute | solution.py:34
  33.9 1.6 %collective-permute-start.12 = (bf16[512,128]{1,0:T(8,128)(2,1)S(1)}, bf16[512,128]{1,0:T(8,128)(2,1)S(1)}, u32[]{:S(2)}, u32[]{:S(2)}) collective-permute-start(bf16[512,128]{1,0:T(8,128)(2,1)S(1)} %collective-permute-done.6.one), channel_id=1, source_target_pairs={{0,1},{1,2},{2,3},{3,7},{7,6},{6,5},{5,4},{4,0},{8,9},{9,10},{10,1... | collective-permute-start | bytes 393224 | tf_op jit(solution)/shard_map/ppermute | solution.py:34
  38.9 1.6 %collective-permute-done.13.other = bf16[512,128]{1,0:T(8,128)(2,1)S(1)} collective-permute-done((bf16[512,128]{1,0:T(8,128)(2,1)S(1)}, bf16[512,128]{1,0:T(8,128)(2,1)S(1)}, u32[]{:S(2)}, u32[]{:S(2)}) %collective-permute-start.13) | collective-permute-done | bytes 131104 | tf_op jit(solution)/shard_map/ppermute | solution.py:34
  41.4 1.6 %collective-permute-start.15 = (bf16[336,128]{1,0:T(8,128)(2,1)S(1)}, bf16[336,128]{1,0:T(8,128)(2,1)S(1)}, u32[]{:S(2)}, u32[]{:S(2)}) collective-permute-start(bf16[336,128]{1,0:T(8,128)(2,1)S(1)} %get-tuple-element.79), channel_id=1, source_target_pairs={{0,16},{8,24},{16,0},{24,8},{1,17},{9,25},{17,1},{25,9},{2,18},{10... | collective-permute-start | bytes 258056 | tf_op jit(solution)/shard_map/ppermute | solution.py:37
  43.0 1.4 %collective-permute-start.16 = (bf16[336,128]{1,0:T(8,128)(2,1)S(1)}, bf16[336,128]{1,0:T(8,128)(2,1)S(1)}, u32[]{:S(2)}, u32[]{:S(2)}) collective-permute-start(bf16[336,128]{1,0:T(8,128)(2,1)S(1)} %get-tuple-element.80), channel_id=1, source_target_pairs={{0,24},{8,0},{16,8},{24,16},{1,25},{9,1},{17,9},{25,17},{2,26},{10... | collective-permute-start | bytes 258056 | tf_op jit(solution)/shard_map/ppermute | solution.py:37
  47.3 2.0 %collective-permute-start.17 = (bf16[336,128]{1,0:T(8,128)(2,1)S(1)}, bf16[336,128]{1,0:T(8,128)(2,1)S(1)}, u32[]{:S(2)}, u32[]{:S(2)}) collective-permute-start(bf16[336,128]{1,0:T(8,128)(2,1)S(1)} %get-tuple-element.83), channel_id=1, source_target_pairs={{0,24},{8,0},{16,8},{24,16},{1,25},{9,1},{17,9},{25,17},{2,26},{10... | collective-permute-start | bytes 258056 | tf_op jit(solution)/shard_map/ppermute | solution.py:37
  49.8 1.9 %collective-permute-done.17.refs_1_ = bf16[336,128]{1,0:T(8,128)(2,1)S(1)} collective-permute-done((bf16[336,128]{1,0:T(8,128)(2,1)S(1)}, bf16[336,128]{1,0:T(8,128)(2,1)S(1)}, u32[]{:S(2)}, u32[]{:S(2)}) %collective-permute-start.17) | collective-permute-done | bytes 86048 | tf_op jit(solution)/shard_map/ppermute | solution.py:37
  51.7 2.9 %collective-permute-done.18.refs_2_ = bf16[336,128]{1,0:T(8,128)(2,1)S(1)} collective-permute-done((bf16[336,128]{1,0:T(8,128)(2,1)S(1)}, bf16[336,128]{1,0:T(8,128)(2,1)S(1)}, u32[]{:S(2)}, u32[]{:S(2)}) %collective-permute-start.18) | collective-permute-done | bytes 86048 | tf_op jit(solution)/shard_map/ppermute | solution.py:37
  55.2 1.5 %collective-permute-start.26 = (bf16[128,512]{1,0:T(8,128)(2,1)S(1)}, bf16[128,512]{1,0:T(8,128)(2,1)S(1)}, u32[]{:S(2)}, u32[]{:S(2)}) collective-permute-start(bf16[128,512]{1,0:T(8,128)(2,1)S(1)} %get-tuple-element.93), channel_id=1, source_target_pairs={{0,1},{1,2},{2,3},{3,7},{7,6},{6,5},{5,4},{4,0},{8,9},{9,10},{10,1... | collective-permute-start | bytes 393224 | tf_op jit(solution)/shard_map/ppermute | solution.py:34
  58.4 1.6 %collective-permute-start.21 = (bf16[128,512]{1,0:T(8,128)(2,1)S(1)}, bf16[128,512]{1,0:T(8,128)(2,1)S(1)}, u32[]{:S(2)}, u32[]{:S(2)}) collective-permute-start(bf16[128,512]{1,0:T(8,128)(2,1)S(1)} %get-tuple-element.88), channel_id=1, source_target_pairs={{0,1},{1,2},{2,3},{3,7},{7,6},{6,5},{5,4},{4,0},{8,9},{9,10},{10,1... | collective-permute-start | bytes 393224 | tf_op jit(solution)/shard_map/ppermute | solution.py:34
  60.0 1.4 %collective-permute-done.26.refs_0_ = bf16[128,512]{1,0:T(8,128)(2,1)S(1)} collective-permute-done((bf16[128,512]{1,0:T(8,128)(2,1)S(1)}, bf16[128,512]{1,0:T(8,128)(2,1)S(1)}, u32[]{:S(2)}, u32[]{:S(2)}) %collective-permute-start.26) | collective-permute-done | bytes 131104 | tf_op jit(solution)/shard_map/ppermute | solution.py:34
  63.0 1.8 %collective-permute-start.28 = (bf16[128,512]{1,0:T(8,128)(2,1)S(1)}, bf16[128,512]{1,0:T(8,128)(2,1)S(1)}, u32[]{:S(2)}, u32[]{:S(2)}) collective-permute-start(bf16[128,512]{1,0:T(8,128)(2,1)S(1)} %get-tuple-element.95), channel_id=1, source_target_pairs={{0,1},{1,2},{2,3},{3,7},{7,6},{6,5},{5,4},{4,0},{8,9},{9,10},{10,1... | collective-permute-start | bytes 393224 | tf_op jit(solution)/shard_map/ppermute | solution.py:34
  66.3 1.5 %collective-permute-start.23 = (bf16[128,512]{1,0:T(8,128)(2,1)S(1)}, bf16[128,512]{1,0:T(8,128)(2,1)S(1)}, u32[]{:S(2)}, u32[]{:S(2)}) collective-permute-start(bf16[128,512]{1,0:T(8,128)(2,1)S(1)} %get-tuple-element.90), channel_id=1, source_target_pairs={{0,1},{1,2},{2,3},{3,7},{7,6},{6,5},{5,4},{4,0},{8,9},{9,10},{10,1... | collective-permute-start | bytes 393224 | tf_op jit(solution)/shard_map/ppermute | solution.py:34
  68.1 1.6 %collective-permute-done.29.refs_1_ = bf16[128,512]{1,0:T(8,128)(2,1)S(1)} collective-permute-done((bf16[128,512]{1,0:T(8,128)(2,1)S(1)}, bf16[128,512]{1,0:T(8,128)(2,1)S(1)}, u32[]{:S(2)}, u32[]{:S(2)}) %collective-permute-start.29) | collective-permute-done | bytes 131104 | tf_op jit(solution)/shard_map/ppermute | solution.py:34
  73.4 1.8 %collective-permute-start.25 = (bf16[128,512]{1,0:T(8,128)(2,1)S(1)}, bf16[128,512]{1,0:T(8,128)(2,1)S(1)}, u32[]{:S(2)}, u32[]{:S(2)}) collective-permute-start(bf16[128,512]{1,0:T(8,128)(2,1)S(1)} %get-tuple-element.92), channel_id=1, source_target_pairs={{0,1},{1,2},{2,3},{3,7},{7,6},{6,5},{5,4},{4,0},{8,9},{9,10},{10,1... | collective-permute-start | bytes 393224 | tf_op jit(solution)/shard_map/ppermute | solution.py:34
  77.8 1.3 %collective-permute-start.33 = (bf16[128,512]{1,0:T(8,128)(2,1)S(1)}, bf16[128,512]{1,0:T(8,128)(2,1)S(1)}, u32[]{:S(2)}, u32[]{:S(2)}) collective-permute-start(bf16[128,512]{1,0:T(8,128)(2,1)S(1)} %get-tuple-element.100), channel_id=1, source_target_pairs={{0,4},{1,0},{2,1},{3,2},{7,3},{6,7},{5,6},{4,5},{8,12},{9,8},{10,9... | collective-permute-start | bytes 393224 | tf_op jit(solution)/shard_map/ppermute | solution.py:34
  (73 shorter events, 29.6 us)
Async XLA Ops:
  7.0 13.0 %collective-permute-start = (bf16[512,128]{1,0:T(8,128)(2,1)S(1)}, bf16[512,128]{1,0:T(8,128)(2,1)S(1)}, u32[]{:S(2)}, u32[]{:S(2)}) collective-permute-start(bf16[512,128]{1,0:T(8,128)(2,1)S(1)} %get-tuple-element.52.low), channel_id=1, source_target_pairs={{0,1},{1,2},{2,3},{3,7},{7,6},{6,5},{5,4},{4,0},{8,9},{9,10},{10,1... | collective-permute-start | bytes 393224 | tf_op jit(solution)/shard_map/ppermute | solution.py:34
  10.0 9.9 %collective-permute-start.1 = (bf16[512,128]{1,0:T(8,128)(2,1)S(1)}, bf16[512,128]{1,0:T(8,128)(2,1)S(1)}, u32[]{:S(2)}, u32[]{:S(2)}) collective-permute-start(bf16[512,128]{1,0:T(8,128)(2,1)S(1)} %get-tuple-element.53.high), channel_id=1, source_target_pairs={{0,4},{1,0},{2,1},{3,2},{7,3},{6,7},{5,6},{4,5},{8,12},{9,8},{10,9... | collective-permute-start | bytes 393224 | tf_op jit(solution)/shard_map/ppermute | solution.py:34
  10.0 12.0 %collective-permute-start.5 = (bf16[512,128]{1,0:T(8,128)(2,1)S(1)}, bf16[512,128]{1,0:T(8,128)(2,1)S(1)}, u32[]{:S(2)}, u32[]{:S(2)}) collective-permute-start(bf16[512,128]{1,0:T(8,128)(2,1)S(1)} %get-tuple-element.52.low), channel_id=1, source_target_pairs={{0,4},{1,0},{2,1},{3,2},{7,3},{6,7},{5,6},{4,5},{8,12},{9,8},{10,9... | collective-permute-start | bytes 393224 | tf_op jit(solution)/shard_map/ppermute | solution.py:34
  12.0 10.1 %collective-permute-start.4 = (bf16[512,128]{1,0:T(8,128)(2,1)S(1)}, bf16[512,128]{1,0:T(8,128)(2,1)S(1)}, u32[]{:S(2)}, u32[]{:S(2)}) collective-permute-start(bf16[512,128]{1,0:T(8,128)(2,1)S(1)} %get-tuple-element.53.high), channel_id=1, source_target_pairs={{0,1},{1,2},{2,3},{3,7},{7,6},{6,5},{5,4},{4,0},{8,9},{9,10},{10,1... | collective-permute-start | bytes 393224 | tf_op jit(solution)/shard_map/ppermute | solution.py:34
  20.0 5.9 %collective-permute-start.2 = (bf16[512,128]{1,0:T(8,128)(2,1)S(1)}, bf16[512,128]{1,0:T(8,128)(2,1)S(1)}, u32[]{:S(2)}, u32[]{:S(2)}) collective-permute-start(bf16[512,128]{1,0:T(8,128)(2,1)S(1)} %collective-permute-done.one), channel_id=1, source_target_pairs={{0,1},{1,2},{2,3},{3,7},{7,6},{6,5},{5,4},{4,0},{8,9},{9,10},{10,1... | collective-permute-start | bytes 393224 | tf_op jit(solution)/shard_map/ppermute | solution.py:34
  22.0 5.3 %collective-permute-start.3 = (bf16[512,128]{1,0:T(8,128)(2,1)S(1)}, bf16[512,128]{1,0:T(8,128)(2,1)S(1)}, u32[]{:S(2)}, u32[]{:S(2)}) collective-permute-start(bf16[512,128]{1,0:T(8,128)(2,1)S(1)} %collective-permute-done.1.other), channel_id=1, source_target_pairs={{0,4},{1,0},{2,1},{3,2},{7,3},{6,7},{5,6},{4,5},{8,12},{9,8},{10,9... | collective-permute-start | bytes 393224 | tf_op jit(solution)/shard_map/ppermute | solution.py:34
  22.1 7.3 %collective-permute-start.8 = (bf16[512,128]{1,0:T(8,128)(2,1)S(1)}, bf16[512,128]{1,0:T(8,128)(2,1)S(1)}, u32[]{:S(2)}, u32[]{:S(2)}) collective-permute-start(bf16[512,128]{1,0:T(8,128)(2,1)S(1)} %collective-permute-done.4.one), channel_id=1, source_target_pairs={{0,1},{1,2},{2,3},{3,7},{7,6},{6,5},{5,4},{4,0},{8,9},{9,10},{10,1... | collective-permute-start | bytes 393224 | tf_op jit(solution)/shard_map/ppermute | solution.py:34
  24.1 5.6 %collective-permute-start.9 = (bf16[512,128]{1,0:T(8,128)(2,1)S(1)}, bf16[512,128]{1,0:T(8,128)(2,1)S(1)}, u32[]{:S(2)}, u32[]{:S(2)}) collective-permute-start(bf16[512,128]{1,0:T(8,128)(2,1)S(1)} %collective-permute-done.5.other), channel_id=1, source_target_pairs={{0,4},{1,0},{2,1},{3,2},{7,3},{6,7},{5,6},{4,5},{8,12},{9,8},{10,9... | collective-permute-start | bytes 393224 | tf_op jit(solution)/shard_map/ppermute | solution.py:34
  27.3 6.1 %collective-permute-start.6 = (bf16[512,128]{1,0:T(8,128)(2,1)S(1)}, bf16[512,128]{1,0:T(8,128)(2,1)S(1)}, u32[]{:S(2)}, u32[]{:S(2)}) collective-permute-start(bf16[512,128]{1,0:T(8,128)(2,1)S(1)} %collective-permute-done.2.one), channel_id=1, source_target_pairs={{0,1},{1,2},{2,3},{3,7},{7,6},{6,5},{5,4},{4,0},{8,9},{9,10},{10,1... | collective-permute-start | bytes 393224 | tf_op jit(solution)/shard_map/ppermute | solution.py:34
  29.6 6.3 %collective-permute-start.10 = (bf16[512,128]{1,0:T(8,128)(2,1)S(1)}, bf16[512,128]{1,0:T(8,128)(2,1)S(1)}, u32[]{:S(2)}, u32[]{:S(2)}) collective-permute-start(bf16[512,128]{1,0:T(8,128)(2,1)S(1)} %collective-permute-done.8.one), channel_id=1, source_target_pairs={{0,1},{1,2},{2,3},{3,7},{7,6},{6,5},{5,4},{4,0},{8,9},{9,10},{10,1... | collective-permute-start | bytes 393224 | tf_op jit(solution)/shard_map/ppermute | solution.py:34
  31.2 5.7 %collective-permute-start.11 = (bf16[512,128]{1,0:T(8,128)(2,1)S(1)}, bf16[512,128]{1,0:T(8,128)(2,1)S(1)}, u32[]{:S(2)}, u32[]{:S(2)}) collective-permute-start(bf16[512,128]{1,0:T(8,128)(2,1)S(1)} %collective-permute-done.9.other), channel_id=1, source_target_pairs={{0,4},{1,0},{2,1},{3,2},{7,3},{6,7},{5,6},{4,5},{8,12},{9,8},{10,9... | collective-permute-start | bytes 393224 | tf_op jit(solution)/shard_map/ppermute | solution.py:34
  41.4 5.4 %collective-permute-start.15 = (bf16[336,128]{1,0:T(8,128)(2,1)S(1)}, bf16[336,128]{1,0:T(8,128)(2,1)S(1)}, u32[]{:S(2)}, u32[]{:S(2)}) collective-permute-start(bf16[336,128]{1,0:T(8,128)(2,1)S(1)} %get-tuple-element.79), channel_id=1, source_target_pairs={{0,16},{8,24},{16,0},{24,8},{1,17},{9,25},{17,1},{25,9},{2,18},{10... | collective-permute-start | bytes 258056 | tf_op jit(solution)/shard_map/ppermute | solution.py:37
  49.2 5.3 %collective-permute-start.18 = (bf16[336,128]{1,0:T(8,128)(2,1)S(1)}, bf16[336,128]{1,0:T(8,128)(2,1)S(1)}, u32[]{:S(2)}, u32[]{:S(2)}) collective-permute-start(bf16[336,128]{1,0:T(8,128)(2,1)S(1)} %get-tuple-element.84), channel_id=1, source_target_pairs={{0,16},{8,24},{16,0},{24,8},{1,17},{9,25},{17,1},{25,9},{2,18},{10... | collective-permute-start | bytes 258056 | tf_op jit(solution)/shard_map/ppermute | solution.py:37
  55.2 6.2 %collective-permute-start.26 = (bf16[128,512]{1,0:T(8,128)(2,1)S(1)}, bf16[128,512]{1,0:T(8,128)(2,1)S(1)}, u32[]{:S(2)}, u32[]{:S(2)}) collective-permute-start(bf16[128,512]{1,0:T(8,128)(2,1)S(1)} %get-tuple-element.93), channel_id=1, source_target_pairs={{0,1},{1,2},{2,3},{3,7},{7,6},{6,5},{5,4},{4,0},{8,9},{9,10},{10,1... | collective-permute-start | bytes 393224 | tf_op jit(solution)/shard_map/ppermute | solution.py:34
  56.8 5.6 %collective-permute-start.27 = (bf16[128,512]{1,0:T(8,128)(2,1)S(1)}, bf16[128,512]{1,0:T(8,128)(2,1)S(1)}, u32[]{:S(2)}, u32[]{:S(2)}) collective-permute-start(bf16[128,512]{1,0:T(8,128)(2,1)S(1)} %get-tuple-element.94), channel_id=1, source_target_pairs={{0,4},{1,0},{2,1},{3,2},{7,3},{6,7},{5,6},{4,5},{8,12},{9,8},{10,9... | collective-permute-start | bytes 393224 | tf_op jit(solution)/shard_map/ppermute | solution.py:34
  57.9 7.2 %collective-permute-start.20 = (bf16[128,512]{1,0:T(8,128)(2,1)S(1)}, bf16[128,512]{1,0:T(8,128)(2,1)S(1)}, u32[]{:S(2)}, u32[]{:S(2)}) collective-permute-start(bf16[128,512]{1,0:T(8,128)(2,1)S(1)} %get-tuple-element.87), channel_id=1, source_target_pairs={{0,4},{1,0},{2,1},{3,2},{7,3},{6,7},{5,6},{4,5},{8,12},{9,8},{10,9... | collective-permute-start | bytes 393224 | tf_op jit(solution)/shard_map/ppermute | solution.py:34
  58.4 6.7 %collective-permute-start.21 = (bf16[128,512]{1,0:T(8,128)(2,1)S(1)}, bf16[128,512]{1,0:T(8,128)(2,1)S(1)}, u32[]{:S(2)}, u32[]{:S(2)}) collective-permute-start(bf16[128,512]{1,0:T(8,128)(2,1)S(1)} %get-tuple-element.88), channel_id=1, source_target_pairs={{0,1},{1,2},{2,3},{3,7},{7,6},{6,5},{5,4},{4,0},{8,9},{9,10},{10,1... | collective-permute-start | bytes 393224 | tf_op jit(solution)/shard_map/ppermute | solution.py:34
  63.0 5.1 %collective-permute-start.28 = (bf16[128,512]{1,0:T(8,128)(2,1)S(1)}, bf16[128,512]{1,0:T(8,128)(2,1)S(1)}, u32[]{:S(2)}, u32[]{:S(2)}) collective-permute-start(bf16[128,512]{1,0:T(8,128)(2,1)S(1)} %get-tuple-element.95), channel_id=1, source_target_pairs={{0,1},{1,2},{2,3},{3,7},{7,6},{6,5},{5,4},{4,0},{8,9},{9,10},{10,1... | collective-permute-start | bytes 393224 | tf_op jit(solution)/shard_map/ppermute | solution.py:34
  65.7 6.8 %collective-permute-start.22 = (bf16[128,512]{1,0:T(8,128)(2,1)S(1)}, bf16[128,512]{1,0:T(8,128)(2,1)S(1)}, u32[]{:S(2)}, u32[]{:S(2)}) collective-permute-start(bf16[128,512]{1,0:T(8,128)(2,1)S(1)} %get-tuple-element.89), channel_id=1, source_target_pairs={{0,4},{1,0},{2,1},{3,2},{7,3},{6,7},{5,6},{4,5},{8,12},{9,8},{10,9... | collective-permute-start | bytes 393224 | tf_op jit(solution)/shard_map/ppermute | solution.py:34
  66.3 6.3 %collective-permute-start.23 = (bf16[128,512]{1,0:T(8,128)(2,1)S(1)}, bf16[128,512]{1,0:T(8,128)(2,1)S(1)}, u32[]{:S(2)}, u32[]{:S(2)}) collective-permute-start(bf16[128,512]{1,0:T(8,128)(2,1)S(1)} %get-tuple-element.90), channel_id=1, source_target_pairs={{0,1},{1,2},{2,3},{3,7},{7,6},{6,5},{5,4},{4,0},{8,9},{9,10},{10,1... | collective-permute-start | bytes 393224 | tf_op jit(solution)/shard_map/ppermute | solution.py:34
  70.4 5.0 %collective-permute-start.30 = (bf16[128,512]{1,0:T(8,128)(2,1)S(1)}, bf16[128,512]{1,0:T(8,128)(2,1)S(1)}, u32[]{:S(2)}, u32[]{:S(2)}) collective-permute-start(bf16[128,512]{1,0:T(8,128)(2,1)S(1)} %get-tuple-element.97), channel_id=1, source_target_pairs={{0,1},{1,2},{2,3},{3,7},{7,6},{6,5},{5,4},{4,0},{8,9},{9,10},{10,1... | collective-permute-start | bytes 393224 | tf_op jit(solution)/shard_map/ppermute | solution.py:34
  73.2 7.3 %collective-permute-start.24 = (bf16[128,512]{1,0:T(8,128)(2,1)S(1)}, bf16[128,512]{1,0:T(8,128)(2,1)S(1)}, u32[]{:S(2)}, u32[]{:S(2)}) collective-permute-start(bf16[128,512]{1,0:T(8,128)(2,1)S(1)} %get-tuple-element.91), channel_id=1, source_target_pairs={{0,4},{1,0},{2,1},{3,2},{7,3},{6,7},{5,6},{4,5},{8,12},{9,8},{10,9... | collective-permute-start | bytes 393224 | tf_op jit(solution)/shard_map/ppermute | solution.py:34
  73.4 7.0 %collective-permute-start.25 = (bf16[128,512]{1,0:T(8,128)(2,1)S(1)}, bf16[128,512]{1,0:T(8,128)(2,1)S(1)}, u32[]{:S(2)}, u32[]{:S(2)}) collective-permute-start(bf16[128,512]{1,0:T(8,128)(2,1)S(1)} %get-tuple-element.92), channel_id=1, source_target_pairs={{0,1},{1,2},{2,3},{3,7},{7,6},{6,5},{5,4},{4,0},{8,9},{9,10},{10,1... | collective-permute-start | bytes 393224 | tf_op jit(solution)/shard_map/ppermute | solution.py:34
  77.0 5.0 %collective-permute-start.32 = (bf16[128,512]{1,0:T(8,128)(2,1)S(1)}, bf16[128,512]{1,0:T(8,128)(2,1)S(1)}, u32[]{:S(2)}, u32[]{:S(2)}) collective-permute-start(bf16[128,512]{1,0:T(8,128)(2,1)S(1)} %get-tuple-element.99), channel_id=1, source_target_pairs={{0,1},{1,2},{2,3},{3,7},{7,6},{6,5},{5,4},{4,0},{8,9},{9,10},{10,1... | collective-permute-start | bytes 393224 | tf_op jit(solution)/shard_map/ppermute | solution.py:34
  (14 other events, 84.3 us)

commit v4 on v3

--- a/solution.py
+++ b/solution.py
@@ -39,7 +39,7 @@
     return order, along, shifted
 
 
-def call(kernel, name, outs, operands, specs, scratch=(), limit=4, flops=0, bytes_accessed=0):
+def call(kernel, name, outs, operands, specs, scratch=(), limit=12, flops=0, bytes_accessed=0):
     return pl.pallas_call(
         kernel,
         out_shape=[pltpu.VMEM(shape, dtype) for shape, dtype in outs],
@@ -65,18 +65,18 @@
     return snake((place + distance) % (rows * line))
 
 
-def columns_of(decoders, distance, which, half):
-    start = owner_at(distance) * (2 * half) + which * half
-    return decoders[:, pl.ds(pl.multiple_of(start, half), half)]
+def columns_of(decoders, distance, which, count, mine):
+    start = owner_at(distance) * mine + which * count
+    return decoders[:, pl.ds(pl.multiple_of(start, count), count)]
 
 
 def upright(row, lanes):
     return jnp.broadcast_to(row, (lanes, row.shape[1])).T
 
 
-def encode_kernel(ids, cache, weight, bias, low, high, ids_, held, blocks, bias_, across, sems):
+def encode_kernel(ids, cache, weight, bias, latents, ids_, held, blocks, bias_, across, sems):
     count, block = blocks.shape[:2]
-    tokens, half = across.shape[1], low.shape[0]
+    tokens = across.shape[1]
     copies = [
         pltpu.make_async_copy(ids, ids_.at[0], sems.at[count]),
         pltpu.make_async_copy(cache.at[0], held, sems.at[count + 1]),
@@ -100,21 +100,20 @@
         streams[i].wait()
         pre = jnp.dot(blocks[i], across[...], preferred_element_type=F32)
         pre = pre + upright(bias_[:, i * block : (i + 1) * block], tokens)
-        out = low if (i + 1) * block <= half else high
-        start = i * block % half
-        out[start : start + block] = jnp.maximum(pre, 0.0).astype(BF16)
+        latents[i * block : (i + 1) * block] = jnp.maximum(pre, 0.0).astype(BF16)
 
 
 def decoded(decoders, pieces):
     total = None
     for distance, which, piece in pieces:
-        columns = columns_of(decoders, distance, which, piece.shape[0])
+        mine = decoders.shape[1] // (lax.axis_size("dp") * lax.axis_size("tensor"))
+        columns = columns_of(decoders, distance, which, piece.shape[0], mine)
         part = jnp.dot(columns, piece[...], preferred_element_type=F32)
         total = part if total is None else total + part
     return total
 
 
-def load_decode_kernel(source, low, high, decoders, total, sems):
+def load_decode_kernel(source, latents, decoders, total, sems):
     layers = sems.shape[0]
     rows = source.shape[0] // layers
     copies = []
@@ -125,21 +124,32 @@
     for i in range(layers):
         part = pl.ds(i * rows, rows)
         copies[i].wait()
-        total[part] = decoded(decoders.at[part], [(0, 0, low), (0, 1, high)])
-
-
-def decode_kernel(decoders, before, one, other, total, *, pieces):
+        total[part] = decoded(decoders.at[part], [(0, 0, latents)])
+
+
+def split_kernel(rise, fall, *outs):
+    half = rise.shape[0] // 2
+    for value, low, high in ((rise, *outs[:2]), (fall, *outs[2:])):
+        low[...] = value[:half]
+        high[...] = value[half:]
+
+
+def decode_kernel(decoders, before, one, other, total, *, pieces, layers):
     (d0, w0), (d1, w1) = pieces
-    total[...] = before[...] + decoded(decoders, [(d0, w0, one), (d1, w1, other)])
-
-
-def decode_last_kernel(decoders, before, one, other, own, *sent, pieces):
+    rows = total.shape[0] // layers
+    for i in range(layers):
+        part = pl.ds(i * rows, rows)
+        both = [(d0, w0, one), (d1, w1, other)]
+        total[part] = before[part] + decoded(decoders.at[part], both)
+
+
+def decode_last_kernel(decoders, before, one, other, *outs, pieces):
     (d0, w0), (d1, w1) = pieces
-    total = before[...] + decoded(decoders, [(d0, w0, one), (d1, w1, other)])
-    rows = own.shape[0]
-    own[...] = total[:rows]
-    for offset, out in enumerate(sent, 1):
-        out[...] = total[offset * rows : (offset + 1) * rows].astype(BF16)
+    rows = outs[0].shape[0]
+    for i, out in enumerate(outs):
+        part = pl.ds(i * rows, rows)
+        both = [(d0, w0, one), (d1, w1, other)]
+        out[...] = (before[part] + decoded(decoders.at[part], both)).astype(out.dtype)
 
 
 def error_kernel(own, incoming, bias, target, returned, *refs, layers):
@@ -162,7 +172,7 @@
 
 
 def gradient(decoders, back, distance, which, half):
-    columns = columns_of(decoders, distance, which, half)
+    columns = columns_of(decoders, distance, which, half, 2 * half)
     return jnp.dot(back[...], columns, preferred_element_type=F32)
 
 
@@ -173,28 +183,29 @@
         out[...] = gradient(decoders, back, distance, which, out.shape[1]).astype(BF16)
 
 
-def gradient_kernel(decoders, back, *refs, pieces):
-    count = len(pieces)
-    came, outs = refs[:-count], refs[-count:]
-    for i, (distance, which) in enumerate(pieces):
-        total = gradient(decoders, back, distance, which, outs[i].shape[1])
-        if came:
-            total = total + came[i][...].astype(F32)
-        outs[i][...] = total.astype(BF16)
+def gradient_kernel(decoders, back, *outs, pieces):
+    for (distance, which), out in zip(pieces, outs):
+        part = gradient(decoders, back, distance, which, out.shape[1])
+        out[...] = part.astype(out.dtype)
+
+
+def add_kernel(one, other, came_one, came_other, out_one, out_other):
+    out_one[...] = (one[...] + came_one[...].astype(F32)).astype(BF16)
+    out_other[...] = (other[...] + came_other[...].astype(F32)).astype(BF16)
 
 
 def gradient_own_kernel(decoders, back, low, high, total):
     half = low.shape[1]
     for which, came in ((0, low), (1, high)):
         part = gradient(decoders, back, 0, which, half) + came[...].astype(F32)
-        total[:, which * half : (which + 1) * half] = part
+        total[which * half : (which + 1) * half, :] = part.T
 
 
 def gradient_last_kernel(before, low, high, out):
     half = low.shape[1]
     for which, came in ((0, low), (1, high)):
-        part = before[:, which * half : (which + 1) * half] + came[...].astype(F32)
-        out[which * half : (which + 1) * half, :] = part.T
+        part = slice(which * half, (which + 1) * half)
+        out[part, :] = before[part, :] + came[...].T.astype(F32)
 
 
 def tiled_local(cache, token_ids, enc_weight, enc_bias, dec_weight, dec_bias, incoming, target, returned):
@@ -213,10 +224,10 @@
 
     block = min(256, half)
     count = mine // block
-    low, high = call(
+    (latents,) = call(
         encode_kernel,
         "encode",
-        [((half, tokens), BF16)] * 2,
+        [((mine, tokens), BF16)],
         [in_hbm(value) for value in (token_ids, cache, enc_weight, enc_bias)],
         [HBM] * 4,
         [
@@ -227,46 +238,56 @@
             pltpu.VMEM((width, tokens), BF16),
             pltpu.SemaphoreType.DMA((count + 3,)),
         ],
-        limit=20,
+        limit=24,
         flops=2 * tokens * width * (mine + slots),
         bytes_accessed=2 * width * (mine + slots),
     )
     piece_flops = 2 * tokens * half * outs_all
-    outer = [along(low, 1), along(high, -1)]
-    inner = [along(high, 1), along(low, -1)]
-    decoders, total = call(
+    rise, fall = along(latents, 1), along(latents, -1)
+    held, total = call(
         load_decode_kernel,
         "load_decode",
         [(decoders.shape, BF16), ((outs_all, tokens), F32)],
-        (in_hbm(decoders), low, high),
-        [HBM] + [VMEM] * 2,
+        (in_hbm(decoders), latents),
+        [HBM, VMEM],
         [pltpu.SemaphoreType.DMA((layers,))],
         flops=2 * piece_flops,
         bytes_accessed=4 * decoders.size,
     )
-    for step in range(1, far):
+
+    def decode(name, total, pieces, one, other):
+        (total,) = call(
+            functools.partial(decode_kernel, pieces=pieces, layers=layers),
+            name,
+            [((outs_all, tokens), F32)],
+            (held, total, one, other),
+            [VMEM] * 4,
+            flops=2 * piece_flops,
+        )
+        return total
+
+    rise, fall, total = lax.optimization_barrier((rise, fall, total))
+    halves = call(
+        split_kernel, "split", [((half, tokens), BF16)] * 4, (rise, fall), [VMEM] * 2
+    )
+    outer = [along(halves[0], 1), along(halves[3], -1)]
+    inner = [along(halves[1], 1), along(halves[2], -1)]
+    total = decode("decode_1", total, ((size - 1, 0), (1, 0)), rise, fall)
+    for step in range(2, far):
         rise, fall, total = lax.optimization_barrier((*outer, total))
         near = rise, fall
         outer = [along(rise, 1), along(fall, -1)]
         rise, fall, *near = lax.optimization_barrier((*inner, *near))
         if step < far - 1:
             inner = [along(rise, 1), along(fall, -1)]
-        for (one, other), which in ((near, 0), ((rise, fall), 1)):
-            (total,) = call(
-                functools.partial(
-                    decode_kernel, pieces=((size - step, which), (step, 1 - which))
-                ),
-                f"decode_{step}_{which}",
-                [((outs_all, tokens), F32)],
-                (decoders, total, one, other),
-                [VMEM] * 4,
-                flops=2 * piece_flops,
-            )
+        total = decode(f"decode_{step}_0", total, ((size - step, 0), (step, 1)), *near)
+        pieces = ((size - step, 1), (step, 0))
+        total = decode(f"decode_{step}_1", total, pieces, rise, fall)
     own, *sent = call(
         functools.partial(decode_last_kernel, pieces=((far, 0), (far, 1))),
         "decode_last",
         [((columns, tokens), F32)] + [((columns, tokens), BF16)] * (layers - 1),
-        (decoders, total, *outer),
+        (held, total, *outer),
         [VMEM] * 4,
         flops=2 * piece_flops,
     )
@@ -281,41 +302,49 @@
     )
     came = [shifted(value, -offset) for offset, value in enumerate(sent, 1)]
     piece = ((tokens, half), BF16)
+    product = ((tokens, half), F32)
     back, *outer = call(
         functools.partial(gradient_first_kernel, layers=layers, pieces=((far, 0), (far, 1))),
         "gradient_far",
         [((tokens, outs_all), BF16), piece, piece],
-        (decoders, error, *came),
+        (held, error, *came),
         [VMEM] * (layers + 1),
         flops=2 * piece_flops,
     )
-    inner = []
-    for step in range(far - 1, -1, -1):
-        outer = [along(outer[0], 1), along(outer[1], -1)]
-        if step == 0:
-            break
-        inner = call(
-            functools.partial(gradient_kernel, pieces=((size - step, 0), (step, 1))),
-            f"gradient_inner_{step}",
-            [piece, piece],
-            (decoders, back, *inner),
-            [VMEM] * (2 + len(inner)),
+
+    def products(name, kind, pieces, after):
+        nonlocal back
+        back, *_ = lax.optimization_barrier((back, *after))
+        return call(
+            functools.partial(gradient_kernel, pieces=pieces),
+            name,
+            [kind, kind],
+            (held, back),
+            [VMEM] * 2,
             flops=2 * piece_flops,
         )
+
+    def added(name, parts, came):
+        return call(add_kernel, name, [piece, piece], (*parts, *came), [VMEM] * 4)
+
+    last = far - 1
+    outer = [along(outer[0], 1), along(outer[1], -1)]
+    inner = products("gradient_inner", piece, ((size - last, 0), (last, 1)), ())
+    ready = inner
+    for step in range(last, 0, -1):
         inner = [along(inner[0], -1), along(inner[1], 1)]
-        outer = call(
-            functools.partial(gradient_kernel, pieces=((step, 0), (size - step, 1))),
-            f"gradient_outer_{step}",
-            [piece, piece],
-            (decoders, back, *outer),
-            [VMEM] * (2 + len(outer)),
-            flops=2 * piece_flops,
-        )
+        parts = products(f"outer_{step}", product, ((step, 0), (size - step, 1)), ready)
+        ready = added(f"add_outer_{step}", parts, outer)
+        outer = [along(ready[0], 1), along(ready[1], -1)]
+        if step > 1:
+            pieces = ((size - step + 1, 0), (step - 1, 1))
+            parts = products(f"inner_{step - 1}", product, pieces, ready)
+            inner = ready = added(f"add_inner_{step - 1}", parts, inner)
     (part,) = call(
         gradient_own_kernel,
         "gradient_own",
-        [((tokens, mine), F32)],
-        (decoders, back, *inner),
+        [((mine, tokens), F32)],
+        (held, back, *inner),
         [VMEM] * 4,
         flops=2 * piece_flops,
     )
@@ -324,7 +353,7 @@
         out_shape=jax.ShapeDtypeStruct((mine, tokens), F32),
         in_specs=[VMEM] * 3,
         out_specs=VMEM,
-        compiler_params=pltpu.CompilerParams(vmem_limit_bytes=4 * 2**20),
+        compiler_params=pltpu.CompilerParams(vmem_limit_bytes=12 * 2**20),
         name="gradient_last",
     )(part, *outer)
     return (error.T[None], beyond.T[None], lat_grad[None])
@@ -416,7 +445,7 @@
     mine, width = enc_weight.shape[1:]
     whole_tiles = (
         size % 2 == 0
-        and size >= 4
+        and size >= 6
         and mine % 256 == 0
         and width % 128 == 0
         and dec_weight.shape[2] % 16 == 0

time: 83.9 us -> 81.4 us (0.970)
  starting transfers between devices: 35.4 us -> 33.5 us
    ppermute x28 -> x26, starting transfers between devices: 29.9 us -> 27.8 us  [along(): return lax.ppermute(value, GROUP, pairs)]
    ppermute x28 -> x26, waiting for transfers between devices: 12.1 us -> 11.3 us  [along(): return lax.ppermute(value, GROUP, pairs)]
    pallas_call x18 -> x23, Pallas kernels: 25.5 us -> 25.7 us  [call(): pl.pallas_call(kernel, out_shape=[pltpu.VMEM(shape, dtype) for shape, dty...]
  transfers between devices with their start and end apart: 34 -> 32, of which waited for: 19 -> 16; matrix products, arithmetic and copies ran while one was open for 2% -> 2% of each run, Pallas kernels for 21% -> 22%
where the time goes in v4:
time: 81.4 us; the launch traced here: 81.2 us
  starting transfers between devices  33.5 us (41%)
  Pallas kernels  26.6 us (33%)
  waiting for transfers between devices  18.9 us (23%)
  local copies, waits for them, and re-layouts  1.33 us (2%)
  between operations  0.94 us (1%)
    ppermute x26, starting transfers between devices, along(): return lax.ppermute(value, GROUP, pairs)  27.8 us
    pallas_call x23, Pallas kernels, call(): pl.pallas_call(kernel, out_shape=[pltpu.VMEM(shape, dtype) for shape, dty...  25.7 us
    ppermute x26, waiting for transfers between devices, along(): return lax.ppermute(value, GROUP, pairs)  11.3 us
    ppermute x6, waiting for transfers between devices, shifted(): lax.ppermute(value, 'section', [(i, (i + by) % layers) for i in range(lay...  7.56 us
    ppermute x6, starting transfers between devices, shifted(): lax.ppermute(value, 'section', [(i, (i + by) % layers) for i in range(lay...  5.69 us
  transfers between devices with their start and end apart: 32, of which 16 were waited for; matrix products, arithmetic and copies ran while one was open for 2% of the time, Pallas kernels for 22%

profile of v4, /device:TPU:0, one launch (start us, length us, event | category | flops | bytes accessed | tf_op | source)
XLA Modules:
  0.0 81.2 jit_solution(2539553527462301479)
XLA Ops:
  0.6 6.3 %encode.1.latents = bf16[1024,128]{1,0:T(8,128)(2,1)S(1)} custom-call(s32[128]{0:T(128)} %ids.1, bf16[1,256,5376]{2,1,0:T(8,128)(2,1)} %cache.1, bf16[1,1024,5376]{2,1,0:T(8,128)(2,1)} %weight.1, f32[1,1024]{1,0:T(1,128)} %bias.2), custom_call_target="tpu_custom_call" | custom-call | flops 1761607680 | bytes 13762560 | tf_op jit(solution)/shard_map/encode/pallas_call | solution.py:43
  7.0 3.1 %collective-permute-start = (bf16[1024,128]{1,0:T(8,128)(2,1)S(1)}, bf16[1024,128]{1,0:T(8,128)(2,1)S(1)}, u32[]{:S(2)}, u32[]{:S(2)}) collective-permute-start(bf16[1024,128]{1,0:T(8,128)(2,1)S(1)} %encode.1.latents), channel_id=1, source_target_pairs={{0,1},{1,2},{2,3},{3,7},{7,6},{6,5},{5,4},{4,0},{8,9},{9,10},{10,1... | collective-permute-start | bytes 786440 | tf_op jit(solution)/shard_map/ppermute | solution.py:34
  10.0 7.9 %load_decode.1 = (bf16[1344,8192]{1,0:T(8,128)(2,1)S(1)}, f32[1344,128]{1,0:T(8,128)S(1)}) custom-call(bf16[1344,8192]{1,0:T(8,128)(2,1)} %bitcast.22, bf16[1024,128]{1,0:T(8,128)(2,1)S(1)} %encode.1.latents), custom_call_target="tpu_custom_call" | custom-call | flops 352321536 | bytes 44040192 | tf_op jit(solution)/shard_map/load_decode/pallas_call | solution.py:43
  18.0 2.1 %collective-permute-start.2 = (bf16[512,128]{1,0:T(8,128)(2,1)S(1)}, bf16[512,128]{1,0:T(8,128)(2,1)S(1)}, u32[]{:S(2)}, u32[]{:S(2)}) collective-permute-start(bf16[512,128]{1,0:T(8,128)(2,1)S(1)} %get-tuple-element.69), channel_id=1, source_target_pairs={{0,1},{1,2},{2,3},{3,7},{7,6},{6,5},{5,4},{4,0},{8,9},{9,10},{10,1... | collective-permute-start | bytes 393224 | tf_op jit(solution)/shard_map/ppermute | solution.py:34
  20.1 2.0 %collective-permute-start.6 = (bf16[512,128]{1,0:T(8,128)(2,1)S(1)}, bf16[512,128]{1,0:T(8,128)(2,1)S(1)}, u32[]{:S(2)}, u32[]{:S(2)}) collective-permute-start(bf16[512,128]{1,0:T(8,128)(2,1)S(1)} %get-tuple-element.75), channel_id=1, source_target_pairs={{0,1},{1,2},{2,3},{3,7},{7,6},{6,5},{5,4},{4,0},{8,9},{9,10},{10,1... | collective-permute-start | bytes 393224 | tf_op jit(solution)/shard_map/ppermute | solution.py:34
  22.1 1.6 %decode_1.1.before = f32[1344,128]{1,0:T(8,128)S(1)} custom-call(bf16[1344,8192]{1,0:T(8,128)(2,1)S(1)} %get-tuple-element.65.decoders, f32[1344,128]{1,0:T(8,128)S(1)} %get-tuple-element.71.before, bf16[1024,128]{1,0:T(8,128)(2,1)S(1)} %collective-permute-done.rise.one, bf16[1024,128]{1,0:T(8,128)(2,1)S(1)} %collective-permute-done.1.fall.other), custom_call_target="tpu_custom_call" | custom-call | flops 352321536 | tf_op jit(solution)/shard_map/decode_1/pallas_call | solution.py:43
  24.4 1.6 %collective-permute-done.3.other = bf16[512,128]{1,0:T(8,128)(2,1)S(1)} collective-permute-done((bf16[512,128]{1,0:T(8,128)(2,1)S(1)}, bf16[512,128]{1,0:T(8,128)(2,1)S(1)}, u32[]{:S(2)}, u32[]{:S(2)}) %collective-permute-start.3) | collective-permute-done | bytes 131104 | tf_op jit(solution)/shard_map/ppermute | solution.py:34
  25.9 1.6 %collective-permute-start.4 = (bf16[512,128]{1,0:T(8,128)(2,1)S(1)}, bf16[512,128]{1,0:T(8,128)(2,1)S(1)}, u32[]{:S(2)}, u32[]{:S(2)}) collective-permute-start(bf16[512,128]{1,0:T(8,128)(2,1)S(1)} %collective-permute-done.2.one), channel_id=1, source_target_pairs={{0,1},{1,2},{2,3},{3,7},{7,6},{6,5},{5,4},{4,0},{8,9},{9,10},{10,1... | collective-permute-start | bytes 393224 | tf_op jit(solution)/shard_map/ppermute | solution.py:34
  27.9 1.6 %collective-permute-start.8 = (bf16[512,128]{1,0:T(8,128)(2,1)S(1)}, bf16[512,128]{1,0:T(8,128)(2,1)S(1)}, u32[]{:S(2)}, u32[]{:S(2)}) collective-permute-start(bf16[512,128]{1,0:T(8,128)(2,1)S(1)} %collective-permute-done.6.one), channel_id=1, source_target_pairs={{0,1},{1,2},{2,3},{3,7},{7,6},{6,5},{5,4},{4,0},{8,9},{9,10},{10,1... | collective-permute-start | bytes 393224 | tf_op jit(solution)/shard_map/ppermute | solution.py:34
  32.5 1.6 %collective-permute-start.10 = (bf16[512,128]{1,0:T(8,128)(2,1)S(1)}, bf16[512,128]{1,0:T(8,128)(2,1)S(1)}, u32[]{:S(2)}, u32[]{:S(2)}) collective-permute-start(bf16[512,128]{1,0:T(8,128)(2,1)S(1)} %collective-permute-done.4.one), channel_id=1, source_target_pairs={{0,1},{1,2},{2,3},{3,7},{7,6},{6,5},{5,4},{4,0},{8,9},{9,10},{10,1... | collective-permute-start | bytes 393224 | tf_op jit(solution)/shard_map/ppermute | solution.py:34
  37.5 1.5 %collective-permute-done.11.other = bf16[512,128]{1,0:T(8,128)(2,1)S(1)} collective-permute-done((bf16[512,128]{1,0:T(8,128)(2,1)S(1)}, bf16[512,128]{1,0:T(8,128)(2,1)S(1)}, u32[]{:S(2)}, u32[]{:S(2)}) %collective-permute-start.11) | collective-permute-done | bytes 131104 | tf_op jit(solution)/shard_map/ppermute | solution.py:34
  40.1 1.6 %collective-permute-start.13 = (bf16[336,128]{1,0:T(8,128)(2,1)S(1)}, bf16[336,128]{1,0:T(8,128)(2,1)S(1)}, u32[]{:S(2)}, u32[]{:S(2)}) collective-permute-start(bf16[336,128]{1,0:T(8,128)(2,1)S(1)} %get-tuple-element.90), channel_id=1, source_target_pairs={{0,16},{8,24},{16,0},{24,8},{1,17},{9,25},{17,1},{25,9},{2,18},{10... | collective-permute-start | bytes 258056 | tf_op jit(solution)/shard_map/ppermute | solution.py:37
  41.7 1.4 %collective-permute-start.14 = (bf16[336,128]{1,0:T(8,128)(2,1)S(1)}, bf16[336,128]{1,0:T(8,128)(2,1)S(1)}, u32[]{:S(2)}, u32[]{:S(2)}) collective-permute-start(bf16[336,128]{1,0:T(8,128)(2,1)S(1)} %get-tuple-element.91), channel_id=1, source_target_pairs={{0,24},{8,0},{16,8},{24,16},{1,25},{9,1},{17,9},{25,17},{2,26},{10... | collective-permute-start | bytes 258056 | tf_op jit(solution)/shard_map/ppermute | solution.py:37
  43.1 1.2 %collective-permute-done.12.refs_0_ = bf16[336,128]{1,0:T(8,128)(2,1)S(1)} collective-permute-done((bf16[336,128]{1,0:T(8,128)(2,1)S(1)}, bf16[336,128]{1,0:T(8,128)(2,1)S(1)}, u32[]{:S(2)}, u32[]{:S(2)}) %collective-permute-start.12) | collective-permute-done | bytes 86048 | tf_op jit(solution)/shard_map/ppermute | solution.py:37
  44.4 1.2 %collective-permute-done.13.refs_1_ = bf16[336,128]{1,0:T(8,128)(2,1)S(1)} collective-permute-done((bf16[336,128]{1,0:T(8,128)(2,1)S(1)}, bf16[336,128]{1,0:T(8,128)(2,1)S(1)}, u32[]{:S(2)}, u32[]{:S(2)}) %collective-permute-start.13) | collective-permute-done | bytes 86048 | tf_op jit(solution)/shard_map/ppermute | solution.py:37
  46.0 2.0 %collective-permute-start.15 = (bf16[336,128]{1,0:T(8,128)(2,1)S(1)}, bf16[336,128]{1,0:T(8,128)(2,1)S(1)}, u32[]{:S(2)}, u32[]{:S(2)}) collective-permute-start(bf16[336,128]{1,0:T(8,128)(2,1)S(1)} %get-tuple-element.94), channel_id=1, source_target_pairs={{0,24},{8,0},{16,8},{24,16},{1,25},{9,1},{17,9},{25,17},{2,26},{10... | collective-permute-start | bytes 258056 | tf_op jit(solution)/shard_map/ppermute | solution.py:37
  48.5 1.9 %collective-permute-done.15.refs_1_ = bf16[336,128]{1,0:T(8,128)(2,1)S(1)} collective-permute-done((bf16[336,128]{1,0:T(8,128)(2,1)S(1)}, bf16[336,128]{1,0:T(8,128)(2,1)S(1)}, u32[]{:S(2)}, u32[]{:S(2)}) %collective-permute-start.15) | collective-permute-done | bytes 86048 | tf_op jit(solution)/shard_map/ppermute | solution.py:37
  50.4 2.9 %collective-permute-done.16.refs_2_ = bf16[336,128]{1,0:T(8,128)(2,1)S(1)} collective-permute-done((bf16[336,128]{1,0:T(8,128)(2,1)S(1)}, bf16[336,128]{1,0:T(8,128)(2,1)S(1)}, u32[]{:S(2)}, u32[]{:S(2)}) %collective-permute-start.16) | collective-permute-done | bytes 86048 | tf_op jit(solution)/shard_map/ppermute | solution.py:37
  54.0 1.5 %collective-permute-start.18 = (bf16[128,512]{1,0:T(8,128)(2,1)S(1)}, bf16[128,512]{1,0:T(8,128)(2,1)S(1)}, u32[]{:S(2)}, u32[]{:S(2)}) collective-permute-start(bf16[128,512]{1,0:T(8,128)(2,1)S(1)} %get-tuple-element.103), channel_id=1, source_target_pairs={{0,1},{1,2},{2,3},{3,7},{7,6},{6,5},{5,4},{4,0},{8,9},{9,10},{10,1... | collective-permute-start | bytes 393224 | tf_op jit(solution)/shard_map/ppermute | solution.py:34
  57.2 1.6 %collective-permute-start.21 = (bf16[128,512]{1,0:T(8,128)(2,1)S(1)}, bf16[128,512]{1,0:T(8,128)(2,1)S(1)}, u32[]{:S(2)}, u32[]{:S(2)}) collective-permute-start(bf16[128,512]{1,0:T(8,128)(2,1)S(1)} %get-tuple-element.99), channel_id=1, source_target_pairs={{0,1},{1,2},{2,3},{3,7},{7,6},{6,5},{5,4},{4,0},{8,9},{9,10},{10,1... | collective-permute-start | bytes 393224 | tf_op jit(solution)/shard_map/ppermute | solution.py:34
  61.2 1.4 %collective-permute-start.22 = (bf16[128,512]{1,0:T(8,128)(2,1)S(1)}, bf16[128,512]{1,0:T(8,128)(2,1)S(1)}, u32[]{:S(2)}, u32[]{:S(2)}) collective-permute-start(bf16[128,512]{1,0:T(8,128)(2,1)S(1)} %get-tuple-element.105), channel_id=1, source_target_pairs={{0,1},{1,2},{2,3},{3,7},{7,6},{6,5},{5,4},{4,0},{8,9},{9,10},{10,1... | collective-permute-start | bytes 393224 | tf_op jit(solution)/shard_map/ppermute | solution.py:34
  64.5 1.5 %collective-permute-start.25 = (bf16[128,512]{1,0:T(8,128)(2,1)S(1)}, bf16[128,512]{1,0:T(8,128)(2,1)S(1)}, u32[]{:S(2)}, u32[]{:S(2)}) collective-permute-start(bf16[128,512]{1,0:T(8,128)(2,1)S(1)} %get-tuple-element.111), channel_id=1, source_target_pairs={{0,1},{1,2},{2,3},{3,7},{7,6},{6,5},{5,4},{4,0},{8,9},{9,10},{10,1... | collective-permute-start | bytes 393224 | tf_op jit(solution)/shard_map/ppermute | solution.py:34
  67.6 1.5 %collective-permute-start.28 = (bf16[128,512]{1,0:T(8,128)(2,1)S(1)}, bf16[128,512]{1,0:T(8,128)(2,1)S(1)}, u32[]{:S(2)}, u32[]{:S(2)}) collective-permute-start(bf16[128,512]{1,0:T(8,128)(2,1)S(1)} %get-tuple-element.115), channel_id=1, source_target_pairs={{0,1},{1,2},{2,3},{3,7},{7,6},{6,5},{5,4},{4,0},{8,9},{9,10},{10,1... | collective-permute-start | bytes 393224 | tf_op jit(solution)/shard_map/ppermute | solution.py:34
  71.1 1.3 %collective-permute-start.27 = (bf16[128,512]{1,0:T(8,128)(2,1)S(1)}, bf16[128,512]{1,0:T(8,128)(2,1)S(1)}, u32[]{:S(2)}, u32[]{:S(2)}) collective-permute-start(bf16[128,512]{1,0:T(8,128)(2,1)S(1)} %get-tuple-element.121), channel_id=1, source_target_pairs={{0,1},{1,2},{2,3},{3,7},{7,6},{6,5},{5,4},{4,0},{8,9},{9,10},{10,1... | collective-permute-start | bytes 393224 | tf_op jit(solution)/shard_map/ppermute | solution.py:34
  (74 shorter events, 28.5 us)
Async XLA Ops:
  7.0 11.0 %collective-permute-start = (bf16[1024,128]{1,0:T(8,128)(2,1)S(1)}, bf16[1024,128]{1,0:T(8,128)(2,1)S(1)}, u32[]{:S(2)}, u32[]{:S(2)}) collective-permute-start(bf16[1024,128]{1,0:T(8,128)(2,1)S(1)} %encode.1.latents), channel_id=1, source_target_pairs={{0,1},{1,2},{2,3},{3,7},{7,6},{6,5},{5,4},{4,0},{8,9},{9,10},{10,1... | collective-permute-start | bytes 786440 | tf_op jit(solution)/shard_map/ppermute | solution.py:34
  10.0 7.9 %collective-permute-start.1 = (bf16[1024,128]{1,0:T(8,128)(2,1)S(1)}, bf16[1024,128]{1,0:T(8,128)(2,1)S(1)}, u32[]{:S(2)}, u32[]{:S(2)}) collective-permute-start(bf16[1024,128]{1,0:T(8,128)(2,1)S(1)} %encode.1.latents), channel_id=1, source_target_pairs={{0,4},{1,0},{2,1},{3,2},{7,3},{6,7},{5,6},{4,5},{8,12},{9,8},{10,9... | collective-permute-start | bytes 786440 | tf_op jit(solution)/shard_map/ppermute | solution.py:34
  18.0 6.4 %collective-permute-start.2 = (bf16[512,128]{1,0:T(8,128)(2,1)S(1)}, bf16[512,128]{1,0:T(8,128)(2,1)S(1)}, u32[]{:S(2)}, u32[]{:S(2)}) collective-permute-start(bf16[512,128]{1,0:T(8,128)(2,1)S(1)} %get-tuple-element.69), channel_id=1, source_target_pairs={{0,1},{1,2},{2,3},{3,7},{7,6},{6,5},{5,4},{4,0},{8,9},{9,10},{10,1... | collective-permute-start | bytes 393224 | tf_op jit(solution)/shard_map/ppermute | solution.py:34
  20.1 5.9 %collective-permute-start.3 = (bf16[512,128]{1,0:T(8,128)(2,1)S(1)}, bf16[512,128]{1,0:T(8,128)(2,1)S(1)}, u32[]{:S(2)}, u32[]{:S(2)}) collective-permute-start(bf16[512,128]{1,0:T(8,128)(2,1)S(1)} %get-tuple-element.70), channel_id=1, source_target_pairs={{0,4},{1,0},{2,1},{3,2},{7,3},{6,7},{5,6},{4,5},{8,12},{9,8},{10,9... | collective-permute-start | bytes 393224 | tf_op jit(solution)/shard_map/ppermute | solution.py:34
  20.1 7.9 %collective-permute-start.6 = (bf16[512,128]{1,0:T(8,128)(2,1)S(1)}, bf16[512,128]{1,0:T(8,128)(2,1)S(1)}, u32[]{:S(2)}, u32[]{:S(2)}) collective-permute-start(bf16[512,128]{1,0:T(8,128)(2,1)S(1)} %get-tuple-element.75), channel_id=1, source_target_pairs={{0,1},{1,2},{2,3},{3,7},{7,6},{6,5},{5,4},{4,0},{8,9},{9,10},{10,1... | collective-permute-start | bytes 393224 | tf_op jit(solution)/shard_map/ppermute | solution.py:34
  22.1 5.9 %collective-permute-start.7 = (bf16[512,128]{1,0:T(8,128)(2,1)S(1)}, bf16[512,128]{1,0:T(8,128)(2,1)S(1)}, u32[]{:S(2)}, u32[]{:S(2)}) collective-permute-start(bf16[512,128]{1,0:T(8,128)(2,1)S(1)} %get-tuple-element.76), channel_id=1, source_target_pairs={{0,4},{1,0},{2,1},{3,2},{7,3},{6,7},{5,6},{4,5},{8,12},{9,8},{10,9... | collective-permute-start | bytes 393224 | tf_op jit(solution)/shard_map/ppermute | solution.py:34
  25.9 5.9 %collective-permute-start.4 = (bf16[512,128]{1,0:T(8,128)(2,1)S(1)}, bf16[512,128]{1,0:T(8,128)(2,1)S(1)}, u32[]{:S(2)}, u32[]{:S(2)}) collective-permute-start(bf16[512,128]{1,0:T(8,128)(2,1)S(1)} %collective-permute-done.2.one), channel_id=1, source_target_pairs={{0,1},{1,2},{2,3},{3,7},{7,6},{6,5},{5,4},{4,0},{8,9},{9,10},{10,1... | collective-permute-start | bytes 393224 | tf_op jit(solution)/shard_map/ppermute | solution.py:34
  27.9 6.5 %collective-permute-start.8 = (bf16[512,128]{1,0:T(8,128)(2,1)S(1)}, bf16[512,128]{1,0:T(8,128)(2,1)S(1)}, u32[]{:S(2)}, u32[]{:S(2)}) collective-permute-start(bf16[512,128]{1,0:T(8,128)(2,1)S(1)} %collective-permute-done.6.one), channel_id=1, source_target_pairs={{0,1},{1,2},{2,3},{3,7},{7,6},{6,5},{5,4},{4,0},{8,9},{9,10},{10,1... | collective-permute-start | bytes 393224 | tf_op jit(solution)/shard_map/ppermute | solution.py:34
  29.5 6.1 %collective-permute-start.9 = (bf16[512,128]{1,0:T(8,128)(2,1)S(1)}, bf16[512,128]{1,0:T(8,128)(2,1)S(1)}, u32[]{:S(2)}, u32[]{:S(2)}) collective-permute-start(bf16[512,128]{1,0:T(8,128)(2,1)S(1)} %collective-permute-done.7.other), channel_id=1, source_target_pairs={{0,4},{1,0},{2,1},{3,2},{7,3},{6,7},{5,6},{4,5},{8,12},{9,8},{10,9... | collective-permute-start | bytes 393224 | tf_op jit(solution)/shard_map/ppermute | solution.py:34
  32.5 5.1 %collective-permute-start.10 = (bf16[512,128]{1,0:T(8,128)(2,1)S(1)}, bf16[512,128]{1,0:T(8,128)(2,1)S(1)}, u32[]{:S(2)}, u32[]{:S(2)}) collective-permute-start(bf16[512,128]{1,0:T(8,128)(2,1)S(1)} %collective-permute-done.4.one), channel_id=1, source_target_pairs={{0,1},{1,2},{2,3},{3,7},{7,6},{6,5},{5,4},{4,0},{8,9},{9,10},{10,1... | collective-permute-start | bytes 393224 | tf_op jit(solution)/shard_map/ppermute | solution.py:34
  40.1 5.4 %collective-permute-start.13 = (bf16[336,128]{1,0:T(8,128)(2,1)S(1)}, bf16[336,128]{1,0:T(8,128)(2,1)S(1)}, u32[]{:S(2)}, u32[]{:S(2)}) collective-permute-start(bf16[336,128]{1,0:T(8,128)(2,1)S(1)} %get-tuple-element.90), channel_id=1, source_target_pairs={{0,16},{8,24},{16,0},{24,8},{1,17},{9,25},{17,1},{25,9},{2,18},{10... | collective-permute-start | bytes 258056 | tf_op jit(solution)/shard_map/ppermute | solution.py:37
  48.0 5.3 %collective-permute-start.16 = (bf16[336,128]{1,0:T(8,128)(2,1)S(1)}, bf16[336,128]{1,0:T(8,128)(2,1)S(1)}, u32[]{:S(2)}, u32[]{:S(2)}) collective-permute-start(bf16[336,128]{1,0:T(8,128)(2,1)S(1)} %get-tuple-element.95), channel_id=1, source_target_pairs={{0,16},{8,24},{16,0},{24,8},{1,17},{9,25},{17,1},{25,9},{2,18},{10... | collective-permute-start | bytes 258056 | tf_op jit(solution)/shard_map/ppermute | solution.py:37
  54.0 6.2 %collective-permute-start.18 = (bf16[128,512]{1,0:T(8,128)(2,1)S(1)}, bf16[128,512]{1,0:T(8,128)(2,1)S(1)}, u32[]{:S(2)}, u32[]{:S(2)}) collective-permute-start(bf16[128,512]{1,0:T(8,128)(2,1)S(1)} %get-tuple-element.103), channel_id=1, source_target_pairs={{0,1},{1,2},{2,3},{3,7},{7,6},{6,5},{5,4},{4,0},{8,9},{9,10},{10,1... | collective-permute-start | bytes 393224 | tf_op jit(solution)/shard_map/ppermute | solution.py:34
  55.5 5.6 %collective-permute-start.19 = (bf16[128,512]{1,0:T(8,128)(2,1)S(1)}, bf16[128,512]{1,0:T(8,128)(2,1)S(1)}, u32[]{:S(2)}, u32[]{:S(2)}) collective-permute-start(bf16[128,512]{1,0:T(8,128)(2,1)S(1)} %get-tuple-element.104), channel_id=1, source_target_pairs={{0,4},{1,0},{2,1},{3,2},{7,3},{6,7},{5,6},{4,5},{8,12},{9,8},{10,9... | collective-permute-start | bytes 393224 | tf_op jit(solution)/shard_map/ppermute | solution.py:34
  56.7 7.2 %collective-permute-start.20 = (bf16[128,512]{1,0:T(8,128)(2,1)S(1)}, bf16[128,512]{1,0:T(8,128)(2,1)S(1)}, u32[]{:S(2)}, u32[]{:S(2)}) collective-permute-start(bf16[128,512]{1,0:T(8,128)(2,1)S(1)} %get-tuple-element.98), channel_id=1, source_target_pairs={{0,4},{1,0},{2,1},{3,2},{7,3},{6,7},{5,6},{4,5},{8,12},{9,8},{10,9... | collective-permute-start | bytes 393224 | tf_op jit(solution)/shard_map/ppermute | solution.py:34
  57.2 6.7 %collective-permute-start.21 = (bf16[128,512]{1,0:T(8,128)(2,1)S(1)}, bf16[128,512]{1,0:T(8,128)(2,1)S(1)}, u32[]{:S(2)}, u32[]{:S(2)}) collective-permute-start(bf16[128,512]{1,0:T(8,128)(2,1)S(1)} %get-tuple-element.99), channel_id=1, source_target_pairs={{0,1},{1,2},{2,3},{3,7},{7,6},{6,5},{5,4},{4,0},{8,9},{9,10},{10,1... | collective-permute-start | bytes 393224 | tf_op jit(solution)/shard_map/ppermute | solution.py:34
  61.2 5.4 %collective-permute-start.22 = (bf16[128,512]{1,0:T(8,128)(2,1)S(1)}, bf16[128,512]{1,0:T(8,128)(2,1)S(1)}, u32[]{:S(2)}, u32[]{:S(2)}) collective-permute-start(bf16[128,512]{1,0:T(8,128)(2,1)S(1)} %get-tuple-element.105), channel_id=1, source_target_pairs={{0,1},{1,2},{2,3},{3,7},{7,6},{6,5},{5,4},{4,0},{8,9},{9,10},{10,1... | collective-permute-start | bytes 393224 | tf_op jit(solution)/shard_map/ppermute | solution.py:34
  63.9 6.4 %collective-permute-start.24 = (bf16[128,512]{1,0:T(8,128)(2,1)S(1)}, bf16[128,512]{1,0:T(8,128)(2,1)S(1)}, u32[]{:S(2)}, u32[]{:S(2)}) collective-permute-start(bf16[128,512]{1,0:T(8,128)(2,1)S(1)} %get-tuple-element.110), channel_id=1, source_target_pairs={{0,4},{1,0},{2,1},{3,2},{7,3},{6,7},{5,6},{4,5},{8,12},{9,8},{10,9... | collective-permute-start | bytes 393224 | tf_op jit(solution)/shard_map/ppermute | solution.py:34
  64.5 5.8 %collective-permute-start.25 = (bf16[128,512]{1,0:T(8,128)(2,1)S(1)}, bf16[128,512]{1,0:T(8,128)(2,1)S(1)}, u32[]{:S(2)}, u32[]{:S(2)}) collective-permute-start(bf16[128,512]{1,0:T(8,128)(2,1)S(1)} %get-tuple-element.111), channel_id=1, source_target_pairs={{0,1},{1,2},{2,3},{3,7},{7,6},{6,5},{5,4},{4,0},{8,9},{9,10},{10,1... | collective-permute-start | bytes 393224 | tf_op jit(solution)/shard_map/ppermute | solution.py:34
  67.6 5.4 %collective-permute-start.28 = (bf16[128,512]{1,0:T(8,128)(2,1)S(1)}, bf16[128,512]{1,0:T(8,128)(2,1)S(1)}, u32[]{:S(2)}, u32[]{:S(2)}) collective-permute-start(bf16[128,512]{1,0:T(8,128)(2,1)S(1)} %get-tuple-element.115), channel_id=1, source_target_pairs={{0,1},{1,2},{2,3},{3,7},{7,6},{6,5},{5,4},{4,0},{8,9},{9,10},{10,1... | collective-permute-start | bytes 393224 | tf_op jit(solution)/shard_map/ppermute | solution.py:34
  69.1 5.0 %collective-permute-start.29 = (bf16[128,512]{1,0:T(8,128)(2,1)S(1)}, bf16[128,512]{1,0:T(8,128)(2,1)S(1)}, u32[]{:S(2)}, u32[]{:S(2)}) collective-permute-start(bf16[128,512]{1,0:T(8,128)(2,1)S(1)} %get-tuple-element.116), channel_id=1, source_target_pairs={{0,4},{1,0},{2,1},{3,2},{7,3},{6,7},{5,6},{4,5},{8,12},{9,8},{10,9... | collective-permute-start | bytes 393224 | tf_op jit(solution)/shard_map/ppermute | solution.py:34
  70.4 7.2 %collective-permute-start.26 = (bf16[128,512]{1,0:T(8,128)(2,1)S(1)}, bf16[128,512]{1,0:T(8,128)(2,1)S(1)}, u32[]{:S(2)}, u32[]{:S(2)}) collective-permute-start(bf16[128,512]{1,0:T(8,128)(2,1)S(1)} %get-tuple-element.120), channel_id=1, source_target_pairs={{0,4},{1,0},{2,1},{3,2},{7,3},{6,7},{5,6},{4,5},{8,12},{9,8},{10,9... | collective-permute-start | bytes 393224 | tf_op jit(solution)/shard_map/ppermute | solution.py:34
  71.1 6.5 %collective-permute-start.27 = (bf16[128,512]{1,0:T(8,128)(2,1)S(1)}, bf16[128,512]{1,0:T(8,128)(2,1)S(1)}, u32[]{:S(2)}, u32[]{:S(2)}) collective-permute-start(bf16[128,512]{1,0:T(8,128)(2,1)S(1)} %get-tuple-element.121), channel_id=1, source_target_pairs={{0,1},{1,2},{2,3},{3,7},{7,6},{6,5},{5,4},{4,0},{8,9},{9,10},{10,1... | collective-permute-start | bytes 393224 | tf_op jit(solution)/shard_map/ppermute | solution.py:34
  74.2 5.0 %collective-permute-start.30 = (bf16[128,512]{1,0:T(8,128)(2,1)S(1)}, bf16[128,512]{1,0:T(8,128)(2,1)S(1)}, u32[]{:S(2)}, u32[]{:S(2)}) collective-permute-start(bf16[128,512]{1,0:T(8,128)(2,1)S(1)} %get-tuple-element.125), channel_id=1, source_target_pairs={{0,1},{1,2},{2,3},{3,7},{7,6},{6,5},{5,4},{4,0},{8,9},{9,10},{10,1... | collective-permute-start | bytes 393224 | tf_op jit(solution)/shard_map/ppermute | solution.py:34
  (12 other events, 74.8 us)

commit v5 on v4

--- a/solution.py
+++ b/solution.py
@@ -36,7 +36,10 @@
     def shifted(value, by):
         return lax.ppermute(value, "section", [(i, (i + by) % layers) for i in range(layers)])
 
-    return order, along, shifted
+    def swapped(value, bit):
+        return lax.ppermute(value, "section", [(i, i ^ bit) for i in range(layers)])
+
+    return order, along, shifted, swapped
 
 
 def call(kernel, name, outs, operands, specs, scratch=(), limit=12, flops=0, bytes_accessed=0):
@@ -143,44 +146,73 @@
         total[part] = before[part] + decoded(decoders.at[part], both)
 
 
-def decode_last_kernel(decoders, before, one, other, *outs, pieces):
-    (d0, w0), (d1, w1) = pieces
-    rows = outs[0].shape[0]
-    for i, out in enumerate(outs):
-        part = pl.ds(i * rows, rows)
-        both = [(d0, w0, one), (d1, w1, other)]
-        out[...] = (before[part] + decoded(decoders.at[part], both)).astype(out.dtype)
-
-
-def error_kernel(own, incoming, bias, target, returned, *refs, layers):
-    came, (error, beyond, *sent) = refs[: layers - 1], refs[layers - 1 :]
+def decode_last_kernel(decoders, before, one, other, total, sent, *, pieces, layers):
+    decode_kernel(decoders, before, one, other, total, pieces=pieces, layers=layers)
+    sent[...] = total[...].astype(BF16)
+
+
+def ahead_kernel(incoming, bias, target, returned, base, sent):
+    shift = upright(bias[...], incoming.shape[1])
+    base[...] = incoming[...] + shift - target[...].astype(F32)
+    sent[...] = jnp.where(lax.axis_index("section") < 2, returned[...], base[...].astype(BF16))
+
+
+def ahead_pair_kernel(base, returned, came, sent):
+    rows = base.shape[0]
+    even = lax.axis_index("section") % 2 == 0
+    sent[:rows] = jnp.where(even, came[...], base[...].astype(BF16))
+    sent[rows:] = jnp.where(even, returned[...], came[...])
+
+
+def chip_sum_kernel(total, mate, sums, sent, after):
     section = lax.axis_index("section")
-    shift = upright(bias[...], incoming.shape[1])
-    within = own[...] + (incoming[...] + shift) - target[...].astype(F32)
-    after = jnp.zeros_like(within)
-    for offset in range(1, layers):
-        part = came[offset - 1][...].astype(F32)
-        inside = section >= offset
-        within = within + jnp.where(inside, part, 0.0)
-        after = after + jnp.where(inside, 0.0, part)
-    mine = within.astype(BF16)
-    error[...] = mine
-    beyond[...] = after
-    passed = returned[...]
-    for offset in range(1, layers):
-        sent[offset - 1][...] = jnp.where(section >= offset, mine, passed)
+    rows = after.shape[0]
+    even = section % 2 == 0
+    for reach in range(5):
+        part = None
+        for offset, mine in ((reach, even), (reach - 1, jnp.logical_not(even))):
+            if 0 <= offset < 4:
+                cut = pl.ds(offset * rows, rows)
+                value = jnp.where(mine, total[cut], mate[cut].astype(F32))
+                part = value if part is None else part + value
+        sums[pl.ds(reach * rows, rows)] = part
+    for i in range(2):
+        lower, upper = sums[pl.ds((2 + i) * rows, rows)], sums[pl.ds(i * rows, rows)]
+        sent[pl.ds(i * rows, rows)] = jnp.where(section < 2, lower, upper).astype(BF16)
+    after[...] = jnp.where(even, sums[pl.ds(2 * rows, rows)], sums[pl.ds(3 * rows, rows)]).astype(BF16)
+
+
+def error_kernel(decoders, base, sums, across, first, pair, back, error, *outs, pieces):
+    section = lax.axis_index("section")
+    rows = base.shape[0]
+    low_chip = section < 2
+    recon = [sums[pl.ds(layer * rows, rows)] for layer in range(2)]
+    for i in range(2):
+        whole = jnp.where(low_chip, sums[pl.ds((2 + i) * rows, rows)], recon[i])
+        recon.append(whole + across[pl.ds(i * rows, rows)].astype(F32))
+    starts = [base[...], pair[:rows].astype(F32), first[...].astype(F32), pair[rows:].astype(F32)]
+    upstream = []
+    for offset, start in enumerate(starts):
+        part = jnp.zeros_like(start)
+        for layer in range(offset, 4):
+            part = jnp.where(section + offset == layer, recon[layer], part)
+        upstream.append((start + part).astype(BF16))
+    error[...] = upstream[0]
+    back[...] = jnp.concatenate(upstream, 0).T
+    for (distance, which), out in zip(pieces, outs):
+        out[...] = gradient(decoders, back, distance, which, out.shape[1]).astype(BF16)
+
+
+def outgoing_kernel(sums, came, beyond):
+    section = lax.axis_index("section")
+    rows = beyond.shape[0]
+    own = jnp.where(section % 2 == 0, sums[pl.ds(4 * rows, rows)], 0.0)
+    beyond[...] = own + jnp.where(section < 2, came[...].astype(F32), 0.0)
 
 
 def gradient(decoders, back, distance, which, half):
     columns = columns_of(decoders, distance, which, half, 2 * half)
     return jnp.dot(back[...], columns, preferred_element_type=F32)
-
-
-def gradient_first_kernel(decoders, *refs, layers, pieces):
-    parts, (back, *outs) = refs[:layers], refs[layers:]
-    back[...] = jnp.concatenate([part[...] for part in parts], 0).T
-    for (distance, which), out in zip(pieces, outs):
-        out[...] = gradient(decoders, back, distance, which, out.shape[1]).astype(BF16)
 
 
 def gradient_kernel(decoders, back, *outs, pieces):
@@ -209,7 +241,7 @@
 
 
 def tiled_local(cache, token_ids, enc_weight, enc_bias, dec_weight, dec_bias, incoming, target, returned):
-    order, along, shifted = ring_tools()
+    order, along, _, swapped = ring_tools()
     size = len(order)
     far = size // 2
     layers = lax.axis_size("section")
@@ -273,42 +305,63 @@
     outer = [along(halves[0], 1), along(halves[3], -1)]
     inner = [along(halves[1], 1), along(halves[2], -1)]
     total = decode("decode_1", total, ((size - 1, 0), (1, 0)), rise, fall)
+    base, sent = call(
+        ahead_kernel,
+        "ahead",
+        [((columns, tokens), F32), ((columns, tokens), BF16)],
+        (incoming[0].T, dec_bias, target[0].T, returned[0].T),
+        [VMEM] * 4,
+    )
+    first = swapped(sent, 2)
     for step in range(2, far):
         rise, fall, total = lax.optimization_barrier((*outer, total))
         near = rise, fall
         outer = [along(rise, 1), along(fall, -1)]
+        if step == 2:
+            first, *inner = lax.optimization_barrier((first, *inner))
         rise, fall, *near = lax.optimization_barrier((*inner, *near))
         if step < far - 1:
             inner = [along(rise, 1), along(fall, -1)]
         total = decode(f"decode_{step}_0", total, ((size - step, 0), (step, 1)), *near)
         pieces = ((size - step, 1), (step, 0))
         total = decode(f"decode_{step}_1", total, pieces, rise, fall)
-    own, *sent = call(
-        functools.partial(decode_last_kernel, pieces=((far, 0), (far, 1))),
+    (sent,) = call(
+        ahead_pair_kernel,
+        "ahead_pair",
+        [((2 * columns, tokens), BF16)],
+        (base, returned[0].T, first),
+        [VMEM] * 3,
+    )
+    pair = swapped(sent, 1)
+    *outer, pair = lax.optimization_barrier((*outer, pair))
+    total, sent = call(
+        functools.partial(decode_last_kernel, pieces=((far, 0), (far, 1)), layers=layers),
         "decode_last",
-        [((columns, tokens), F32)] + [((columns, tokens), BF16)] * (layers - 1),
+        [((outs_all, tokens), F32), ((outs_all, tokens), BF16)],
         (held, total, *outer),
         [VMEM] * 4,
         flops=2 * piece_flops,
     )
-    came = [shifted(value, offset) for offset, value in enumerate(sent, 1)]
-    error, beyond, *sent = call(
-        functools.partial(error_kernel, layers=layers),
-        "error",
-        [((columns, tokens), BF16), ((columns, tokens), F32)]
-        + [((columns, tokens), BF16)] * (layers - 1),
-        (own, incoming[0].T, dec_bias, target[0].T, returned[0].T, *came),
-        [VMEM] * (layers + 4),
-    )
-    came = [shifted(value, -offset) for offset, value in enumerate(sent, 1)]
+    sums, sent, after = call(
+        chip_sum_kernel,
+        "chip_sum",
+        [
+            (((layers + 1) * columns, tokens), F32),
+            ((2 * columns, tokens), BF16),
+            ((columns, tokens), BF16),
+        ],
+        (total, swapped(sent, 1)),
+        [VMEM] * 2,
+    )
+    across = swapped(sent, 2)
     piece = ((tokens, half), BF16)
     product = ((tokens, half), F32)
-    back, *outer = call(
-        functools.partial(gradient_first_kernel, layers=layers, pieces=((far, 0), (far, 1))),
-        "gradient_far",
-        [((tokens, outs_all), BF16), piece, piece],
-        (held, error, *came),
-        [VMEM] * (layers + 1),
+    back, error, *outer = call(
+        functools.partial(error_kernel, pieces=((far, 0), (far, 1))),
+        "error",
+        [((tokens, outs_all), BF16), ((columns, tokens), BF16), piece, piece],
+        (held, base, sums, across, first, pair),
+        [VMEM] * 6,
         flops=2 * piece_flops,
     )
 
@@ -331,8 +384,12 @@
     outer = [along(outer[0], 1), along(outer[1], -1)]
     inner = products("gradient_inner", piece, ((size - last, 0), (last, 1)), ())
     ready = inner
+    after, *_ = lax.optimization_barrier((after, *inner))
+    came = swapped(after, 2)
     for step in range(last, 0, -1):
         inner = [along(inner[0], -1), along(inner[1], 1)]
+        if step == last - 1:
+            back, came = lax.optimization_barrier((back, came))
         parts = products(f"outer_{step}", product, ((step, 0), (size - step, 1)), ready)
         ready = added(f"add_outer_{step}", parts, outer)
         outer = [along(ready[0], 1), along(ready[1], -1)]
@@ -340,6 +397,13 @@
             pieces = ((size - step + 1, 0), (step - 1, 1))
             parts = products(f"inner_{step - 1}", product, pieces, ready)
             inner = ready = added(f"add_inner_{step - 1}", parts, inner)
+    (beyond,) = call(
+        outgoing_kernel,
+        "outgoing",
+        [((columns, tokens), F32)],
+        (sums, came),
+        [VMEM] * 2,
+    )
     (part,) = call(
         gradient_own_kernel,
         "gradient_own",
@@ -360,7 +424,7 @@
 
 
 def plain_local(cache, token_ids, enc_weight, enc_bias, dec_weight, dec_bias, incoming, target, returned):
-    order, along, shifted = ring_tools()
+    order, along, shifted, _ = ring_tools()
     size = len(order)
     layers = lax.axis_size("section")
     section = lax.axis_index("section")
@@ -446,6 +510,7 @@
     whole_tiles = (
         size % 2 == 0
         and size >= 6
+        and lax.axis_size("section") == 4
         and mine % 256 == 0
         and width % 128 == 0
         and dec_weight.shape[2] % 16 == 0

time: 81.4 us -> 77.5 us (0.952)
  waiting for transfers between devices: 18.9 us -> 14.8 us
    ppermute x26, waiting for transfers between devices: 11.3 us -> 8.21 us  [along(): return lax.ppermute(value, GROUP, pairs)]
    ppermute x6 -> x5, waiting for transfers between devices: 7.56 us -> 6.59 us  [swapped(): return lax.ppermute(value, 'section', [(i, i ^ bit) for i in range(layers)])]
    pallas_call x23 -> x26, Pallas kernels: 25.7 us -> 26.2 us  [call(): pl.pallas_call(kernel, out_shape=[pltpu.VMEM(shape, dtype) for shape, dty...]
    ppermute x6 -> x5, starting transfers between devices: 5.69 us -> 5.13 us  [swapped(): return lax.ppermute(value, 'section', [(i, i ^ bit) for i in range(layers)])]
  transfers between devices with their start and end apart: 32 -> 31, of which waited for: 16 -> 13; matrix products, arithmetic and copies ran while one was open for 2% -> 2% of each run, Pallas kernels for 22% -> 23%
where the time goes in v5:
time: 77.5 us; the launch traced here: 77.3 us
  starting transfers between devices  33.1 us (43%)
  Pallas kernels  27.2 us (35%)
  waiting for transfers between devices  14.8 us (19%)
  local copies, waits for them, and re-layouts  1.32 us (2%)
  between operations  0.94 us (1%)
    ppermute x26, starting transfers between devices, along(): return lax.ppermute(value, GROUP, pairs)  28 us
    pallas_call x26, Pallas kernels, call(): pl.pallas_call(kernel, out_shape=[pltpu.VMEM(shape, dtype) for shape, dty...  26.2 us
    ppermute x26, waiting for transfers between devices, along(): return lax.ppermute(value, GROUP, pairs)  8.21 us
    ppermute x5, waiting for transfers between devices, swapped(): return lax.ppermute(value, 'section', [(i, i ^ bit) for i in range(layers)])  6.59 us
    ppermute x5, starting transfers between devices, swapped(): return lax.ppermute(value, 'section', [(i, i ^ bit) for i in range(layers)])  5.13 us
  transfers between devices with their start and end apart: 31, of which 13 were waited for; matrix products, arithmetic and copies ran while one was open for 2% of the time, Pallas kernels for 23%

profile of v5, /device:TPU:0, one launch (start us, length us, event | category | flops | bytes accessed | tf_op | source)
XLA Modules:
  0.0 77.3 jit_solution(17149084109945305716)
XLA Ops:
  0.7 6.4 %encode.1.latents = bf16[1024,128]{1,0:T(8,128)(2,1)S(1)} custom-call(s32[128]{0:T(128)} %ids.1, bf16[1,256,5376]{2,1,0:T(8,128)(2,1)} %cache.1, bf16[1,1024,5376]{2,1,0:T(8,128)(2,1)} %weight.1, f32[1,1024]{1,0:T(1,128)} %bias.2), custom_call_target="tpu_custom_call" | custom-call | flops 1761607680 | bytes 13762560 | tf_op jit(solution)/shard_map/encode/pallas_call | solution.py:46
  7.1 3.0 %collective-permute-start.1 = (bf16[1024,128]{1,0:T(8,128)(2,1)S(1)}, bf16[1024,128]{1,0:T(8,128)(2,1)S(1)}, u32[]{:S(2)}, u32[]{:S(2)}) collective-permute-start(bf16[1024,128]{1,0:T(8,128)(2,1)S(1)} %encode.1.latents), channel_id=1, source_target_pairs={{0,4},{1,0},{2,1},{3,2},{7,3},{6,7},{5,6},{4,5},{8,12},{9,8},{10,9... | collective-permute-start | bytes 786440 | tf_op jit(solution)/shard_map/ppermute | solution.py:34
  10.2 7.9 %load_decode.1 = (bf16[1344,8192]{1,0:T(8,128)(2,1)S(1)}, f32[1344,128]{1,0:T(8,128)S(1)}) custom-call(bf16[1344,8192]{1,0:T(8,128)(2,1)} %bitcast.23, bf16[1024,128]{1,0:T(8,128)(2,1)S(1)} %encode.1.latents), custom_call_target="tpu_custom_call" | custom-call | flops 352321536 | bytes 44040192 | tf_op jit(solution)/shard_map/load_decode/pallas_call | solution.py:46
  18.1 2.0 %collective-permute-start.2 = (bf16[512,128]{1,0:T(8,128)(2,1)S(1)}, bf16[512,128]{1,0:T(8,128)(2,1)S(1)}, u32[]{:S(2)}, u32[]{:S(2)}) collective-permute-start(bf16[512,128]{1,0:T(8,128)(2,1)S(1)} %get-tuple-element.78), channel_id=1, source_target_pairs={{0,1},{1,2},{2,3},{3,7},{7,6},{6,5},{5,4},{4,0},{8,9},{9,10},{10,1... | collective-permute-start | bytes 393224 | tf_op jit(solution)/shard_map/ppermute | solution.py:34
  20.2 2.0 %collective-permute-start.7 = (bf16[512,128]{1,0:T(8,128)(2,1)S(1)}, bf16[512,128]{1,0:T(8,128)(2,1)S(1)}, u32[]{:S(2)}, u32[]{:S(2)}) collective-permute-start(bf16[512,128]{1,0:T(8,128)(2,1)S(1)} %get-tuple-element.85), channel_id=1, source_target_pairs={{0,1},{1,2},{2,3},{3,7},{7,6},{6,5},{5,4},{4,0},{8,9},{9,10},{10,1... | collective-permute-start | bytes 393224 | tf_op jit(solution)/shard_map/ppermute | solution.py:34
  22.4 2.0 %collective-permute-start.6 = (bf16[336,128]{1,0:T(8,128)(2,1)S(1)}, bf16[336,128]{1,0:T(8,128)(2,1)S(1)}, u32[]{:S(2)}, u32[]{:S(2)}) collective-permute-start(bf16[336,128]{1,0:T(8,128)(2,1)S(1)} %get-tuple-element.84), channel_id=1, source_target_pairs={{0,16},{8,24},{16,0},{24,8},{1,17},{9,25},{17,1},{25,9},{2,18},{10... | collective-permute-start | bytes 258056 | tf_op jit(solution)/shard_map/ppermute | solution.py:40
  24.4 1.6 %decode_1.1.before = f32[1344,128]{1,0:T(8,128)S(1)} custom-call(bf16[1344,8192]{1,0:T(8,128)(2,1)S(1)} %get-tuple-element.73.decoders, f32[1344,128]{1,0:T(8,128)S(1)} %get-tuple-element.80.before, bf16[1024,128]{1,0:T(8,128)(2,1)S(1)} %collective-permute-done.rise.one, bf16[1024,128]{1,0:T(8,128)(2,1)S(1)} %collective-permute-done.1.fall.other), custom_call_target="tpu_custom_call" | custom-call | flops 352321536 | tf_op jit(solution)/shard_map/decode_1/pallas_call | solution.py:46
  26.0 1.6 %collective-permute-start.4 = (bf16[512,128]{1,0:T(8,128)(2,1)S(1)}, bf16[512,128]{1,0:T(8,128)(2,1)S(1)}, u32[]{:S(2)}, u32[]{:S(2)}) collective-permute-start(bf16[512,128]{1,0:T(8,128)(2,1)S(1)} %collective-permute-done.2.one), channel_id=1, source_target_pairs={{0,1},{1,2},{2,3},{3,7},{7,6},{6,5},{5,4},{4,0},{8,9},{9,10},{10,1... | collective-permute-start | bytes 393224 | tf_op jit(solution)/shard_map/ppermute | solution.py:34
  28.1 1.6 %collective-permute-start.9 = (bf16[512,128]{1,0:T(8,128)(2,1)S(1)}, bf16[512,128]{1,0:T(8,128)(2,1)S(1)}, u32[]{:S(2)}, u32[]{:S(2)}) collective-permute-start(bf16[512,128]{1,0:T(8,128)(2,1)S(1)} %collective-permute-done.7.one), channel_id=1, source_target_pairs={{0,1},{1,2},{2,3},{3,7},{7,6},{6,5},{5,4},{4,0},{8,9},{9,10},{10,1... | collective-permute-start | bytes 393224 | tf_op jit(solution)/shard_map/ppermute | solution.py:34
  32.6 1.6 %collective-permute-start.11 = (bf16[512,128]{1,0:T(8,128)(2,1)S(1)}, bf16[512,128]{1,0:T(8,128)(2,1)S(1)}, u32[]{:S(2)}, u32[]{:S(2)}) collective-permute-start(bf16[512,128]{1,0:T(8,128)(2,1)S(1)} %collective-permute-done.4.one), channel_id=1, source_target_pairs={{0,1},{1,2},{2,3},{3,7},{7,6},{6,5},{5,4},{4,0},{8,9},{9,10},{10,1... | collective-permute-start | bytes 393224 | tf_op jit(solution)/shard_map/ppermute | solution.py:34
  36.5 1.6 %collective-permute-done.11.one = bf16[512,128]{1,0:T(8,128)(2,1)S(1)} collective-permute-done((bf16[512,128]{1,0:T(8,128)(2,1)S(1)}, bf16[512,128]{1,0:T(8,128)(2,1)S(1)}, u32[]{:S(2)}, u32[]{:S(2)}) %collective-permute-start.11) | collective-permute-done | bytes 131104 | tf_op jit(solution)/shard_map/ppermute | solution.py:34
  38.1 1.3 %collective-permute-done.12.other = bf16[512,128]{1,0:T(8,128)(2,1)S(1)} collective-permute-done((bf16[512,128]{1,0:T(8,128)(2,1)S(1)}, bf16[512,128]{1,0:T(8,128)(2,1)S(1)}, u32[]{:S(2)}, u32[]{:S(2)}) %collective-permute-start.12) | collective-permute-done | bytes 131104 | tf_op jit(solution)/shard_map/ppermute | solution.py:34
  40.4 1.6 %collective-permute-done.14.mate = bf16[1344,128]{1,0:T(8,128)(2,1)S(1)} collective-permute-done((bf16[1344,128]{1,0:T(8,128)(2,1)S(1)}, bf16[1344,128]{1,0:T(8,128)(2,1)S(1)}, u32[]{:S(2)}, u32[]{:S(2)}) %collective-permute-start.14) | collective-permute-done | bytes 344096 | tf_op jit(solution)/shard_map/ppermute | solution.py:40
  42.3 1.5 %collective-permute-start.15 = (bf16[672,128]{1,0:T(8,128)(2,1)S(1)}, bf16[672,128]{1,0:T(8,128)(2,1)S(1)}, u32[]{:S(2)}, u32[]{:S(2)}) collective-permute-start(bf16[672,128]{1,0:T(8,128)(2,1)S(1)} %get-tuple-element.106), channel_id=1, source_target_pairs={{0,16},{8,24},{16,0},{24,8},{1,17},{9,25},{17,1},{25,9},{2,18},{10... | collective-permute-start | bytes 516104 | tf_op jit(solution)/shard_map/ppermute | solution.py:40
  43.8 4.9 %collective-permute-done.15.across = bf16[672,128]{1,0:T(8,128)(2,1)S(1)} collective-permute-done((bf16[672,128]{1,0:T(8,128)(2,1)S(1)}, bf16[672,128]{1,0:T(8,128)(2,1)S(1)}, u32[]{:S(2)}, u32[]{:S(2)}) %collective-permute-start.15) | collective-permute-done | bytes 172064 | tf_op jit(solution)/shard_map/ppermute | solution.py:40
  49.5 1.6 %collective-permute-start.16 = (bf16[128,512]{1,0:T(8,128)(2,1)S(1)}, bf16[128,512]{1,0:T(8,128)(2,1)S(1)}, u32[]{:S(2)}, u32[]{:S(2)}) collective-permute-start(bf16[128,512]{1,0:T(8,128)(2,1)S(1)} %get-tuple-element.115), channel_id=1, source_target_pairs={{0,1},{1,2},{2,3},{3,7},{7,6},{6,5},{5,4},{4,0},{8,9},{9,10},{10,1... | collective-permute-start | bytes 393224 | tf_op jit(solution)/shard_map/ppermute | solution.py:34
  52.7 1.6 %collective-permute-start.20 = (bf16[128,512]{1,0:T(8,128)(2,1)S(1)}, bf16[128,512]{1,0:T(8,128)(2,1)S(1)}, u32[]{:S(2)}, u32[]{:S(2)}) collective-permute-start(bf16[128,512]{1,0:T(8,128)(2,1)S(1)} %get-tuple-element.111), channel_id=1, source_target_pairs={{0,1},{1,2},{2,3},{3,7},{7,6},{6,5},{5,4},{4,0},{8,9},{9,10},{10,1... | collective-permute-start | bytes 393224 | tf_op jit(solution)/shard_map/ppermute | solution.py:34
  54.2 1.5 %collective-permute-start.18 = (bf16[336,128]{1,0:T(8,128)(2,1)S(1)}, bf16[336,128]{1,0:T(8,128)(2,1)S(1)}, u32[]{:S(2)}, u32[]{:S(2)}) collective-permute-start(bf16[336,128]{1,0:T(8,128)(2,1)S(1)} %get-tuple-element.121), channel_id=1, source_target_pairs={{0,16},{8,24},{16,0},{24,8},{1,17},{9,25},{17,1},{25,9},{2,18},{10... | collective-permute-start | bytes 258056 | tf_op jit(solution)/shard_map/ppermute | solution.py:40
  57.0 1.6 %collective-permute-start.21 = (bf16[128,512]{1,0:T(8,128)(2,1)S(1)}, bf16[128,512]{1,0:T(8,128)(2,1)S(1)}, u32[]{:S(2)}, u32[]{:S(2)}) collective-permute-start(bf16[128,512]{1,0:T(8,128)(2,1)S(1)} %get-tuple-element.117), channel_id=1, source_target_pairs={{0,1},{1,2},{2,3},{3,7},{7,6},{6,5},{5,4},{4,0},{8,9},{9,10},{10,1... | collective-permute-start | bytes 393224 | tf_op jit(solution)/shard_map/ppermute | solution.py:34
  60.3 1.5 %collective-permute-start.24 = (bf16[128,512]{1,0:T(8,128)(2,1)S(1)}, bf16[128,512]{1,0:T(8,128)(2,1)S(1)}, u32[]{:S(2)}, u32[]{:S(2)}) collective-permute-start(bf16[128,512]{1,0:T(8,128)(2,1)S(1)} %get-tuple-element.127), channel_id=1, source_target_pairs={{0,1},{1,2},{2,3},{3,7},{7,6},{6,5},{5,4},{4,0},{8,9},{9,10},{10,1... | collective-permute-start | bytes 393224 | tf_op jit(solution)/shard_map/ppermute | solution.py:34
  62.5 1.1 %collective-permute-done.22.came_other = bf16[128,512]{1,0:T(8,128)(2,1)S(1)} collective-permute-done((bf16[128,512]{1,0:T(8,128)(2,1)S(1)}, bf16[128,512]{1,0:T(8,128)(2,1)S(1)}, u32[]{:S(2)}, u32[]{:S(2)}) %collective-permute-start.22) | collective-permute-done | bytes 131104 | tf_op jit(solution)/shard_map/ppermute | solution.py:34
  63.6 1.5 %collective-permute-start.27 = (bf16[128,512]{1,0:T(8,128)(2,1)S(1)}, bf16[128,512]{1,0:T(8,128)(2,1)S(1)}, u32[]{:S(2)}, u32[]{:S(2)}) collective-permute-start(bf16[128,512]{1,0:T(8,128)(2,1)S(1)} %get-tuple-element.131), channel_id=1, source_target_pairs={{0,1},{1,2},{2,3},{3,7},{7,6},{6,5},{5,4},{4,0},{8,9},{9,10},{10,1... | collective-permute-start | bytes 393224 | tf_op jit(solution)/shard_map/ppermute | solution.py:34
  66.9 1.6 %collective-permute-start.26 = (bf16[128,512]{1,0:T(8,128)(2,1)S(1)}, bf16[128,512]{1,0:T(8,128)(2,1)S(1)}, u32[]{:S(2)}, u32[]{:S(2)}) collective-permute-start(bf16[128,512]{1,0:T(8,128)(2,1)S(1)} %get-tuple-element.137), channel_id=1, source_target_pairs={{0,1},{1,2},{2,3},{3,7},{7,6},{6,5},{5,4},{4,0},{8,9},{9,10},{10,1... | collective-permute-start | bytes 393224 | tf_op jit(solution)/shard_map/ppermute | solution.py:34
  75.2 1.2 %collective-permute-done.30.high = bf16[128,512]{1,0:T(8,128)(2,1)S(1)} collective-permute-done((bf16[128,512]{1,0:T(8,128)(2,1)S(1)}, bf16[128,512]{1,0:T(8,128)(2,1)S(1)}, u32[]{:S(2)}, u32[]{:S(2)}) %collective-permute-start.30) | collective-permute-done | bytes 131104 | tf_op jit(solution)/shard_map/ppermute | solution.py:34
  (75 shorter events, 22.5 us)
Async XLA Ops:
  7.1 11.0 %collective-permute-start.1 = (bf16[1024,128]{1,0:T(8,128)(2,1)S(1)}, bf16[1024,128]{1,0:T(8,128)(2,1)S(1)}, u32[]{:S(2)}, u32[]{:S(2)}) collective-permute-start(bf16[1024,128]{1,0:T(8,128)(2,1)S(1)} %encode.1.latents), channel_id=1, source_target_pairs={{0,4},{1,0},{2,1},{3,2},{7,3},{6,7},{5,6},{4,5},{8,12},{9,8},{10,9... | collective-permute-start | bytes 786440 | tf_op jit(solution)/shard_map/ppermute | solution.py:34
  10.1 8.0 %collective-permute-start = (bf16[1024,128]{1,0:T(8,128)(2,1)S(1)}, bf16[1024,128]{1,0:T(8,128)(2,1)S(1)}, u32[]{:S(2)}, u32[]{:S(2)}) collective-permute-start(bf16[1024,128]{1,0:T(8,128)(2,1)S(1)} %encode.1.latents), channel_id=1, source_target_pairs={{0,1},{1,2},{2,3},{3,7},{7,6},{6,5},{5,4},{4,0},{8,9},{9,10},{10,1... | collective-permute-start | bytes 786440 | tf_op jit(solution)/shard_map/ppermute | solution.py:34
  18.1 7.9 %collective-permute-start.2 = (bf16[512,128]{1,0:T(8,128)(2,1)S(1)}, bf16[512,128]{1,0:T(8,128)(2,1)S(1)}, u32[]{:S(2)}, u32[]{:S(2)}) collective-permute-start(bf16[512,128]{1,0:T(8,128)(2,1)S(1)} %get-tuple-element.78), channel_id=1, source_target_pairs={{0,1},{1,2},{2,3},{3,7},{7,6},{6,5},{5,4},{4,0},{8,9},{9,10},{10,1... | collective-permute-start | bytes 393224 | tf_op jit(solution)/shard_map/ppermute | solution.py:34
  20.1 5.9 %collective-permute-start.3 = (bf16[512,128]{1,0:T(8,128)(2,1)S(1)}, bf16[512,128]{1,0:T(8,128)(2,1)S(1)}, u32[]{:S(2)}, u32[]{:S(2)}) collective-permute-start(bf16[512,128]{1,0:T(8,128)(2,1)S(1)} %get-tuple-element.79), channel_id=1, source_target_pairs={{0,4},{1,0},{2,1},{3,2},{7,3},{6,7},{5,6},{4,5},{8,12},{9,8},{10,9... | collective-permute-start | bytes 393224 | tf_op jit(solution)/shard_map/ppermute | solution.py:34
  20.2 7.9 %collective-permute-start.7 = (bf16[512,128]{1,0:T(8,128)(2,1)S(1)}, bf16[512,128]{1,0:T(8,128)(2,1)S(1)}, u32[]{:S(2)}, u32[]{:S(2)}) collective-permute-start(bf16[512,128]{1,0:T(8,128)(2,1)S(1)} %get-tuple-element.85), channel_id=1, source_target_pairs={{0,1},{1,2},{2,3},{3,7},{7,6},{6,5},{5,4},{4,0},{8,9},{9,10},{10,1... | collective-permute-start | bytes 393224 | tf_op jit(solution)/shard_map/ppermute | solution.py:34
  22.2 5.9 %collective-permute-start.8 = (bf16[512,128]{1,0:T(8,128)(2,1)S(1)}, bf16[512,128]{1,0:T(8,128)(2,1)S(1)}, u32[]{:S(2)}, u32[]{:S(2)}) collective-permute-start(bf16[512,128]{1,0:T(8,128)(2,1)S(1)} %get-tuple-element.86), channel_id=1, source_target_pairs={{0,4},{1,0},{2,1},{3,2},{7,3},{6,7},{5,6},{4,5},{8,12},{9,8},{10,9... | collective-permute-start | bytes 393224 | tf_op jit(solution)/shard_map/ppermute | solution.py:34
  22.4 5.7 %collective-permute-start.6 = (bf16[336,128]{1,0:T(8,128)(2,1)S(1)}, bf16[336,128]{1,0:T(8,128)(2,1)S(1)}, u32[]{:S(2)}, u32[]{:S(2)}) collective-permute-start(bf16[336,128]{1,0:T(8,128)(2,1)S(1)} %get-tuple-element.84), channel_id=1, source_target_pairs={{0,16},{8,24},{16,0},{24,8},{1,17},{9,25},{17,1},{25,9},{2,18},{10... | collective-permute-start | bytes 258056 | tf_op jit(solution)/shard_map/ppermute | solution.py:40
  26.0 6.1 %collective-permute-start.4 = (bf16[512,128]{1,0:T(8,128)(2,1)S(1)}, bf16[512,128]{1,0:T(8,128)(2,1)S(1)}, u32[]{:S(2)}, u32[]{:S(2)}) collective-permute-start(bf16[512,128]{1,0:T(8,128)(2,1)S(1)} %collective-permute-done.2.one), channel_id=1, source_target_pairs={{0,1},{1,2},{2,3},{3,7},{7,6},{6,5},{5,4},{4,0},{8,9},{9,10},{10,1... | collective-permute-start | bytes 393224 | tf_op jit(solution)/shard_map/ppermute | solution.py:34
  28.1 6.5 %collective-permute-start.9 = (bf16[512,128]{1,0:T(8,128)(2,1)S(1)}, bf16[512,128]{1,0:T(8,128)(2,1)S(1)}, u32[]{:S(2)}, u32[]{:S(2)}) collective-permute-start(bf16[512,128]{1,0:T(8,128)(2,1)S(1)} %collective-permute-done.7.one), channel_id=1, source_target_pairs={{0,1},{1,2},{2,3},{3,7},{7,6},{6,5},{5,4},{4,0},{8,9},{9,10},{10,1... | collective-permute-start | bytes 393224 | tf_op jit(solution)/shard_map/ppermute | solution.py:34
  30.2 6.3 %collective-permute-start.13 = (bf16[672,128]{1,0:T(8,128)(2,1)S(1)}, bf16[672,128]{1,0:T(8,128)(2,1)S(1)}, u32[]{:S(2)}, u32[]{:S(2)}) collective-permute-start(bf16[672,128]{1,0:T(8,128)(2,1)S(1)} %ahead_pair.1), channel_id=1, source_target_pairs={{0,8},{8,0},{16,24},{24,16},{1,9},{9,1},{17,25},{25,17},{2,10},{10... | collective-permute-start | bytes 516104 | tf_op jit(solution)/shard_map/ppermute | solution.py:40
  32.6 5.5 %collective-permute-start.11 = (bf16[512,128]{1,0:T(8,128)(2,1)S(1)}, bf16[512,128]{1,0:T(8,128)(2,1)S(1)}, u32[]{:S(2)}, u32[]{:S(2)}) collective-permute-start(bf16[512,128]{1,0:T(8,128)(2,1)S(1)} %collective-permute-done.4.one), channel_id=1, source_target_pairs={{0,1},{1,2},{2,3},{3,7},{7,6},{6,5},{5,4},{4,0},{8,9},{9,10},{10,1... | collective-permute-start | bytes 393224 | tf_op jit(solution)/shard_map/ppermute | solution.py:34
  34.2 5.2 %collective-permute-start.12 = (bf16[512,128]{1,0:T(8,128)(2,1)S(1)}, bf16[512,128]{1,0:T(8,128)(2,1)S(1)}, u32[]{:S(2)}, u32[]{:S(2)}) collective-permute-start(bf16[512,128]{1,0:T(8,128)(2,1)S(1)} %collective-permute-done.5.other), channel_id=1, source_target_pairs={{0,4},{1,0},{2,1},{3,2},{7,3},{6,7},{5,6},{4,5},{8,12},{9,8},{10,9... | collective-permute-start | bytes 393224 | tf_op jit(solution)/shard_map/ppermute | solution.py:34
  42.3 6.5 %collective-permute-start.15 = (bf16[672,128]{1,0:T(8,128)(2,1)S(1)}, bf16[672,128]{1,0:T(8,128)(2,1)S(1)}, u32[]{:S(2)}, u32[]{:S(2)}) collective-permute-start(bf16[672,128]{1,0:T(8,128)(2,1)S(1)} %get-tuple-element.106), channel_id=1, source_target_pairs={{0,16},{8,24},{16,0},{24,8},{1,17},{9,25},{17,1},{25,9},{2,18},{10... | collective-permute-start | bytes 516104 | tf_op jit(solution)/shard_map/ppermute | solution.py:40
  49.5 6.9 %collective-permute-start.16 = (bf16[128,512]{1,0:T(8,128)(2,1)S(1)}, bf16[128,512]{1,0:T(8,128)(2,1)S(1)}, u32[]{:S(2)}, u32[]{:S(2)}) collective-permute-start(bf16[128,512]{1,0:T(8,128)(2,1)S(1)} %get-tuple-element.115), channel_id=1, source_target_pairs={{0,1},{1,2},{2,3},{3,7},{7,6},{6,5},{5,4},{4,0},{8,9},{9,10},{10,1... | collective-permute-start | bytes 393224 | tf_op jit(solution)/shard_map/ppermute | solution.py:34
  51.1 5.8 %collective-permute-start.17 = (bf16[128,512]{1,0:T(8,128)(2,1)S(1)}, bf16[128,512]{1,0:T(8,128)(2,1)S(1)}, u32[]{:S(2)}, u32[]{:S(2)}) collective-permute-start(bf16[128,512]{1,0:T(8,128)(2,1)S(1)} %get-tuple-element.116), channel_id=1, source_target_pairs={{0,4},{1,0},{2,1},{3,2},{7,3},{6,7},{5,6},{4,5},{8,12},{9,8},{10,9... | collective-permute-start | bytes 393224 | tf_op jit(solution)/shard_map/ppermute | solution.py:34
  52.2 7.5 %collective-permute-start.19 = (bf16[128,512]{1,0:T(8,128)(2,1)S(1)}, bf16[128,512]{1,0:T(8,128)(2,1)S(1)}, u32[]{:S(2)}, u32[]{:S(2)}) collective-permute-start(bf16[128,512]{1,0:T(8,128)(2,1)S(1)} %get-tuple-element.110), channel_id=1, source_target_pairs={{0,4},{1,0},{2,1},{3,2},{7,3},{6,7},{5,6},{4,5},{8,12},{9,8},{10,9... | collective-permute-start | bytes 393224 | tf_op jit(solution)/shard_map/ppermute | solution.py:34
  52.7 7.0 %collective-permute-start.20 = (bf16[128,512]{1,0:T(8,128)(2,1)S(1)}, bf16[128,512]{1,0:T(8,128)(2,1)S(1)}, u32[]{:S(2)}, u32[]{:S(2)}) collective-permute-start(bf16[128,512]{1,0:T(8,128)(2,1)S(1)} %get-tuple-element.111), channel_id=1, source_target_pairs={{0,1},{1,2},{2,3},{3,7},{7,6},{6,5},{5,4},{4,0},{8,9},{9,10},{10,1... | collective-permute-start | bytes 393224 | tf_op jit(solution)/shard_map/ppermute | solution.py:34
  57.0 5.5 %collective-permute-start.21 = (bf16[128,512]{1,0:T(8,128)(2,1)S(1)}, bf16[128,512]{1,0:T(8,128)(2,1)S(1)}, u32[]{:S(2)}, u32[]{:S(2)}) collective-permute-start(bf16[128,512]{1,0:T(8,128)(2,1)S(1)} %get-tuple-element.117), channel_id=1, source_target_pairs={{0,1},{1,2},{2,3},{3,7},{7,6},{6,5},{5,4},{4,0},{8,9},{9,10},{10,1... | collective-permute-start | bytes 393224 | tf_op jit(solution)/shard_map/ppermute | solution.py:34
  59.8 6.6 %collective-permute-start.23 = (bf16[128,512]{1,0:T(8,128)(2,1)S(1)}, bf16[128,512]{1,0:T(8,128)(2,1)S(1)}, u32[]{:S(2)}, u32[]{:S(2)}) collective-permute-start(bf16[128,512]{1,0:T(8,128)(2,1)S(1)} %get-tuple-element.126), channel_id=1, source_target_pairs={{0,4},{1,0},{2,1},{3,2},{7,3},{6,7},{5,6},{4,5},{8,12},{9,8},{10,9... | collective-permute-start | bytes 393224 | tf_op jit(solution)/shard_map/ppermute | solution.py:34
  60.3 6.1 %collective-permute-start.24 = (bf16[128,512]{1,0:T(8,128)(2,1)S(1)}, bf16[128,512]{1,0:T(8,128)(2,1)S(1)}, u32[]{:S(2)}, u32[]{:S(2)}) collective-permute-start(bf16[128,512]{1,0:T(8,128)(2,1)S(1)} %get-tuple-element.127), channel_id=1, source_target_pairs={{0,1},{1,2},{2,3},{3,7},{7,6},{6,5},{5,4},{4,0},{8,9},{9,10},{10,1... | collective-permute-start | bytes 393224 | tf_op jit(solution)/shard_map/ppermute | solution.py:34
  63.6 5.6 %collective-permute-start.27 = (bf16[128,512]{1,0:T(8,128)(2,1)S(1)}, bf16[128,512]{1,0:T(8,128)(2,1)S(1)}, u32[]{:S(2)}, u32[]{:S(2)}) collective-permute-start(bf16[128,512]{1,0:T(8,128)(2,1)S(1)} %get-tuple-element.131), channel_id=1, source_target_pairs={{0,1},{1,2},{2,3},{3,7},{7,6},{6,5},{5,4},{4,0},{8,9},{9,10},{10,1... | collective-permute-start | bytes 393224 | tf_op jit(solution)/shard_map/ppermute | solution.py:34
  66.4 7.2 %collective-permute-start.25 = (bf16[128,512]{1,0:T(8,128)(2,1)S(1)}, bf16[128,512]{1,0:T(8,128)(2,1)S(1)}, u32[]{:S(2)}, u32[]{:S(2)}) collective-permute-start(bf16[128,512]{1,0:T(8,128)(2,1)S(1)} %get-tuple-element.136), channel_id=1, source_target_pairs={{0,4},{1,0},{2,1},{3,2},{7,3},{6,7},{5,6},{4,5},{8,12},{9,8},{10,9... | collective-permute-start | bytes 393224 | tf_op jit(solution)/shard_map/ppermute | solution.py:34
  66.9 6.7 %collective-permute-start.26 = (bf16[128,512]{1,0:T(8,128)(2,1)S(1)}, bf16[128,512]{1,0:T(8,128)(2,1)S(1)}, u32[]{:S(2)}, u32[]{:S(2)}) collective-permute-start(bf16[128,512]{1,0:T(8,128)(2,1)S(1)} %get-tuple-element.137), channel_id=1, source_target_pairs={{0,1},{1,2},{2,3},{3,7},{7,6},{6,5},{5,4},{4,0},{8,9},{9,10},{10,1... | collective-permute-start | bytes 393224 | tf_op jit(solution)/shard_map/ppermute | solution.py:34
  71.2 5.2 %collective-permute-start.30 = (bf16[128,512]{1,0:T(8,128)(2,1)S(1)}, bf16[128,512]{1,0:T(8,128)(2,1)S(1)}, u32[]{:S(2)}, u32[]{:S(2)}) collective-permute-start(bf16[128,512]{1,0:T(8,128)(2,1)S(1)} %get-tuple-element.142), channel_id=1, source_target_pairs={{0,4},{1,0},{2,1},{3,2},{7,3},{6,7},{5,6},{4,5},{8,12},{9,8},{10,9... | collective-permute-start | bytes 393224 | tf_op jit(solution)/shard_map/ppermute | solution.py:34
  (11 other events, 117.8 us)

commit v6 on v5

--- a/solution.py
+++ b/solution.py
@@ -303,8 +303,9 @@
         split_kernel, "split", [((half, tokens), BF16)] * 4, (rise, fall), [VMEM] * 2
     )
     outer = [along(halves[0], 1), along(halves[3], -1)]
-    inner = [along(halves[1], 1), along(halves[2], -1)]
     total = decode("decode_1", total, ((size - 1, 0), (1, 0)), rise, fall)
+    one, other, total = lax.optimization_barrier((halves[1], halves[2], total))
+    inner = [along(one, 1), along(other, -1)]
     base, sent = call(
         ahead_kernel,
         "ahead",
@@ -312,12 +313,14 @@
         (incoming[0].T, dec_bias, target[0].T, returned[0].T),
         [VMEM] * 4,
     )
-    first = swapped(sent, 2)
     for step in range(2, far):
-        rise, fall, total = lax.optimization_barrier((*outer, total))
+        tied = (sent, total) if step == 2 else ()
+        rise, fall, *tied = lax.optimization_barrier((*outer, *tied))
         near = rise, fall
         outer = [along(rise, 1), along(fall, -1)]
         if step == 2:
+            sent, total = tied
+            first = swapped(sent, 2)
             first, *inner = lax.optimization_barrier((first, *inner))
         rise, fall, *near = lax.optimization_barrier((*inner, *near))
         if step < far - 1:

time: 77.5 us -> 77.2 us (level)
  transfers between devices with their start and end apart: 31 -> 31, of which waited for: 13 -> 15; matrix products, arithmetic and copies ran while one was open for 2% -> 2% of each run, Pallas kernels for 23% -> 23%
where the time goes in v6:
time: 77.2 us; the launch traced here: 77 us
  starting transfers between devices  32.7 us (42%)
  Pallas kernels  27.1 us (35%)
  waiting for transfers between devices  15 us (19%)
  local copies, waits for them, and re-layouts  1.32 us (2%)
  between operations  0.92 us (1%)
    ppermute x26, starting transfers between devices, along(): return lax.ppermute(value, GROUP, pairs)  27.9 us
    pallas_call x26, Pallas kernels, call(): pl.pallas_call(kernel, out_shape=[pltpu.VMEM(shape, dtype) for shape, dty...  26.2 us
    ppermute x26, waiting for transfers between devices, along(): return lax.ppermute(value, GROUP, pairs)  7.9 us
    ppermute x5, waiting for transfers between devices, swapped(): return lax.ppermute(value, 'section', [(i, i ^ bit) for i in range(layers)])  7.05 us
    ppermute x5, starting transfers between devices, swapped(): return lax.ppermute(value, 'section', [(i, i ^ bit) for i in range(layers)])  4.78 us
  transfers between devices with their start and end apart: 31, of which 15 were waited for; matrix products, arithmetic and copies ran while one was open for 2% of the time, Pallas kernels for 23%

profile of v6, /device:TPU:0, one launch (start us, length us, event | category | flops | bytes accessed | tf_op | source)
XLA Modules:
  0.0 77.0 jit_solution(16672323552146290681)
XLA Ops:
  0.6 6.3 %encode.1.latents = bf16[1024,128]{1,0:T(8,128)(2,1)S(1)} custom-call(s32[128]{0:T(128)} %ids.1, bf16[1,256,5376]{2,1,0:T(8,128)(2,1)} %cache.1, bf16[1,1024,5376]{2,1,0:T(8,128)(2,1)} %weight.1, f32[1,1024]{1,0:T(1,128)} %bias.2), custom_call_target="tpu_custom_call" | custom-call | flops 1761607680 | bytes 13762560 | tf_op jit(solution)/shard_map/encode/pallas_call | solution.py:46
  7.0 3.0 %collective-permute-start.1 = (bf16[1024,128]{1,0:T(8,128)(2,1)S(1)}, bf16[1024,128]{1,0:T(8,128)(2,1)S(1)}, u32[]{:S(2)}, u32[]{:S(2)}) collective-permute-start(bf16[1024,128]{1,0:T(8,128)(2,1)S(1)} %encode.1.latents), channel_id=1, source_target_pairs={{0,4},{1,0},{2,1},{3,2},{7,3},{6,7},{5,6},{4,5},{8,12},{9,8},{10,9... | collective-permute-start | bytes 786440 | tf_op jit(solution)/shard_map/ppermute | solution.py:34
  10.1 7.9 %load_decode.1 = (bf16[1344,8192]{1,0:T(8,128)(2,1)S(1)}, f32[1344,128]{1,0:T(8,128)S(1)}) custom-call(bf16[1344,8192]{1,0:T(8,128)(2,1)} %bitcast.23, bf16[1024,128]{1,0:T(8,128)(2,1)S(1)} %encode.1.latents), custom_call_target="tpu_custom_call" | custom-call | flops 352321536 | bytes 44040192 | tf_op jit(solution)/shard_map/load_decode/pallas_call | solution.py:46
  18.1 2.0 %collective-permute-start.2 = (bf16[512,128]{1,0:T(8,128)(2,1)S(1)}, bf16[512,128]{1,0:T(8,128)(2,1)S(1)}, u32[]{:S(2)}, u32[]{:S(2)}) collective-permute-start(bf16[512,128]{1,0:T(8,128)(2,1)S(1)} %get-tuple-element.81), channel_id=1, source_target_pairs={{0,1},{1,2},{2,3},{3,7},{7,6},{6,5},{5,4},{4,0},{8,9},{9,10},{10,1... | collective-permute-start | bytes 393224 | tf_op jit(solution)/shard_map/ppermute | solution.py:34
  20.2 1.6 %decode_1.1.before = f32[1344,128]{1,0:T(8,128)S(1)} custom-call(bf16[1344,8192]{1,0:T(8,128)(2,1)S(1)} %get-tuple-element.76.decoders, f32[1344,128]{1,0:T(8,128)S(1)} %get-tuple-element.86.before, bf16[1024,128]{1,0:T(8,128)(2,1)S(1)} %collective-permute-done.rise.one, bf16[1024,128]{1,0:T(8,128)(2,1)S(1)} %collective-permute-done.1.fall.other), custom_call_target="tpu_custom_call" | custom-call | flops 352321536 | tf_op jit(solution)/shard_map/decode_1/pallas_call | solution.py:46
  21.8 2.0 %collective-permute-start.5 = (bf16[512,128]{1,0:T(8,128)(2,1)S(1)}, bf16[512,128]{1,0:T(8,128)(2,1)S(1)}, u32[]{:S(2)}, u32[]{:S(2)}) collective-permute-start(bf16[512,128]{1,0:T(8,128)(2,1)S(1)} %get-tuple-element.90), channel_id=1, source_target_pairs={{0,1},{1,2},{2,3},{3,7},{7,6},{6,5},{5,4},{4,0},{8,9},{9,10},{10,1... | collective-permute-start | bytes 393224 | tf_op jit(solution)/shard_map/ppermute | solution.py:34
  24.0 1.2 %collective-permute-done.3.other = bf16[512,128]{1,0:T(8,128)(2,1)S(1)} collective-permute-done((bf16[512,128]{1,0:T(8,128)(2,1)S(1)}, bf16[512,128]{1,0:T(8,128)(2,1)S(1)}, u32[]{:S(2)}, u32[]{:S(2)}) %collective-permute-start.3) | collective-permute-done | bytes 131104 | tf_op jit(solution)/shard_map/ppermute | solution.py:34
  25.3 1.5 %collective-permute-start.4 = (bf16[336,128]{1,0:T(8,128)(2,1)S(1)}, bf16[336,128]{1,0:T(8,128)(2,1)S(1)}, u32[]{:S(2)}, u32[]{:S(2)}) collective-permute-start(bf16[336,128]{1,0:T(8,128)(2,1)S(1)} %get-tuple-element.89), channel_id=1, source_target_pairs={{0,16},{8,24},{16,0},{24,8},{1,17},{9,25},{17,1},{25,9},{2,18},{10... | collective-permute-start | bytes 258056 | tf_op jit(solution)/shard_map/ppermute | solution.py:40
  26.8 1.6 %collective-permute-start.9 = (bf16[512,128]{1,0:T(8,128)(2,1)S(1)}, bf16[512,128]{1,0:T(8,128)(2,1)S(1)}, u32[]{:S(2)}, u32[]{:S(2)}) collective-permute-start(bf16[512,128]{1,0:T(8,128)(2,1)S(1)} %collective-permute-done.2.one), channel_id=1, source_target_pairs={{0,1},{1,2},{2,3},{3,7},{7,6},{6,5},{5,4},{4,0},{8,9},{9,10},{10,1... | collective-permute-start | bytes 393224 | tf_op jit(solution)/shard_map/ppermute | solution.py:34
  29.8 1.6 %collective-permute-start.7 = (bf16[512,128]{1,0:T(8,128)(2,1)S(1)}, bf16[512,128]{1,0:T(8,128)(2,1)S(1)}, u32[]{:S(2)}, u32[]{:S(2)}) collective-permute-start(bf16[512,128]{1,0:T(8,128)(2,1)S(1)} %collective-permute-done.5.one), channel_id=1, source_target_pairs={{0,1},{1,2},{2,3},{3,7},{7,6},{6,5},{5,4},{4,0},{8,9},{9,10},{10,1... | collective-permute-start | bytes 393224 | tf_op jit(solution)/shard_map/ppermute | solution.py:34
  32.2 1.3 %collective-permute-done.10.other = bf16[512,128]{1,0:T(8,128)(2,1)S(1)} collective-permute-done((bf16[512,128]{1,0:T(8,128)(2,1)S(1)}, bf16[512,128]{1,0:T(8,128)(2,1)S(1)}, u32[]{:S(2)}, u32[]{:S(2)}) %collective-permute-start.10) | collective-permute-done | bytes 131104 | tf_op jit(solution)/shard_map/ppermute | solution.py:34
  33.5 1.6 %collective-permute-start.11 = (bf16[512,128]{1,0:T(8,128)(2,1)S(1)}, bf16[512,128]{1,0:T(8,128)(2,1)S(1)}, u32[]{:S(2)}, u32[]{:S(2)}) collective-permute-start(bf16[512,128]{1,0:T(8,128)(2,1)S(1)} %collective-permute-done.9.one), channel_id=1, source_target_pairs={{0,1},{1,2},{2,3},{3,7},{7,6},{6,5},{5,4},{4,0},{8,9},{9,10},{10,1... | collective-permute-start | bytes 393224 | tf_op jit(solution)/shard_map/ppermute | solution.py:34
  41.1 1.6 %collective-permute-done.14.mate = bf16[1344,128]{1,0:T(8,128)(2,1)S(1)} collective-permute-done((bf16[1344,128]{1,0:T(8,128)(2,1)S(1)}, bf16[1344,128]{1,0:T(8,128)(2,1)S(1)}, u32[]{:S(2)}, u32[]{:S(2)}) %collective-permute-start.14) | collective-permute-done | bytes 344096 | tf_op jit(solution)/shard_map/ppermute | solution.py:40
  42.9 1.6 %collective-permute-start.15 = (bf16[672,128]{1,0:T(8,128)(2,1)S(1)}, bf16[672,128]{1,0:T(8,128)(2,1)S(1)}, u32[]{:S(2)}, u32[]{:S(2)}) collective-permute-start(bf16[672,128]{1,0:T(8,128)(2,1)S(1)} %get-tuple-element.112), channel_id=1, source_target_pairs={{0,16},{8,24},{16,0},{24,8},{1,17},{9,25},{17,1},{25,9},{2,18},{10... | collective-permute-start | bytes 516104 | tf_op jit(solution)/shard_map/ppermute | solution.py:40
  44.5 4.9 %collective-permute-done.15.across = bf16[672,128]{1,0:T(8,128)(2,1)S(1)} collective-permute-done((bf16[672,128]{1,0:T(8,128)(2,1)S(1)}, bf16[672,128]{1,0:T(8,128)(2,1)S(1)}, u32[]{:S(2)}, u32[]{:S(2)}) %collective-permute-start.15) | collective-permute-done | bytes 172064 | tf_op jit(solution)/shard_map/ppermute | solution.py:40
  50.1 1.5 %collective-permute-start.16 = (bf16[128,512]{1,0:T(8,128)(2,1)S(1)}, bf16[128,512]{1,0:T(8,128)(2,1)S(1)}, u32[]{:S(2)}, u32[]{:S(2)}) collective-permute-start(bf16[128,512]{1,0:T(8,128)(2,1)S(1)} %get-tuple-element.121), channel_id=1, source_target_pairs={{0,1},{1,2},{2,3},{3,7},{7,6},{6,5},{5,4},{4,0},{8,9},{9,10},{10,1... | collective-permute-start | bytes 393224 | tf_op jit(solution)/shard_map/ppermute | solution.py:34
  53.4 1.6 %collective-permute-start.20 = (bf16[128,512]{1,0:T(8,128)(2,1)S(1)}, bf16[128,512]{1,0:T(8,128)(2,1)S(1)}, u32[]{:S(2)}, u32[]{:S(2)}) collective-permute-start(bf16[128,512]{1,0:T(8,128)(2,1)S(1)} %get-tuple-element.117), channel_id=1, source_target_pairs={{0,1},{1,2},{2,3},{3,7},{7,6},{6,5},{5,4},{4,0},{8,9},{9,10},{10,1... | collective-permute-start | bytes 393224 | tf_op jit(solution)/shard_map/ppermute | solution.py:34
  54.9 1.5 %collective-permute-start.18 = (bf16[336,128]{1,0:T(8,128)(2,1)S(1)}, bf16[336,128]{1,0:T(8,128)(2,1)S(1)}, u32[]{:S(2)}, u32[]{:S(2)}) collective-permute-start(bf16[336,128]{1,0:T(8,128)(2,1)S(1)} %get-tuple-element.127), channel_id=1, source_target_pairs={{0,16},{8,24},{16,0},{24,8},{1,17},{9,25},{17,1},{25,9},{2,18},{10... | collective-permute-start | bytes 258056 | tf_op jit(solution)/shard_map/ppermute | solution.py:40
  57.6 1.1 %collective-permute-start.21 = (bf16[128,512]{1,0:T(8,128)(2,1)S(1)}, bf16[128,512]{1,0:T(8,128)(2,1)S(1)}, u32[]{:S(2)}, u32[]{:S(2)}) collective-permute-start(bf16[128,512]{1,0:T(8,128)(2,1)S(1)} %get-tuple-element.123), channel_id=1, source_target_pairs={{0,1},{1,2},{2,3},{3,7},{7,6},{6,5},{5,4},{4,0},{8,9},{9,10},{10,1... | collective-permute-start | bytes 393224 | tf_op jit(solution)/shard_map/ppermute | solution.py:34
  60.9 1.5 %collective-permute-start.24 = (bf16[128,512]{1,0:T(8,128)(2,1)S(1)}, bf16[128,512]{1,0:T(8,128)(2,1)S(1)}, u32[]{:S(2)}, u32[]{:S(2)}) collective-permute-start(bf16[128,512]{1,0:T(8,128)(2,1)S(1)} %get-tuple-element.133), channel_id=1, source_target_pairs={{0,1},{1,2},{2,3},{3,7},{7,6},{6,5},{5,4},{4,0},{8,9},{9,10},{10,1... | collective-permute-start | bytes 393224 | tf_op jit(solution)/shard_map/ppermute | solution.py:34
  63.7 1.4 %collective-permute-start.27 = (bf16[128,512]{1,0:T(8,128)(2,1)S(1)}, bf16[128,512]{1,0:T(8,128)(2,1)S(1)}, u32[]{:S(2)}, u32[]{:S(2)}) collective-permute-start(bf16[128,512]{1,0:T(8,128)(2,1)S(1)} %get-tuple-element.137), channel_id=1, source_target_pairs={{0,1},{1,2},{2,3},{3,7},{7,6},{6,5},{5,4},{4,0},{8,9},{9,10},{10,1... | collective-permute-start | bytes 393224 | tf_op jit(solution)/shard_map/ppermute | solution.py:34
  67.5 1.4 %collective-permute-start.26 = (bf16[128,512]{1,0:T(8,128)(2,1)S(1)}, bf16[128,512]{1,0:T(8,128)(2,1)S(1)}, u32[]{:S(2)}, u32[]{:S(2)}) collective-permute-start(bf16[128,512]{1,0:T(8,128)(2,1)S(1)} %get-tuple-element.143), channel_id=1, source_target_pairs={{0,1},{1,2},{2,3},{3,7},{7,6},{6,5},{5,4},{4,0},{8,9},{9,10},{10,1... | collective-permute-start | bytes 393224 | tf_op jit(solution)/shard_map/ppermute | solution.py:34
  70.1 1.0 %collective-permute-start.29 = (bf16[128,512]{1,0:T(8,128)(2,1)S(1)}, bf16[128,512]{1,0:T(8,128)(2,1)S(1)}, u32[]{:S(2)}, u32[]{:S(2)}) collective-permute-start(bf16[128,512]{1,0:T(8,128)(2,1)S(1)} %get-tuple-element.147), channel_id=1, source_target_pairs={{0,1},{1,2},{2,3},{3,7},{7,6},{6,5},{5,4},{4,0},{8,9},{9,10},{10,1... | collective-permute-start | bytes 393224 | tf_op jit(solution)/shard_map/ppermute | solution.py:34
  71.1 1.0 %collective-permute-start.30 = (bf16[128,512]{1,0:T(8,128)(2,1)S(1)}, bf16[128,512]{1,0:T(8,128)(2,1)S(1)}, u32[]{:S(2)}, u32[]{:S(2)}) collective-permute-start(bf16[128,512]{1,0:T(8,128)(2,1)S(1)} %get-tuple-element.148), channel_id=1, source_target_pairs={{0,4},{1,0},{2,1},{3,2},{7,3},{6,7},{5,6},{4,5},{8,12},{9,8},{10,9... | collective-permute-start | bytes 393224 | tf_op jit(solution)/shard_map/ppermute | solution.py:34
  (75 shorter events, 24.3 us)
Async XLA Ops:
  7.0 11.1 %collective-permute-start.1 = (bf16[1024,128]{1,0:T(8,128)(2,1)S(1)}, bf16[1024,128]{1,0:T(8,128)(2,1)S(1)}, u32[]{:S(2)}, u32[]{:S(2)}) collective-permute-start(bf16[1024,128]{1,0:T(8,128)(2,1)S(1)} %encode.1.latents), channel_id=1, source_target_pairs={{0,4},{1,0},{2,1},{3,2},{7,3},{6,7},{5,6},{4,5},{8,12},{9,8},{10,9... | collective-permute-start | bytes 786440 | tf_op jit(solution)/shard_map/ppermute | solution.py:34
  9.9 8.1 %collective-permute-start = (bf16[1024,128]{1,0:T(8,128)(2,1)S(1)}, bf16[1024,128]{1,0:T(8,128)(2,1)S(1)}, u32[]{:S(2)}, u32[]{:S(2)}) collective-permute-start(bf16[1024,128]{1,0:T(8,128)(2,1)S(1)} %encode.1.latents), channel_id=1, source_target_pairs={{0,1},{1,2},{2,3},{3,7},{7,6},{6,5},{5,4},{4,0},{8,9},{9,10},{10,1... | collective-permute-start | bytes 786440 | tf_op jit(solution)/shard_map/ppermute | solution.py:34
  18.1 5.9 %collective-permute-start.2 = (bf16[512,128]{1,0:T(8,128)(2,1)S(1)}, bf16[512,128]{1,0:T(8,128)(2,1)S(1)}, u32[]{:S(2)}, u32[]{:S(2)}) collective-permute-start(bf16[512,128]{1,0:T(8,128)(2,1)S(1)} %get-tuple-element.81), channel_id=1, source_target_pairs={{0,1},{1,2},{2,3},{3,7},{7,6},{6,5},{5,4},{4,0},{8,9},{9,10},{10,1... | collective-permute-start | bytes 393224 | tf_op jit(solution)/shard_map/ppermute | solution.py:34
  20.1 5.2 %collective-permute-start.3 = (bf16[512,128]{1,0:T(8,128)(2,1)S(1)}, bf16[512,128]{1,0:T(8,128)(2,1)S(1)}, u32[]{:S(2)}, u32[]{:S(2)}) collective-permute-start(bf16[512,128]{1,0:T(8,128)(2,1)S(1)} %get-tuple-element.82), channel_id=1, source_target_pairs={{0,4},{1,0},{2,1},{3,2},{7,3},{6,7},{5,6},{4,5},{8,12},{9,8},{10,9... | collective-permute-start | bytes 393224 | tf_op jit(solution)/shard_map/ppermute | solution.py:34
  21.8 7.0 %collective-permute-start.5 = (bf16[512,128]{1,0:T(8,128)(2,1)S(1)}, bf16[512,128]{1,0:T(8,128)(2,1)S(1)}, u32[]{:S(2)}, u32[]{:S(2)}) collective-permute-start(bf16[512,128]{1,0:T(8,128)(2,1)S(1)} %get-tuple-element.90), channel_id=1, source_target_pairs={{0,1},{1,2},{2,3},{3,7},{7,6},{6,5},{5,4},{4,0},{8,9},{9,10},{10,1... | collective-permute-start | bytes 393224 | tf_op jit(solution)/shard_map/ppermute | solution.py:34
  23.8 5.4 %collective-permute-start.6 = (bf16[512,128]{1,0:T(8,128)(2,1)S(1)}, bf16[512,128]{1,0:T(8,128)(2,1)S(1)}, u32[]{:S(2)}, u32[]{:S(2)}) collective-permute-start(bf16[512,128]{1,0:T(8,128)(2,1)S(1)} %get-tuple-element.91), channel_id=1, source_target_pairs={{0,4},{1,0},{2,1},{3,2},{7,3},{6,7},{5,6},{4,5},{8,12},{9,8},{10,9... | collective-permute-start | bytes 393224 | tf_op jit(solution)/shard_map/ppermute | solution.py:34
  26.8 5.4 %collective-permute-start.9 = (bf16[512,128]{1,0:T(8,128)(2,1)S(1)}, bf16[512,128]{1,0:T(8,128)(2,1)S(1)}, u32[]{:S(2)}, u32[]{:S(2)}) collective-permute-start(bf16[512,128]{1,0:T(8,128)(2,1)S(1)} %collective-permute-done.2.one), channel_id=1, source_target_pairs={{0,1},{1,2},{2,3},{3,7},{7,6},{6,5},{5,4},{4,0},{8,9},{9,10},{10,1... | collective-permute-start | bytes 393224 | tf_op jit(solution)/shard_map/ppermute | solution.py:34
  28.4 5.2 %collective-permute-start.10 = (bf16[512,128]{1,0:T(8,128)(2,1)S(1)}, bf16[512,128]{1,0:T(8,128)(2,1)S(1)}, u32[]{:S(2)}, u32[]{:S(2)}) collective-permute-start(bf16[512,128]{1,0:T(8,128)(2,1)S(1)} %collective-permute-done.3.other), channel_id=1, source_target_pairs={{0,4},{1,0},{2,1},{3,2},{7,3},{6,7},{5,6},{4,5},{8,12},{9,8},{10,9... | collective-permute-start | bytes 393224 | tf_op jit(solution)/shard_map/ppermute | solution.py:34
  29.8 7.6 %collective-permute-start.7 = (bf16[512,128]{1,0:T(8,128)(2,1)S(1)}, bf16[512,128]{1,0:T(8,128)(2,1)S(1)}, u32[]{:S(2)}, u32[]{:S(2)}) collective-permute-start(bf16[512,128]{1,0:T(8,128)(2,1)S(1)} %collective-permute-done.5.one), channel_id=1, source_target_pairs={{0,1},{1,2},{2,3},{3,7},{7,6},{6,5},{5,4},{4,0},{8,9},{9,10},{10,1... | collective-permute-start | bytes 393224 | tf_op jit(solution)/shard_map/ppermute | solution.py:34
  31.3 6.1 %collective-permute-start.8 = (bf16[512,128]{1,0:T(8,128)(2,1)S(1)}, bf16[512,128]{1,0:T(8,128)(2,1)S(1)}, u32[]{:S(2)}, u32[]{:S(2)}) collective-permute-start(bf16[512,128]{1,0:T(8,128)(2,1)S(1)} %collective-permute-done.6.other), channel_id=1, source_target_pairs={{0,4},{1,0},{2,1},{3,2},{7,3},{6,7},{5,6},{4,5},{8,12},{9,8},{10,9... | collective-permute-start | bytes 393224 | tf_op jit(solution)/shard_map/ppermute | solution.py:34
  31.8 7.4 %collective-permute-start.13 = (bf16[672,128]{1,0:T(8,128)(2,1)S(1)}, bf16[672,128]{1,0:T(8,128)(2,1)S(1)}, u32[]{:S(2)}, u32[]{:S(2)}) collective-permute-start(bf16[672,128]{1,0:T(8,128)(2,1)S(1)} %ahead_pair.1), channel_id=1, source_target_pairs={{0,8},{8,0},{16,24},{24,16},{1,9},{9,1},{17,25},{25,17},{2,10},{10... | collective-permute-start | bytes 516104 | tf_op jit(solution)/shard_map/ppermute | solution.py:40
  33.5 5.7 %collective-permute-start.11 = (bf16[512,128]{1,0:T(8,128)(2,1)S(1)}, bf16[512,128]{1,0:T(8,128)(2,1)S(1)}, u32[]{:S(2)}, u32[]{:S(2)}) collective-permute-start(bf16[512,128]{1,0:T(8,128)(2,1)S(1)} %collective-permute-done.9.one), channel_id=1, source_target_pairs={{0,1},{1,2},{2,3},{3,7},{7,6},{6,5},{5,4},{4,0},{8,9},{9,10},{10,1... | collective-permute-start | bytes 393224 | tf_op jit(solution)/shard_map/ppermute | solution.py:34
  42.9 6.5 %collective-permute-start.15 = (bf16[672,128]{1,0:T(8,128)(2,1)S(1)}, bf16[672,128]{1,0:T(8,128)(2,1)S(1)}, u32[]{:S(2)}, u32[]{:S(2)}) collective-permute-start(bf16[672,128]{1,0:T(8,128)(2,1)S(1)} %get-tuple-element.112), channel_id=1, source_target_pairs={{0,16},{8,24},{16,0},{24,8},{1,17},{9,25},{17,1},{25,9},{2,18},{10... | collective-permute-start | bytes 516104 | tf_op jit(solution)/shard_map/ppermute | solution.py:40
  50.1 6.9 %collective-permute-start.16 = (bf16[128,512]{1,0:T(8,128)(2,1)S(1)}, bf16[128,512]{1,0:T(8,128)(2,1)S(1)}, u32[]{:S(2)}, u32[]{:S(2)}) collective-permute-start(bf16[128,512]{1,0:T(8,128)(2,1)S(1)} %get-tuple-element.121), channel_id=1, source_target_pairs={{0,1},{1,2},{2,3},{3,7},{7,6},{6,5},{5,4},{4,0},{8,9},{9,10},{10,1... | collective-permute-start | bytes 393224 | tf_op jit(solution)/shard_map/ppermute | solution.py:34
  51.7 5.8 %collective-permute-start.17 = (bf16[128,512]{1,0:T(8,128)(2,1)S(1)}, bf16[128,512]{1,0:T(8,128)(2,1)S(1)}, u32[]{:S(2)}, u32[]{:S(2)}) collective-permute-start(bf16[128,512]{1,0:T(8,128)(2,1)S(1)} %get-tuple-element.122), channel_id=1, source_target_pairs={{0,4},{1,0},{2,1},{3,2},{7,3},{6,7},{5,6},{4,5},{8,12},{9,8},{10,9... | collective-permute-start | bytes 393224 | tf_op jit(solution)/shard_map/ppermute | solution.py:34
  52.8 7.4 %collective-permute-start.19 = (bf16[128,512]{1,0:T(8,128)(2,1)S(1)}, bf16[128,512]{1,0:T(8,128)(2,1)S(1)}, u32[]{:S(2)}, u32[]{:S(2)}) collective-permute-start(bf16[128,512]{1,0:T(8,128)(2,1)S(1)} %get-tuple-element.116), channel_id=1, source_target_pairs={{0,4},{1,0},{2,1},{3,2},{7,3},{6,7},{5,6},{4,5},{8,12},{9,8},{10,9... | collective-permute-start | bytes 393224 | tf_op jit(solution)/shard_map/ppermute | solution.py:34
  53.4 6.9 %collective-permute-start.20 = (bf16[128,512]{1,0:T(8,128)(2,1)S(1)}, bf16[128,512]{1,0:T(8,128)(2,1)S(1)}, u32[]{:S(2)}, u32[]{:S(2)}) collective-permute-start(bf16[128,512]{1,0:T(8,128)(2,1)S(1)} %get-tuple-element.117), channel_id=1, source_target_pairs={{0,1},{1,2},{2,3},{3,7},{7,6},{6,5},{5,4},{4,0},{8,9},{9,10},{10,1... | collective-permute-start | bytes 393224 | tf_op jit(solution)/shard_map/ppermute | solution.py:34
  57.6 5.6 %collective-permute-start.21 = (bf16[128,512]{1,0:T(8,128)(2,1)S(1)}, bf16[128,512]{1,0:T(8,128)(2,1)S(1)}, u32[]{:S(2)}, u32[]{:S(2)}) collective-permute-start(bf16[128,512]{1,0:T(8,128)(2,1)S(1)} %get-tuple-element.123), channel_id=1, source_target_pairs={{0,1},{1,2},{2,3},{3,7},{7,6},{6,5},{5,4},{4,0},{8,9},{9,10},{10,1... | collective-permute-start | bytes 393224 | tf_op jit(solution)/shard_map/ppermute | solution.py:34
  60.4 6.4 %collective-permute-start.23 = (bf16[128,512]{1,0:T(8,128)(2,1)S(1)}, bf16[128,512]{1,0:T(8,128)(2,1)S(1)}, u32[]{:S(2)}, u32[]{:S(2)}) collective-permute-start(bf16[128,512]{1,0:T(8,128)(2,1)S(1)} %get-tuple-element.132), channel_id=1, source_target_pairs={{0,4},{1,0},{2,1},{3,2},{7,3},{6,7},{5,6},{4,5},{8,12},{9,8},{10,9... | collective-permute-start | bytes 393224 | tf_op jit(solution)/shard_map/ppermute | solution.py:34
  60.9 5.8 %collective-permute-start.24 = (bf16[128,512]{1,0:T(8,128)(2,1)S(1)}, bf16[128,512]{1,0:T(8,128)(2,1)S(1)}, u32[]{:S(2)}, u32[]{:S(2)}) collective-permute-start(bf16[128,512]{1,0:T(8,128)(2,1)S(1)} %get-tuple-element.133), channel_id=1, source_target_pairs={{0,1},{1,2},{2,3},{3,7},{7,6},{6,5},{5,4},{4,0},{8,9},{9,10},{10,1... | collective-permute-start | bytes 393224 | tf_op jit(solution)/shard_map/ppermute | solution.py:34
  63.7 5.8 %collective-permute-start.27 = (bf16[128,512]{1,0:T(8,128)(2,1)S(1)}, bf16[128,512]{1,0:T(8,128)(2,1)S(1)}, u32[]{:S(2)}, u32[]{:S(2)}) collective-permute-start(bf16[128,512]{1,0:T(8,128)(2,1)S(1)} %get-tuple-element.137), channel_id=1, source_target_pairs={{0,1},{1,2},{2,3},{3,7},{7,6},{6,5},{5,4},{4,0},{8,9},{9,10},{10,1... | collective-permute-start | bytes 393224 | tf_op jit(solution)/shard_map/ppermute | solution.py:34
  66.9 6.7 %collective-permute-start.25 = (bf16[128,512]{1,0:T(8,128)(2,1)S(1)}, bf16[128,512]{1,0:T(8,128)(2,1)S(1)}, u32[]{:S(2)}, u32[]{:S(2)}) collective-permute-start(bf16[128,512]{1,0:T(8,128)(2,1)S(1)} %get-tuple-element.142), channel_id=1, source_target_pairs={{0,4},{1,0},{2,1},{3,2},{7,3},{6,7},{5,6},{4,5},{8,12},{9,8},{10,9... | collective-permute-start | bytes 393224 | tf_op jit(solution)/shard_map/ppermute | solution.py:34
  67.5 6.0 %collective-permute-start.26 = (bf16[128,512]{1,0:T(8,128)(2,1)S(1)}, bf16[128,512]{1,0:T(8,128)(2,1)S(1)}, u32[]{:S(2)}, u32[]{:S(2)}) collective-permute-start(bf16[128,512]{1,0:T(8,128)(2,1)S(1)} %get-tuple-element.143), channel_id=1, source_target_pairs={{0,1},{1,2},{2,3},{3,7},{7,6},{6,5},{5,4},{4,0},{8,9},{9,10},{10,1... | collective-permute-start | bytes 393224 | tf_op jit(solution)/shard_map/ppermute | solution.py:34
  70.1 5.0 %collective-permute-start.29 = (bf16[128,512]{1,0:T(8,128)(2,1)S(1)}, bf16[128,512]{1,0:T(8,128)(2,1)S(1)}, u32[]{:S(2)}, u32[]{:S(2)}) collective-permute-start(bf16[128,512]{1,0:T(8,128)(2,1)S(1)} %get-tuple-element.147), channel_id=1, source_target_pairs={{0,1},{1,2},{2,3},{3,7},{7,6},{6,5},{5,4},{4,0},{8,9},{9,10},{10,1... | collective-permute-start | bytes 393224 | tf_op jit(solution)/shard_map/ppermute | solution.py:34
  (11 other events, 86.0 us)

commit v7 on v6

--- a/solution.py
+++ b/solution.py
@@ -374,10 +374,10 @@
         return call(
             functools.partial(gradient_kernel, pieces=pieces),
             name,
-            [kind, kind],
+            [kind] * len(pieces),
             (held, back),
             [VMEM] * 2,
-            flops=2 * piece_flops,
+            flops=len(pieces) * piece_flops,
         )
 
     def added(name, parts, came):
@@ -393,13 +393,14 @@
         inner = [along(inner[0], -1), along(inner[1], 1)]
         if step == last - 1:
             back, came = lax.optimization_barrier((back, came))
-        parts = products(f"outer_{step}", product, ((step, 0), (size - step, 1)), ready)
-        ready = added(f"add_outer_{step}", parts, outer)
+        pieces = ((step, 0), (size - step, 1))
+        if step > 1:
+            pieces += ((size - step + 1, 0), (step - 1, 1))
+        parts = products(f"products_{step}", product, pieces, ready)
+        ready = added(f"add_outer_{step}", parts[:2], outer)
         outer = [along(ready[0], 1), along(ready[1], -1)]
         if step > 1:
-            pieces = ((size - step + 1, 0), (step - 1, 1))
-            parts = products(f"inner_{step - 1}", product, pieces, ready)
-            inner = ready = added(f"add_inner_{step - 1}", parts, inner)
+            inner = ready = added(f"add_inner_{step - 1}", parts[2:], inner)
     (beyond,) = call(
         outgoing_kernel,
         "outgoing",

time: 77.2 us -> 77.3 us (level)
    pallas_call x26 -> x24, Pallas kernels: 26.2 us -> 25.8 us  [call(): pl.pallas_call(kernel, out_shape=[pltpu.VMEM(shape, dtype) for shape, dty...]
  transfers between devices with their start and end apart: 31 -> 31, of which waited for: 15 -> 14; matrix products, arithmetic and copies ran while one was open for 2% -> 2% of each run, Pallas kernels for 23% -> 23%
where the time goes in v7:
time: 77.3 us; the launch traced here: 77.1 us
  starting transfers between devices  32.7 us (42%)
  Pallas kernels  26.7 us (35%)
  waiting for transfers between devices  15.5 us (20%)
  local copies, waits for them, and re-layouts  1.32 us (2%)
  between operations  0.9 us (1%)
    ppermute x26, starting transfers between devices, along(): return lax.ppermute(value, GROUP, pairs)  27.9 us
    pallas_call x24, Pallas kernels, call(): pl.pallas_call(kernel, out_shape=[pltpu.VMEM(shape, dtype) for shape, dty...  25.8 us
    ppermute x26, waiting for transfers between devices, along(): return lax.ppermute(value, GROUP, pairs)  8.44 us
    ppermute x5, waiting for transfers between devices, swapped(): return lax.ppermute(value, 'section', [(i, i ^ bit) for i in range(layers)])  7.05 us
    ppermute x5, starting transfers between devices, swapped(): return lax.ppermute(value, 'section', [(i, i ^ bit) for i in range(layers)])  4.78 us
  transfers between devices with their start and end apart: 31, of which 14 were waited for; matrix products, arithmetic and copies ran while one was open for 2% of the time, Pallas kernels for 23%

profile of v7, /device:TPU:0, one launch (start us, length us, event | category | flops | bytes accessed | tf_op | source)
XLA Modules:
  0.0 77.1 jit_solution(10666902147341323807)
XLA Ops:
  0.6 6.3 %encode.1.latents = bf16[1024,128]{1,0:T(8,128)(2,1)S(1)} custom-call(s32[128]{0:T(128)} %ids.1, bf16[1,256,5376]{2,1,0:T(8,128)(2,1)} %cache.1, bf16[1,1024,5376]{2,1,0:T(8,128)(2,1)} %weight.1, f32[1,1024]{1,0:T(1,128)} %bias.2), custom_call_target="tpu_custom_call" | custom-call | flops 1761607680 | bytes 13762560 | tf_op jit(solution)/shard_map/encode/pallas_call | solution.py:46
  7.0 3.0 %collective-permute-start.1 = (bf16[1024,128]{1,0:T(8,128)(2,1)S(1)}, bf16[1024,128]{1,0:T(8,128)(2,1)S(1)}, u32[]{:S(2)}, u32[]{:S(2)}) collective-permute-start(bf16[1024,128]{1,0:T(8,128)(2,1)S(1)} %encode.1.latents), channel_id=1, source_target_pairs={{0,4},{1,0},{2,1},{3,2},{7,3},{6,7},{5,6},{4,5},{8,12},{9,8},{10,9... | collective-permute-start | bytes 786440 | tf_op jit(solution)/shard_map/ppermute | solution.py:34
  10.1 7.9 %load_decode.1 = (bf16[1344,8192]{1,0:T(8,128)(2,1)S(1)}, f32[1344,128]{1,0:T(8,128)S(1)}) custom-call(bf16[1344,8192]{1,0:T(8,128)(2,1)} %bitcast.23, bf16[1024,128]{1,0:T(8,128)(2,1)S(1)} %encode.1.latents), custom_call_target="tpu_custom_call" | custom-call | flops 352321536 | bytes 44040192 | tf_op jit(solution)/shard_map/load_decode/pallas_call | solution.py:46
  18.1 2.0 %collective-permute-start.2 = (bf16[512,128]{1,0:T(8,128)(2,1)S(1)}, bf16[512,128]{1,0:T(8,128)(2,1)S(1)}, u32[]{:S(2)}, u32[]{:S(2)}) collective-permute-start(bf16[512,128]{1,0:T(8,128)(2,1)S(1)} %get-tuple-element.79), channel_id=1, source_target_pairs={{0,1},{1,2},{2,3},{3,7},{7,6},{6,5},{5,4},{4,0},{8,9},{9,10},{10,1... | collective-permute-start | bytes 393224 | tf_op jit(solution)/shard_map/ppermute | solution.py:34
  20.2 1.6 %decode_1.1.before = f32[1344,128]{1,0:T(8,128)S(1)} custom-call(bf16[1344,8192]{1,0:T(8,128)(2,1)S(1)} %get-tuple-element.74.decoders, f32[1344,128]{1,0:T(8,128)S(1)} %get-tuple-element.84.before, bf16[1024,128]{1,0:T(8,128)(2,1)S(1)} %collective-permute-done.rise.one, bf16[1024,128]{1,0:T(8,128)(2,1)S(1)} %collective-permute-done.1.fall.other), custom_call_target="tpu_custom_call" | custom-call | flops 352321536 | tf_op jit(solution)/shard_map/decode_1/pallas_call | solution.py:46
  21.8 2.0 %collective-permute-start.5 = (bf16[512,128]{1,0:T(8,128)(2,1)S(1)}, bf16[512,128]{1,0:T(8,128)(2,1)S(1)}, u32[]{:S(2)}, u32[]{:S(2)}) collective-permute-start(bf16[512,128]{1,0:T(8,128)(2,1)S(1)} %get-tuple-element.88), channel_id=1, source_target_pairs={{0,1},{1,2},{2,3},{3,7},{7,6},{6,5},{5,4},{4,0},{8,9},{9,10},{10,1... | collective-permute-start | bytes 393224 | tf_op jit(solution)/shard_map/ppermute | solution.py:34
  24.0 1.2 %collective-permute-done.3.other = bf16[512,128]{1,0:T(8,128)(2,1)S(1)} collective-permute-done((bf16[512,128]{1,0:T(8,128)(2,1)S(1)}, bf16[512,128]{1,0:T(8,128)(2,1)S(1)}, u32[]{:S(2)}, u32[]{:S(2)}) %collective-permute-start.3) | collective-permute-done | bytes 131104 | tf_op jit(solution)/shard_map/ppermute | solution.py:34
  25.3 1.5 %collective-permute-start.4 = (bf16[336,128]{1,0:T(8,128)(2,1)S(1)}, bf16[336,128]{1,0:T(8,128)(2,1)S(1)}, u32[]{:S(2)}, u32[]{:S(2)}) collective-permute-start(bf16[336,128]{1,0:T(8,128)(2,1)S(1)} %get-tuple-element.87), channel_id=1, source_target_pairs={{0,16},{8,24},{16,0},{24,8},{1,17},{9,25},{17,1},{25,9},{2,18},{10... | collective-permute-start | bytes 258056 | tf_op jit(solution)/shard_map/ppermute | solution.py:40
  26.8 1.6 %collective-permute-start.9 = (bf16[512,128]{1,0:T(8,128)(2,1)S(1)}, bf16[512,128]{1,0:T(8,128)(2,1)S(1)}, u32[]{:S(2)}, u32[]{:S(2)}) collective-permute-start(bf16[512,128]{1,0:T(8,128)(2,1)S(1)} %collective-permute-done.2.one), channel_id=1, source_target_pairs={{0,1},{1,2},{2,3},{3,7},{7,6},{6,5},{5,4},{4,0},{8,9},{9,10},{10,1... | collective-permute-start | bytes 393224 | tf_op jit(solution)/shard_map/ppermute | solution.py:34
  29.8 1.6 %collective-permute-start.7 = (bf16[512,128]{1,0:T(8,128)(2,1)S(1)}, bf16[512,128]{1,0:T(8,128)(2,1)S(1)}, u32[]{:S(2)}, u32[]{:S(2)}) collective-permute-start(bf16[512,128]{1,0:T(8,128)(2,1)S(1)} %collective-permute-done.5.one), channel_id=1, source_target_pairs={{0,1},{1,2},{2,3},{3,7},{7,6},{6,5},{5,4},{4,0},{8,9},{9,10},{10,1... | collective-permute-start | bytes 393224 | tf_op jit(solution)/shard_map/ppermute | solution.py:34
  32.2 1.3 %collective-permute-done.10.other = bf16[512,128]{1,0:T(8,128)(2,1)S(1)} collective-permute-done((bf16[512,128]{1,0:T(8,128)(2,1)S(1)}, bf16[512,128]{1,0:T(8,128)(2,1)S(1)}, u32[]{:S(2)}, u32[]{:S(2)}) %collective-permute-start.10) | collective-permute-done | bytes 131104 | tf_op jit(solution)/shard_map/ppermute | solution.py:34
  33.5 1.6 %collective-permute-start.11 = (bf16[512,128]{1,0:T(8,128)(2,1)S(1)}, bf16[512,128]{1,0:T(8,128)(2,1)S(1)}, u32[]{:S(2)}, u32[]{:S(2)}) collective-permute-start(bf16[512,128]{1,0:T(8,128)(2,1)S(1)} %collective-permute-done.9.one), channel_id=1, source_target_pairs={{0,1},{1,2},{2,3},{3,7},{7,6},{6,5},{5,4},{4,0},{8,9},{9,10},{10,1... | collective-permute-start | bytes 393224 | tf_op jit(solution)/shard_map/ppermute | solution.py:34
  41.1 1.6 %collective-permute-done.14.mate = bf16[1344,128]{1,0:T(8,128)(2,1)S(1)} collective-permute-done((bf16[1344,128]{1,0:T(8,128)(2,1)S(1)}, bf16[1344,128]{1,0:T(8,128)(2,1)S(1)}, u32[]{:S(2)}, u32[]{:S(2)}) %collective-permute-start.14) | collective-permute-done | bytes 344096 | tf_op jit(solution)/shard_map/ppermute | solution.py:40
  42.9 1.6 %collective-permute-start.15 = (bf16[672,128]{1,0:T(8,128)(2,1)S(1)}, bf16[672,128]{1,0:T(8,128)(2,1)S(1)}, u32[]{:S(2)}, u32[]{:S(2)}) collective-permute-start(bf16[672,128]{1,0:T(8,128)(2,1)S(1)} %get-tuple-element.110), channel_id=1, source_target_pairs={{0,16},{8,24},{16,0},{24,8},{1,17},{9,25},{17,1},{25,9},{2,18},{10... | collective-permute-start | bytes 516104 | tf_op jit(solution)/shard_map/ppermute | solution.py:40
  44.5 4.9 %collective-permute-done.15.across = bf16[672,128]{1,0:T(8,128)(2,1)S(1)} collective-permute-done((bf16[672,128]{1,0:T(8,128)(2,1)S(1)}, bf16[672,128]{1,0:T(8,128)(2,1)S(1)}, u32[]{:S(2)}, u32[]{:S(2)}) %collective-permute-start.15) | collective-permute-done | bytes 172064 | tf_op jit(solution)/shard_map/ppermute | solution.py:40
  50.1 1.5 %collective-permute-start.23 = (bf16[128,512]{1,0:T(8,128)(2,1)S(1)}, bf16[128,512]{1,0:T(8,128)(2,1)S(1)}, u32[]{:S(2)}, u32[]{:S(2)}) collective-permute-start(bf16[128,512]{1,0:T(8,128)(2,1)S(1)} %get-tuple-element.137), channel_id=1, source_target_pairs={{0,1},{1,2},{2,3},{3,7},{7,6},{6,5},{5,4},{4,0},{8,9},{9,10},{10,1... | collective-permute-start | bytes 393224 | tf_op jit(solution)/shard_map/ppermute | solution.py:34
  53.4 1.6 %collective-permute-start.18 = (bf16[128,512]{1,0:T(8,128)(2,1)S(1)}, bf16[128,512]{1,0:T(8,128)(2,1)S(1)}, u32[]{:S(2)}, u32[]{:S(2)}) collective-permute-start(bf16[128,512]{1,0:T(8,128)(2,1)S(1)} %get-tuple-element.115), channel_id=1, source_target_pairs={{0,1},{1,2},{2,3},{3,7},{7,6},{6,5},{5,4},{4,0},{8,9},{9,10},{10,1... | collective-permute-start | bytes 393224 | tf_op jit(solution)/shard_map/ppermute | solution.py:34
  54.9 1.5 %collective-permute-start.16 = (bf16[336,128]{1,0:T(8,128)(2,1)S(1)}, bf16[336,128]{1,0:T(8,128)(2,1)S(1)}, u32[]{:S(2)}, u32[]{:S(2)}) collective-permute-start(bf16[336,128]{1,0:T(8,128)(2,1)S(1)} %get-tuple-element.118), channel_id=1, source_target_pairs={{0,16},{8,24},{16,0},{24,8},{1,17},{9,25},{17,1},{25,9},{2,18},{10... | collective-permute-start | bytes 258056 | tf_op jit(solution)/shard_map/ppermute | solution.py:40
  57.6 1.5 %collective-permute-start.25 = (bf16[128,512]{1,0:T(8,128)(2,1)S(1)}, bf16[128,512]{1,0:T(8,128)(2,1)S(1)}, u32[]{:S(2)}, u32[]{:S(2)}) collective-permute-start(bf16[128,512]{1,0:T(8,128)(2,1)S(1)} %get-tuple-element.139), channel_id=1, source_target_pairs={{0,1},{1,2},{2,3},{3,7},{7,6},{6,5},{5,4},{4,0},{8,9},{9,10},{10,1... | collective-permute-start | bytes 393224 | tf_op jit(solution)/shard_map/ppermute | solution.py:34
  60.3 1.5 %collective-permute-start.20 = (bf16[128,512]{1,0:T(8,128)(2,1)S(1)}, bf16[128,512]{1,0:T(8,128)(2,1)S(1)}, u32[]{:S(2)}, u32[]{:S(2)}) collective-permute-start(bf16[128,512]{1,0:T(8,128)(2,1)S(1)} %get-tuple-element.124), channel_id=1, source_target_pairs={{0,1},{1,2},{2,3},{3,7},{7,6},{6,5},{5,4},{4,0},{8,9},{9,10},{10,1... | collective-permute-start | bytes 393224 | tf_op jit(solution)/shard_map/ppermute | solution.py:34
  62.8 1.3 %collective-permute-done.26.came_other = bf16[128,512]{1,0:T(8,128)(2,1)S(1)} collective-permute-done((bf16[128,512]{1,0:T(8,128)(2,1)S(1)}, bf16[128,512]{1,0:T(8,128)(2,1)S(1)}, u32[]{:S(2)}, u32[]{:S(2)}) %collective-permute-start.26) | collective-permute-done | bytes 131104 | tf_op jit(solution)/shard_map/ppermute | solution.py:34
  65.1 1.2 %collective-permute-start.28 = (bf16[128,512]{1,0:T(8,128)(2,1)S(1)}, bf16[128,512]{1,0:T(8,128)(2,1)S(1)}, u32[]{:S(2)}, u32[]{:S(2)}) collective-permute-start(bf16[128,512]{1,0:T(8,128)(2,1)S(1)} %get-tuple-element.142), channel_id=1, source_target_pairs={{0,4},{1,0},{2,1},{3,2},{7,3},{6,7},{5,6},{4,5},{8,12},{9,8},{10,9... | collective-permute-start | bytes 393224 | tf_op jit(solution)/shard_map/ppermute | solution.py:34
  67.1 1.9 %collective-permute-start.22 = (bf16[128,512]{1,0:T(8,128)(2,1)S(1)}, bf16[128,512]{1,0:T(8,128)(2,1)S(1)}, u32[]{:S(2)}, u32[]{:S(2)}) collective-permute-start(bf16[128,512]{1,0:T(8,128)(2,1)S(1)} %get-tuple-element.129), channel_id=1, source_target_pairs={{0,1},{1,2},{2,3},{3,7},{7,6},{6,5},{5,4},{4,0},{8,9},{9,10},{10,1... | collective-permute-start | bytes 393224 | tf_op jit(solution)/shard_map/ppermute | solution.py:34
  70.1 1.1 %collective-permute-start.29 = (bf16[128,512]{1,0:T(8,128)(2,1)S(1)}, bf16[128,512]{1,0:T(8,128)(2,1)S(1)}, u32[]{:S(2)}, u32[]{:S(2)}) collective-permute-start(bf16[128,512]{1,0:T(8,128)(2,1)S(1)} %get-tuple-element.143), channel_id=1, source_target_pairs={{0,1},{1,2},{2,3},{3,7},{7,6},{6,5},{5,4},{4,0},{8,9},{9,10},{10,1... | collective-permute-start | bytes 393224 | tf_op jit(solution)/shard_map/ppermute | solution.py:34
  (73 shorter events, 23.3 us)
Async XLA Ops:
  7.0 11.1 %collective-permute-start.1 = (bf16[1024,128]{1,0:T(8,128)(2,1)S(1)}, bf16[1024,128]{1,0:T(8,128)(2,1)S(1)}, u32[]{:S(2)}, u32[]{:S(2)}) collective-permute-start(bf16[1024,128]{1,0:T(8,128)(2,1)S(1)} %encode.1.latents), channel_id=1, source_target_pairs={{0,4},{1,0},{2,1},{3,2},{7,3},{6,7},{5,6},{4,5},{8,12},{9,8},{10,9... | collective-permute-start | bytes 786440 | tf_op jit(solution)/shard_map/ppermute | solution.py:34
  9.9 8.1 %collective-permute-start = (bf16[1024,128]{1,0:T(8,128)(2,1)S(1)}, bf16[1024,128]{1,0:T(8,128)(2,1)S(1)}, u32[]{:S(2)}, u32[]{:S(2)}) collective-permute-start(bf16[1024,128]{1,0:T(8,128)(2,1)S(1)} %encode.1.latents), channel_id=1, source_target_pairs={{0,1},{1,2},{2,3},{3,7},{7,6},{6,5},{5,4},{4,0},{8,9},{9,10},{10,1... | collective-permute-start | bytes 786440 | tf_op jit(solution)/shard_map/ppermute | solution.py:34
  18.1 5.9 %collective-permute-start.2 = (bf16[512,128]{1,0:T(8,128)(2,1)S(1)}, bf16[512,128]{1,0:T(8,128)(2,1)S(1)}, u32[]{:S(2)}, u32[]{:S(2)}) collective-permute-start(bf16[512,128]{1,0:T(8,128)(2,1)S(1)} %get-tuple-element.79), channel_id=1, source_target_pairs={{0,1},{1,2},{2,3},{3,7},{7,6},{6,5},{5,4},{4,0},{8,9},{9,10},{10,1... | collective-permute-start | bytes 393224 | tf_op jit(solution)/shard_map/ppermute | solution.py:34
  20.1 5.2 %collective-permute-start.3 = (bf16[512,128]{1,0:T(8,128)(2,1)S(1)}, bf16[512,128]{1,0:T(8,128)(2,1)S(1)}, u32[]{:S(2)}, u32[]{:S(2)}) collective-permute-start(bf16[512,128]{1,0:T(8,128)(2,1)S(1)} %get-tuple-element.80), channel_id=1, source_target_pairs={{0,4},{1,0},{2,1},{3,2},{7,3},{6,7},{5,6},{4,5},{8,12},{9,8},{10,9... | collective-permute-start | bytes 393224 | tf_op jit(solution)/shard_map/ppermute | solution.py:34
  21.8 7.0 %collective-permute-start.5 = (bf16[512,128]{1,0:T(8,128)(2,1)S(1)}, bf16[512,128]{1,0:T(8,128)(2,1)S(1)}, u32[]{:S(2)}, u32[]{:S(2)}) collective-permute-start(bf16[512,128]{1,0:T(8,128)(2,1)S(1)} %get-tuple-element.88), channel_id=1, source_target_pairs={{0,1},{1,2},{2,3},{3,7},{7,6},{6,5},{5,4},{4,0},{8,9},{9,10},{10,1... | collective-permute-start | bytes 393224 | tf_op jit(solution)/shard_map/ppermute | solution.py:34
  23.8 5.4 %collective-permute-start.6 = (bf16[512,128]{1,0:T(8,128)(2,1)S(1)}, bf16[512,128]{1,0:T(8,128)(2,1)S(1)}, u32[]{:S(2)}, u32[]{:S(2)}) collective-permute-start(bf16[512,128]{1,0:T(8,128)(2,1)S(1)} %get-tuple-element.89), channel_id=1, source_target_pairs={{0,4},{1,0},{2,1},{3,2},{7,3},{6,7},{5,6},{4,5},{8,12},{9,8},{10,9... | collective-permute-start | bytes 393224 | tf_op jit(solution)/shard_map/ppermute | solution.py:34
  26.8 5.4 %collective-permute-start.9 = (bf16[512,128]{1,0:T(8,128)(2,1)S(1)}, bf16[512,128]{1,0:T(8,128)(2,1)S(1)}, u32[]{:S(2)}, u32[]{:S(2)}) collective-permute-start(bf16[512,128]{1,0:T(8,128)(2,1)S(1)} %collective-permute-done.2.one), channel_id=1, source_target_pairs={{0,1},{1,2},{2,3},{3,7},{7,6},{6,5},{5,4},{4,0},{8,9},{9,10},{10,1... | collective-permute-start | bytes 393224 | tf_op jit(solution)/shard_map/ppermute | solution.py:34
  28.4 5.2 %collective-permute-start.10 = (bf16[512,128]{1,0:T(8,128)(2,1)S(1)}, bf16[512,128]{1,0:T(8,128)(2,1)S(1)}, u32[]{:S(2)}, u32[]{:S(2)}) collective-permute-start(bf16[512,128]{1,0:T(8,128)(2,1)S(1)} %collective-permute-done.3.other), channel_id=1, source_target_pairs={{0,4},{1,0},{2,1},{3,2},{7,3},{6,7},{5,6},{4,5},{8,12},{9,8},{10,9... | collective-permute-start | bytes 393224 | tf_op jit(solution)/shard_map/ppermute | solution.py:34
  29.8 7.6 %collective-permute-start.7 = (bf16[512,128]{1,0:T(8,128)(2,1)S(1)}, bf16[512,128]{1,0:T(8,128)(2,1)S(1)}, u32[]{:S(2)}, u32[]{:S(2)}) collective-permute-start(bf16[512,128]{1,0:T(8,128)(2,1)S(1)} %collective-permute-done.5.one), channel_id=1, source_target_pairs={{0,1},{1,2},{2,3},{3,7},{7,6},{6,5},{5,4},{4,0},{8,9},{9,10},{10,1... | collective-permute-start | bytes 393224 | tf_op jit(solution)/shard_map/ppermute | solution.py:34
  31.3 6.1 %collective-permute-start.8 = (bf16[512,128]{1,0:T(8,128)(2,1)S(1)}, bf16[512,128]{1,0:T(8,128)(2,1)S(1)}, u32[]{:S(2)}, u32[]{:S(2)}) collective-permute-start(bf16[512,128]{1,0:T(8,128)(2,1)S(1)} %collective-permute-done.6.other), channel_id=1, source_target_pairs={{0,4},{1,0},{2,1},{3,2},{7,3},{6,7},{5,6},{4,5},{8,12},{9,8},{10,9... | collective-permute-start | bytes 393224 | tf_op jit(solution)/shard_map/ppermute | solution.py:34
  31.8 7.4 %collective-permute-start.13 = (bf16[672,128]{1,0:T(8,128)(2,1)S(1)}, bf16[672,128]{1,0:T(8,128)(2,1)S(1)}, u32[]{:S(2)}, u32[]{:S(2)}) collective-permute-start(bf16[672,128]{1,0:T(8,128)(2,1)S(1)} %ahead_pair.1), channel_id=1, source_target_pairs={{0,8},{8,0},{16,24},{24,16},{1,9},{9,1},{17,25},{25,17},{2,10},{10... | collective-permute-start | bytes 516104 | tf_op jit(solution)/shard_map/ppermute | solution.py:40
  33.5 5.7 %collective-permute-start.11 = (bf16[512,128]{1,0:T(8,128)(2,1)S(1)}, bf16[512,128]{1,0:T(8,128)(2,1)S(1)}, u32[]{:S(2)}, u32[]{:S(2)}) collective-permute-start(bf16[512,128]{1,0:T(8,128)(2,1)S(1)} %collective-permute-done.9.one), channel_id=1, source_target_pairs={{0,1},{1,2},{2,3},{3,7},{7,6},{6,5},{5,4},{4,0},{8,9},{9,10},{10,1... | collective-permute-start | bytes 393224 | tf_op jit(solution)/shard_map/ppermute | solution.py:34
  42.9 6.5 %collective-permute-start.15 = (bf16[672,128]{1,0:T(8,128)(2,1)S(1)}, bf16[672,128]{1,0:T(8,128)(2,1)S(1)}, u32[]{:S(2)}, u32[]{:S(2)}) collective-permute-start(bf16[672,128]{1,0:T(8,128)(2,1)S(1)} %get-tuple-element.110), channel_id=1, source_target_pairs={{0,16},{8,24},{16,0},{24,8},{1,17},{9,25},{17,1},{25,9},{2,18},{10... | collective-permute-start | bytes 516104 | tf_op jit(solution)/shard_map/ppermute | solution.py:40
  50.1 7.3 %collective-permute-start.23 = (bf16[128,512]{1,0:T(8,128)(2,1)S(1)}, bf16[128,512]{1,0:T(8,128)(2,1)S(1)}, u32[]{:S(2)}, u32[]{:S(2)}) collective-permute-start(bf16[128,512]{1,0:T(8,128)(2,1)S(1)} %get-tuple-element.137), channel_id=1, source_target_pairs={{0,1},{1,2},{2,3},{3,7},{7,6},{6,5},{5,4},{4,0},{8,9},{9,10},{10,1... | collective-permute-start | bytes 393224 | tf_op jit(solution)/shard_map/ppermute | solution.py:34
  51.7 5.8 %collective-permute-start.24 = (bf16[128,512]{1,0:T(8,128)(2,1)S(1)}, bf16[128,512]{1,0:T(8,128)(2,1)S(1)}, u32[]{:S(2)}, u32[]{:S(2)}) collective-permute-start(bf16[128,512]{1,0:T(8,128)(2,1)S(1)} %get-tuple-element.138), channel_id=1, source_target_pairs={{0,4},{1,0},{2,1},{3,2},{7,3},{6,7},{5,6},{4,5},{8,12},{9,8},{10,9... | collective-permute-start | bytes 393224 | tf_op jit(solution)/shard_map/ppermute | solution.py:34
  52.8 6.8 %collective-permute-start.17 = (bf16[128,512]{1,0:T(8,128)(2,1)S(1)}, bf16[128,512]{1,0:T(8,128)(2,1)S(1)}, u32[]{:S(2)}, u32[]{:S(2)}) collective-permute-start(bf16[128,512]{1,0:T(8,128)(2,1)S(1)} %get-tuple-element.114), channel_id=1, source_target_pairs={{0,4},{1,0},{2,1},{3,2},{7,3},{6,7},{5,6},{4,5},{8,12},{9,8},{10,9... | collective-permute-start | bytes 393224 | tf_op jit(solution)/shard_map/ppermute | solution.py:34
  53.4 6.3 %collective-permute-start.18 = (bf16[128,512]{1,0:T(8,128)(2,1)S(1)}, bf16[128,512]{1,0:T(8,128)(2,1)S(1)}, u32[]{:S(2)}, u32[]{:S(2)}) collective-permute-start(bf16[128,512]{1,0:T(8,128)(2,1)S(1)} %get-tuple-element.115), channel_id=1, source_target_pairs={{0,1},{1,2},{2,3},{3,7},{7,6},{6,5},{5,4},{4,0},{8,9},{9,10},{10,1... | collective-permute-start | bytes 393224 | tf_op jit(solution)/shard_map/ppermute | solution.py:34
  57.6 5.2 %collective-permute-start.25 = (bf16[128,512]{1,0:T(8,128)(2,1)S(1)}, bf16[128,512]{1,0:T(8,128)(2,1)S(1)}, u32[]{:S(2)}, u32[]{:S(2)}) collective-permute-start(bf16[128,512]{1,0:T(8,128)(2,1)S(1)} %get-tuple-element.139), channel_id=1, source_target_pairs={{0,1},{1,2},{2,3},{3,7},{7,6},{6,5},{5,4},{4,0},{8,9},{9,10},{10,1... | collective-permute-start | bytes 393224 | tf_op jit(solution)/shard_map/ppermute | solution.py:34
  59.1 5.1 %collective-permute-start.26 = (bf16[128,512]{1,0:T(8,128)(2,1)S(1)}, bf16[128,512]{1,0:T(8,128)(2,1)S(1)}, u32[]{:S(2)}, u32[]{:S(2)}) collective-permute-start(bf16[128,512]{1,0:T(8,128)(2,1)S(1)} %get-tuple-element.140), channel_id=1, source_target_pairs={{0,4},{1,0},{2,1},{3,2},{7,3},{6,7},{5,6},{4,5},{8,12},{9,8},{10,9... | collective-permute-start | bytes 393224 | tf_op jit(solution)/shard_map/ppermute | solution.py:34
  59.7 7.2 %collective-permute-start.19 = (bf16[128,512]{1,0:T(8,128)(2,1)S(1)}, bf16[128,512]{1,0:T(8,128)(2,1)S(1)}, u32[]{:S(2)}, u32[]{:S(2)}) collective-permute-start(bf16[128,512]{1,0:T(8,128)(2,1)S(1)} %get-tuple-element.123), channel_id=1, source_target_pairs={{0,4},{1,0},{2,1},{3,2},{7,3},{6,7},{5,6},{4,5},{8,12},{9,8},{10,9... | collective-permute-start | bytes 393224 | tf_op jit(solution)/shard_map/ppermute | solution.py:34
  60.3 6.6 %collective-permute-start.20 = (bf16[128,512]{1,0:T(8,128)(2,1)S(1)}, bf16[128,512]{1,0:T(8,128)(2,1)S(1)}, u32[]{:S(2)}, u32[]{:S(2)}) collective-permute-start(bf16[128,512]{1,0:T(8,128)(2,1)S(1)} %get-tuple-element.124), channel_id=1, source_target_pairs={{0,1},{1,2},{2,3},{3,7},{7,6},{6,5},{5,4},{4,0},{8,9},{9,10},{10,1... | collective-permute-start | bytes 393224 | tf_op jit(solution)/shard_map/ppermute | solution.py:34
  64.2 5.5 %collective-permute-start.27 = (bf16[128,512]{1,0:T(8,128)(2,1)S(1)}, bf16[128,512]{1,0:T(8,128)(2,1)S(1)}, u32[]{:S(2)}, u32[]{:S(2)}) collective-permute-start(bf16[128,512]{1,0:T(8,128)(2,1)S(1)} %get-tuple-element.141), channel_id=1, source_target_pairs={{0,1},{1,2},{2,3},{3,7},{7,6},{6,5},{5,4},{4,0},{8,9},{9,10},{10,1... | collective-permute-start | bytes 393224 | tf_op jit(solution)/shard_map/ppermute | solution.py:34
  67.0 6.6 %collective-permute-start.21 = (bf16[128,512]{1,0:T(8,128)(2,1)S(1)}, bf16[128,512]{1,0:T(8,128)(2,1)S(1)}, u32[]{:S(2)}, u32[]{:S(2)}) collective-permute-start(bf16[128,512]{1,0:T(8,128)(2,1)S(1)} %get-tuple-element.128), channel_id=1, source_target_pairs={{0,4},{1,0},{2,1},{3,2},{7,3},{6,7},{5,6},{4,5},{8,12},{9,8},{10,9... | collective-permute-start | bytes 393224 | tf_op jit(solution)/shard_map/ppermute | solution.py:34
  67.1 6.4 %collective-permute-start.22 = (bf16[128,512]{1,0:T(8,128)(2,1)S(1)}, bf16[128,512]{1,0:T(8,128)(2,1)S(1)}, u32[]{:S(2)}, u32[]{:S(2)}) collective-permute-start(bf16[128,512]{1,0:T(8,128)(2,1)S(1)} %get-tuple-element.129), channel_id=1, source_target_pairs={{0,1},{1,2},{2,3},{3,7},{7,6},{6,5},{5,4},{4,0},{8,9},{9,10},{10,1... | collective-permute-start | bytes 393224 | tf_op jit(solution)/shard_map/ppermute | solution.py:34
  (11 other events, 86.0 us)
